TPU v7x, 32 devices: a whole 2x2x4 slice. The times are simulated.
32 devices in a mesh: dp: 4 (over x, core), tensor: 8 (over z, y).
Axes of the slice: x: 2, y: 2, z: 4, core: 2. Of those that a mesh axis runs over, the one named last changes fastest.
Arguments:
- tokens: bfloat16 [64, 2560], P(('dp', 'tensor')), may hold values from -6 to 6
- cotangent: bfloat16 [64, 2560], P(('dp', 'tensor')), may hold values from -6 to 6
- gate_weight: bfloat16 [2560, 12800], P('dp', 'tensor'), may hold values from -0.125 to 0.125
- up_weight: bfloat16 [2560, 12800], P('dp', 'tensor'), may hold values from -0.125 to 0.125
- down_weight: bfloat16 [12800, 2560], P('tensor', 'dp'), may hold values from -0.0546875 to 0.0546875
Outputs:
- input_grad: bfloat16 [64, 2560], P(('dp', 'tensor'))
- grad_gate: bfloat16 [2560, 12800], P('dp', 'tensor')
- grad_up: bfloat16 [2560, 12800], P('dp', 'tensor')
- grad_down: bfloat16 [12800, 2560], P('tensor', 'dp')
All inputs are finite; a program needn't handle non-finite values.
Results may differ from a plain program's by a relative error of at most 0.017.
Values may be sent and summed in bfloat16 or wider, within the bound.
No kernel may reach another device: no remote copies, remote signals or barrier semaphores. Data moves between devices by JAX's collectives and lax.ppermute only.
A program may use at most 128 MiB of HBM per device.

v0:
```python
import jax
import jax.numpy as jnp
from jax import lax
from jax.sharding import PartitionSpec as P


def local(tokens, cotangent, gate_weight, up_weight, down_weight):
    n_groups = lax.axis_size("dp")
    units = gate_weight.shape[1]
    group_tok, group_cot = (
        lax.all_gather(tokens, "tensor", axis=0, tiled=True),
        lax.all_gather(cotangent, "tensor", axis=0, tiled=True),
    )
    gate_full, up_full, down_full = (
        lax.all_gather(gate_weight, "dp", axis=0, tiled=True),
        lax.all_gather(up_weight, "dp", axis=0, tiled=True),
        lax.all_gather(down_weight, "dp", axis=1, tiled=True),
    )
    gate = jnp.dot(group_tok, gate_full, preferred_element_type=jnp.float32)
    up = jnp.dot(group_tok, up_full, preferred_element_type=jnp.float32)
    sig = jax.nn.sigmoid(gate)
    hidden = (gate * sig * up).astype(jnp.bfloat16)
    hidden_grad = jnp.einsum("td,fd->tf", group_cot, down_full, preferred_element_type=jnp.float32)
    up_grad = (hidden_grad * gate * sig).astype(jnp.bfloat16)
    gate_grad = (hidden_grad * up * sig * (1.0 + gate * (1.0 - sig))).astype(jnp.bfloat16)
    total = jnp.einsum("tf,df->td", gate_grad, gate_full, preferred_element_type=jnp.float32)
    input_grad = lax.psum_scatter(
        total + jnp.einsum("tf,df->td", up_grad, up_full, preferred_element_type=jnp.float32),
        "tensor",
        scatter_dimension=0,
        tiled=True,
    ).astype(jnp.bfloat16)
    part_gate = jnp.einsum("td,tf->df", group_tok, gate_grad, preferred_element_type=jnp.float32)
    part_up = jnp.einsum("td,tf->df", group_tok, up_grad, preferred_element_type=jnp.float32)
    part_down = jnp.einsum("td,tf->df", group_cot, hidden, preferred_element_type=jnp.float32)
    summed = (
        lax.psum_scatter(
            jnp.concatenate([part_gate, part_up, part_down], axis=1).astype(jnp.bfloat16),
            "dp",
            scatter_dimension=0,
            tiled=True,
        ).astype(jnp.float32)
        / n_groups
    )
    grad_gate = summed[:, :units].astype(jnp.bfloat16)
    grad_up = summed[:, units : 2 * units].astype(jnp.bfloat16)
    grad_down = summed[:, 2 * units :].T.astype(jnp.bfloat16)
    return (input_grad, grad_gate, grad_up, grad_down)


def solution(mesh):
    placed = (
        P(("dp", "tensor"), None),
        P(("dp", "tensor"), None),
        P("dp", "tensor"),
        P("dp", "tensor"),
        P("tensor", "dp"),
    )
    return jax.shard_map(
        local,
        mesh=mesh,
        in_specs=placed,
        out_specs=(
            P(("dp", "tensor"), None),
            P("dp", "tensor"),
            P("dp", "tensor"),
            P("tensor", "dp"),
        ),
        check_vma=False,
    )
```

profile of v0, /device:TPU:0, one launch (start us, length us, event | category | flops | bytes accessed | tf_op | source)
XLA Modules:
  0.0 455.5 jit_solution(12180258628496666761)
XLA Ops:
  7.2 0.7 all-gather.10.cloned.1.call-update
  7.9 0.7 all-gather.8.cloned.1.call-update
  8.7 0.7 all-gather.6.cloned.1.call-update
  9.4 32.5 %all-gather.1 = bf16[8,2,2560]{2,1,0:T(2,128)(2,1)S(1)} all-gather(bf16[1,2,2560]{2,1,0:T(2,128)(2,1)} %bitcast.27), channel_id=1, replica_groups=mesh['dp'=4,'tensor'=8] {'tensor'}, dimensions={0}, use_global_device_ids=true | all-gather | bytes 92160 | tf_op jit(solution)/shard_map/all_gather | solution.py:11
  42.0 30.7 %all-gather = bf16[8,2,2560]{2,1,0:T(2,128)(2,1)S(1)} all-gather(bf16[1,2,2560]{2,1,0:T(2,128)(2,1)} %bitcast.28), channel_id=1, replica_groups=mesh['dp'=4,'tensor'=8] {'tensor'}, dimensions={0}, use_global_device_ids=true | all-gather | bytes 92160 | tf_op jit(solution)/shard_map/all_gather | solution.py:12
  72.8 5.5 %fusion.6 = f32[16,1600]{1,0:T(8,128)S(1)} fusion(bf16[16,2560]{1,0:T(8,128)(2,1)S(1)} %reshape.11, bf16[2560,1600]{0,1:T(8,128)(2,1)} %all-gather.10.cloned.1.call-done), kind=kOutput, calls=%fused_computation.18 | convolution fusion | flops 131072000 | bytes 8376320 | tf_op jit(solution)/shard_map/dot_general | solution.py:19
  78.4 49.7 %all-gather.8.cloned.1.call-done = bf16[2560,1600]{0,1:T(8,128)(2,1)} async-done(((bf16[640,1600]{0,1:T(8,128)(2,1)}), bf16[2560,1600]{0,1:T(8,128)(2,1)}) %all-gather.8.cloned.1.call-update) | async-done | bytes 8192016 | tf_op jit(solution)/shard_map/all_gather | solution.py:16
  128.1 5.5 %fusion.5 = f32[16,1600]{1,0:T(8,128)S(1)} fusion(bf16[16,2560]{1,0:T(8,128)(2,1)S(1)} %reshape.11, bf16[2560,1600]{0,1:T(8,128)(2,1)} %all-gather.8.cloned.1.call-done), kind=kOutput, calls=%fused_computation.17 | convolution fusion | flops 131072000 | bytes 8376320 | tf_op jit(solution)/shard_map/dot_general | solution.py:20
  133.6 6.4 %fusion.2 = bf16[2560,1600]{0,1:T(8,128)(2,1)} fusion(bf16[16,2560]{1,0:T(8,128)(2,1)S(1)} %reshape.9, f32[16,1600]{1,0:T(8,128)S(1)} %fusion.5, f32[16,1600]{1,0:T(8,128)S(1)} %fusion.6), kind=kOutput, calls=%fused_computation.7 | convolution fusion | flops 135321600 | bytes 8478720 | tf_op jit(solution)/shard_map/td,tf->df/dot_general | solution.py:35
  140.0 46.8 %all-gather.6.cloned.1.call-done = bf16[1600,2560]{1,0:T(8,128)(2,1)} async-done(((bf16[1600,640]{1,0:T(8,128)(2,1)}), bf16[1600,2560]{1,0:T(8,128)(2,1)}) %all-gather.6.cloned.1.call-update) | async-done | bytes 8192016 | tf_op jit(solution)/shard_map/all_gather | solution.py:17
  186.8 5.5 %multiply_convert_fusion.2 = (bf16[16,1600]{1,0:T(8,128)(2,1)S(1)}, bf16[16,1600]{1,0:T(8,128)(2,1)S(1)}) fusion(f32[16,1600]{1,0:T(8,128)S(1)} %fusion.6, f32[16,1600]{1,0:T(8,128)S(1)} %fusion.5, bf16[16,2560]{1,0:T(8,128)(2,1)S(1)} %reshape.9, bf16[1600,2560]{1,0:T(8,128)(2,1)} %all-gather.6.cloned.1.call-done), kind=kOutput, calls=%fused_computation.11 | convolution fusion | flops 131404800 | bytes 8581120 | tf_op jit(solution)/shard_map/td,fd->tf/dot_general | solution.py:23
  192.4 5.5 %fusion.1 = bf16[2560,1600]{0,1:T(8,128)(2,1)} fusion(bf16[16,1600]{1,0:T(8,128)(2,1)S(1)} %get-tuple-element.7, bf16[16,2560]{1,0:T(8,128)(2,1)S(1)} %reshape.11), kind=kOutput, calls=%fused_computation.6 | convolution fusion | flops 135168000 | bytes 8325120 | tf_op jit(solution)/shard_map/td,tf->df/dot_general | solution.py:34
  197.8 5.5 %fusion = bf16[2560,1600]{0,1:T(8,128)(2,1)} fusion(bf16[16,1600]{1,0:T(8,128)(2,1)S(1)} %get-tuple-element.8, bf16[16,2560]{1,0:T(8,128)(2,1)S(1)} %reshape.11), kind=kOutput, calls=%fused_computation.5 | convolution fusion | flops 135168000 | bytes 8325120 | tf_op jit(solution)/shard_map/td,tf->df/dot_general | solution.py:33
  203.3 19.1 %pad_maximum_fusion = bf16[2560,4800]{0,1:T(8,128)(2,1)} fusion(bf16[2560,1600]{0,1:T(8,128)(2,1)} %fusion.2, bf16[2560,1600]{0,1:T(8,128)(2,1)} %fusion.1, bf16[2560,1600]{0,1:T(8,128)(2,1)} %fusion), kind=kLoop, calls=%fused_computation | loop fusion | flops 73728000 | bytes 49152000 | tf_op jit(solution)/shard_map/concatenate | solution.py:38
  222.4 31.5 %copy.9 = bf16[2560,4800]{1,0:T(8,128)(2,1)} copy(bf16[2560,4800]{0,1:T(8,128)(2,1)} %pad_maximum_fusion) | data formatting | bytes 49152000
  254.0 0.6 copy-done
  255.8 4.5 fusion.7
  260.3 5.8 %convolution_add_fusion = f32[16,2560]{1,0:T(8,128)S(1)} fusion(f32[16,2560]{1,0:T(8,128)S(1)} %fusion.7, bf16[16,1600]{1,0:T(8,128)(2,1)S(1)} %get-tuple-element.7, bf16[2560,1600]{0,1:T(8,128)(2,1)} %all-gather.8.cloned.1.call-done), kind=kOutput, calls=%fused_computation.8 | convolution fusion | flops 131112960 | bytes 8570880 | tf_op jit(solution)/shard_map/tf,df->td/dot_general | solution.py:28
  266.2 38.7 %all-reduce.2 = bf16[16,2560]{1,0:T(8,128)(2,1)S(1)} all-reduce(f32[16,2560]{1,0:T(8,128)S(1)} %convolution_add_fusion), channel_id=2, replica_groups=mesh['dp'=4,'tensor'=8] {'tensor'}, use_global_device_ids=true, to_apply=%region_0.0.clone | all-reduce | flops 40960 | bytes 245760
  304.9 0.6 dynamic-slice_convert_fusion
  305.5 127.3 %reduce-scatter.4.cloned.1.call-done = bf16[640,4800]{1,0:T(8,128)(2,1)} async-done(((bf16[2560,4800]{1,0:T(8,128)(2,1)}), bf16[640,4800]{1,0:T(8,128)(2,1)}) %reduce-scatter.4.cloned.1.call-update) | async-done | bytes 6144016
  432.8 9.4 %copy.10 = bf16[640,4800]{0,1:T(8,128)(2,1)} copy(bf16[640,4800]{1,0:T(8,128)(2,1)} %reduce-scatter.4.cloned.1.call-done) | data formatting | bytes 12288000
  442.2 3.9 multiply_convert_fusion
  446.1 2.8 slice_bitcast_fusion
  (10 shorter events, 0.8 us)
Async XLA Ops:
  7.2 65.7 %all-gather.10.cloned.1.call-start = ((), (), s32[]{:S(2)}) async-start(), calls=%async_computation.3 | async-start | bytes 10240000 | tf_op jit(solution)/shard_map/all_gather | solution.py:15
  7.9 120.2 %all-gather.8.cloned.1.call-start = ((), (), s32[]{:S(2)}) async-start(), calls=%async_computation.2 | async-start | bytes 10240000 | tf_op jit(solution)/shard_map/all_gather | solution.py:16
  8.6 178.2 %all-gather.6.cloned.1.call-start = ((), (), s32[]{:S(2)}) async-start(), calls=%async_computation.1 | async-start | bytes 10240000 | tf_op jit(solution)/shard_map/all_gather | solution.py:17
  9.4 423.4 %reduce-scatter.4.cloned.1.call-start = ((), (), s32[]{:S(2)}) async-start(), calls=%async_computation.4 | async-start | bytes 31129600
  253.9 0.7 copy-start
Sparse Core Ops, SparseCore 0:
  9.6 59.7 all-gather.9
  71.0 57.0 all-gather.7
  129.7 57.0 all-gather.5
  254.1 178.6 reduce-scatter.3
where the time goes:
time: 457 us; the launch traced here: 455 us
  waiting for transfers between devices  226 us (49%)
  blocking collectives  102 us (22%)
  local copies, waits for them, and re-layouts  45.6 us (10%)
  matrix products  44.3 us (10%)
  other arithmetic  23.1 us (5%)
  between operations  14.5 us (3%)
    unnamed x5, waiting for transfers between devices  129 us
    all_gather x1, waiting for transfers between devices, local(): lax.all_gather(up_weight, 'dp', axis=0, tiled=True)  49.7 us
    all_gather x1, waiting for transfers between devices, local(): lax.all_gather(down_weight, 'dp', axis=1, tiled=True)  46.8 us
    unnamed x7, local copies, waits for them, and re-layouts  42.2 us
    unnamed x1, blocking collectives  38.7 us
    all_gather x1, blocking collectives, local(): lax.all_gather(tokens, 'tensor', axis=0, tiled=True)  32.5 us
    all_gather x1, blocking collectives, local(): lax.all_gather(cotangent, 'tensor', axis=0, tiled=True)  30.7 us
    concatenate x1, other arithmetic, local(): jnp.concatenate([part_gate, part_up, part_down], axis=1)  19.1 us
  transfers between devices with their start and end apart: 4, of which 3 were waited for; matrix products, arithmetic and copies ran while one was open for 6% of the time, Pallas kernels for 0%

commit v1 on v0

v1 whole, which is shorter than its diff:
```python
import jax
import jax.numpy as jnp
from jax import lax
from jax.sharding import PartitionSpec as P

F32 = jnp.float32
BF16 = jnp.bfloat16


def swap_cores(value, n_dp):
    return lax.ppermute(value, "dp", [(i, i ^ 1) for i in range(n_dp)])


def local(tokens, cotangent, gate_weight, up_weight, down_weight):
    n_dp = lax.axis_size("dp")
    n_tensor = lax.axis_size("tensor")
    rows, width = tokens.shape
    depth, units = gate_weight.shape
    group = rows * n_tensor
    chips = n_dp // 2
    half = chips * group
    core = lax.rem(lax.axis_index("dp"), 2)

    joined = jnp.concatenate([tokens, cotangent], axis=0)
    slices = jnp.stack([joined[:, d * depth : (d + 1) * depth] for d in range(n_dp)])
    slices = jnp.broadcast_to(slices[:, None], (n_dp, n_tensor, 2 * rows, depth))
    both = lax.all_to_all(
        slices.reshape(n_dp * n_tensor, 2 * rows, depth), ("dp", "tensor"), split_axis=0, concat_axis=0, tiled=True
    )

    def by_core(value):
        value = value.reshape(chips, 2, group, depth)
        value = jnp.where(core == 0, value[:, ::-1], value)
        return value.transpose(1, 0, 2, 3).reshape(2 * half, depth)

    tok, cot = by_core(both[:, :rows]), by_core(both[:, rows:])

    gate_rows, up_rows = gate_weight.T, up_weight.T
    up_p = jnp.einsum("td,fd->tf", tok, up_rows, preferred_element_type=F32)
    tok_gate, up_p = lax.optimization_barrier((tok, up_p))
    gate_p = jnp.einsum("td,fd->tf", tok_gate, gate_rows, preferred_element_type=F32)
    cot, gate_p = lax.optimization_barrier((cot, gate_p))
    hid_p = jnp.einsum("td,fd->tf", cot, down_weight, preferred_element_type=F32)

    def sum_over_dp(partial):
        got = swap_cores(partial[:half].astype(BF16), n_dp)
        mine = (partial[half:] + got.astype(F32)).astype(BF16)
        total = mine.astype(F32)
        for shift in range(1, chips):
            got = lax.ppermute(mine, "dp", [(i, (i + 2 * shift) % n_dp) for i in range(n_dp)])
            total = total + got.astype(F32)
        return total

    gate, up, hidden_grad = sum_over_dp(gate_p), sum_over_dp(up_p), sum_over_dp(hid_p)

    sig = jax.nn.sigmoid(gate)
    hidden = (gate * sig * up).astype(BF16)
    up_grad = (hidden_grad * gate * sig).astype(BF16)
    gate_grad = (hidden_grad * up * sig * (1.0 + gate * (1.0 - sig))).astype(BF16)
    gate_grad, up_grad, hidden = (
        jnp.concatenate([swap_cores(value, n_dp), value], axis=0) for value in (gate_grad, up_grad, hidden)
    )

    total = jnp.einsum("tf,fd->td", gate_grad, gate_rows, preferred_element_type=F32)
    total = total + jnp.einsum("tf,fd->td", up_grad, up_rows, preferred_element_type=F32)
    shares = total.astype(BF16).reshape(2, chips, group, depth).transpose(1, 0, 2, 3)
    shares = jnp.where(core == 0, shares[:, ::-1], shares).reshape(n_dp * n_tensor, rows, depth)
    shares = lax.all_to_all(shares, ("dp", "tensor"), split_axis=0, concat_axis=0, tiled=True)
    shares = jnp.sum(shares.astype(F32).reshape(n_dp, n_tensor, rows, depth), axis=1)
    input_grad = shares.transpose(1, 0, 2).reshape(rows, width).astype(BF16)

    grad_gate = (jnp.einsum("td,tf->df", tok, gate_grad, preferred_element_type=F32) / n_dp).astype(BF16)
    grad_up = (jnp.einsum("td,tf->df", tok, up_grad, preferred_element_type=F32) / n_dp).astype(BF16)
    grad_down = (jnp.einsum("tf,td->fd", hidden, cot, preferred_element_type=F32) / n_dp).astype(BF16)
    return (input_grad, grad_gate, grad_up, grad_down)


def solution(mesh):
    return jax.shard_map(
        local,
        mesh=mesh,
        in_specs=(
            P(("dp", "tensor"), None),
            P(("dp", "tensor"), None),
            P("dp", "tensor"),
            P("dp", "tensor"),
            P("tensor", "dp"),
        ),
        out_specs=(
            P(("dp", "tensor"), None),
            P("dp", "tensor"),
            P("dp", "tensor"),
            P("tensor", "dp"),
        ),
        check_vma=False,
    )
```

time: 457 us -> 45.9 us (0.10)
  waiting for transfers between devices: 226 us -> 16.1 us
  blocking collectives: 102 us -> 0 us
  local copies, waits for them, and re-layouts: 45.6 us -> 2.15 us
  matrix products: 44.3 us -> 9.33 us
  other arithmetic: 23.1 us -> 1.98 us
  starting transfers between devices: 0.15 us -> 15.2 us
  between operations: 14.5 us -> 0.85 us
    unnamed x5 -> x0, waiting for transfers between devices: 129 us -> none
    all_gather x3 -> x0, waiting for transfers between devices: 96.5 us -> none  [the longest x1 49.7 us: local(): lax.all_gather(up_weight, 'dp', axis=0, tiled=True)]
    all_gather x2 -> x0, blocking collectives: 63.3 us -> none  [the longest x1 32.5 us: local(): lax.all_gather(tokens, 'tensor', axis=0, tiled=True)]
    unnamed x7 -> x6, local copies, waits for them, and re-layouts: 42.2 us -> 0.51 us
    unnamed x1 -> x0, blocking collectives: 38.7 us -> none
    dot_general x8, matrix products: 44.3 us -> 9.33 us  [the longest x1 2.05 us: local(): jnp.einsum('td,tf->df', tok, gate_grad, preferred_element_type=F32) / n_dp]
    concatenate x1 -> x0, other arithmetic: 19.1 us -> none  [local(): jnp.concatenate([part_gate, part_up, part_down], axis=1)]
    all_to_all x0 -> x2, starting transfers between devices: none -> 10.3 us  [the longest x1 7.3 us: local(): lax.all_to_all(slices.reshape(n_dp * n_tensor, 2 * rows, depth), ('dp', '...]
  transfers between devices with their start and end apart: 4 -> 11, of which waited for: 3 -> 6; matrix products, arithmetic and copies ran while one was open for 6% -> 21% of each run, Pallas kernels for 0% -> 0%
where the time goes in v1:
time: 45.9 us; the launch traced here: 45.6 us
  waiting for transfers between devices  16.1 us (35%)
  starting transfers between devices  15.2 us (33%)
  matrix products  9.33 us (20%)
  local copies, waits for them, and re-layouts  2.15 us (5%)
  other arithmetic  1.98 us (4%)
  between operations  0.85 us (2%)
    all_to_all x1, waiting for transfers between devices, local(): lax.all_to_all(slices.reshape(n_dp * n_tensor, 2 * rows, depth), ('dp', '...  7.91 us
    all_to_all x1, starting transfers between devices, local(): lax.all_to_all(slices.reshape(n_dp * n_tensor, 2 * rows, depth), ('dp', '...  7.3 us
    ppermute x3, waiting for transfers between devices, sum_over_dp(): lax.ppermute(mine, 'dp', [(i, (i + 2 * shift) % n_dp) for i in range(n_dp)])  6.14 us
    ppermute x3, starting transfers between devices, sum_over_dp(): lax.ppermute(mine, 'dp', [(i, (i + 2 * shift) % n_dp) for i in range(n_dp)])  3.45 us
    all_to_all x1, starting transfers between devices, local(): lax.all_to_all(shares, ('dp', 'tensor'), split_axis=0, concat_axis=0, til...  2.98 us
    dot_general x1, matrix products, local(): jnp.einsum('td,tf->df', tok, gate_grad, preferred_element_type=F32) / n_dp  2.05 us
    dot_general x1, matrix products, local(): jnp.einsum('td,tf->df', tok, up_grad, preferred_element_type=F32) / n_dp  2.05 us
    dot_general x1, matrix products, local(): jnp.einsum('tf,td->fd', hidden, cot, preferred_element_type=F32) / n_dp  2.03 us
  transfers between devices with their start and end apart: 11, of which 6 were waited for; matrix products, arithmetic and copies ran while one was open for 21% of the time, Pallas kernels for 0%

profile of v1, /device:TPU:0, one launch (start us, length us, event | category | flops | bytes accessed | tf_op | source)
XLA Modules:
  0.0 45.6 jit_solution(8751738524925996754)
XLA Ops:
  0.6 1.0 %fusion.13 = (bf16[1,4,640]{2,1,0:T(4,128)(2,1)S(1)}, bf16[1,4,640]{2,1,0:T(4,128)(2,1)S(1)}, bf16[1,4,640]{2,1,0:T(4,128)(2,1)S(1)}, bf16[1,4,640]{2,1,0:T(4,128)(2,1)S(1)}) fusion(bf16[2,2560]{1,0:T(2,128)(2,1)} %param.6, bf16[2,2560]{1,0:T(2,128)(2,1)} %param.5), kind=kLoop, calls=%fused_computation.45 | loop fusion | flops 40960 | bytes 40960 | tf_op jit(solution)/shard_map/stack | solution.py:25
  1.6 0.7 %broadcast_in_dim.2 = bf16[4,8,4,640]{3,2,1,0:T(4,128)(2,1)} broadcast(bf16[4,4,640]{2,1,0:T(4,128)(2,1)S(1)} %pad_maximum_fusion.6), dimensions={0,2,3} | broadcast | bytes 184320 | tf_op jit(solution)/shard_map/broadcast_in_dim | solution.py:26
  2.4 7.3 %all-to-all-start = ((bf16[32,4,640]{2,1,0:T(4,128)(2,1)}), bf16[32,4,640]{2,1,0:T(4,128)(2,1)S(1)}, u32[]{:S(2)}, u32[]{:S(2)}) async-start(bf16[32,4,640]{2,1,0:T(4,128)(2,1)} %bitcast.4), calls=%async_computation | async-start | bytes 327680 | tf_op jit(solution)/shard_map/all_to_all | solution.py:27
  9.7 7.9 %all-to-all-done = bf16[32,4,640]{2,1,0:T(4,128)(2,1)S(1)} async-done(((bf16[32,4,640]{2,1,0:T(4,128)(2,1)}), bf16[32,4,640]{2,1,0:T(4,128)(2,1)S(1)}, u32[]{:S(2)}, u32[]{:S(2)}) %all-to-all-start) | async-done | bytes 163872 | tf_op jit(solution)/shard_map/all_to_all | solution.py:27
  17.9 0.7 %fusion.21 = f32[64,1600]{1,0:T(8,128)S(1)} fusion(bf16[64,640]{1,0:T(8,128)(2,1)S(1)} %bitcast.37, bf16[640,1600]{0,1:T(8,128)(2,1)S(1)} %copy-done), kind=kOutput, calls=%fused_computation.53 | convolution fusion | flops 131072000 | bytes 2539520 | tf_op jit(solution)/shard_map/td,fd->tf/dot_general | solution.py:39
  18.9 0.5 %copy-done.1 = bf16[640,1600]{0,1:T(8,128)(2,1)S(1)} copy-done((bf16[640,1600]{0,1:T(8,128)(2,1)S(1)}, bf16[640,1600]{0,1:T(8,128)(2,1)}, u32[]{:S(2)}) %copy-start.1) | copy-done | bytes 2048024
  19.4 0.7 %fusion.22 = f32[64,1600]{1,0:T(8,128)S(1)} fusion(bf16[64,640]{1,0:T(8,128)(2,1)S(1)} %bitcast.38, bf16[640,1600]{0,1:T(8,128)(2,1)S(1)} %copy-done.1), kind=kOutput, calls=%fused_computation.54 | convolution fusion | flops 131072000 | bytes 2539520 | tf_op jit(solution)/shard_map/td,fd->tf/dot_general | solution.py:41
  20.4 0.7 %fusion.23 = f32[64,1600]{1,0:T(8,128)S(1)} fusion(bf16[64,640]{1,0:T(8,128)(2,1)S(1)} %bitcast.41, bf16[1600,640]{1,0:T(8,128)(2,1)S(1)} %copy-done.2), kind=kOutput, calls=%fused_computation.55 | convolution fusion | flops 131072000 | bytes 2539520 | tf_op jit(solution)/shard_map/td,fd->tf/dot_general | solution.py:43
  21.6 1.3 %collective-permute-start.3 = (bf16[32,1600]{1,0:T(8,128)(2,1)S(1)}, bf16[32,1600]{1,0:T(8,128)(2,1)S(1)}, u32[]{:S(2)}, u32[]{:S(2)}) collective-permute-start(bf16[32,1600]{1,0:T(8,128)(2,1)S(1)} %add_convert_fusion.1), channel_id=1, source_target_pairs={{0,16},{8,24},{16,0},{24,8},{1,17},{9,25},{17,1},{25,9},{2,18},{10... | collective-permute-start | bytes 307208 | tf_op jit(solution)/shard_map/ppermute | solution.py:50
  22.9 0.9 %collective-permute-start.5 = (bf16[32,1600]{1,0:T(8,128)(2,1)S(1)}, bf16[32,1600]{1,0:T(8,128)(2,1)S(1)}, u32[]{:S(2)}, u32[]{:S(2)}) collective-permute-start(bf16[32,1600]{1,0:T(8,128)(2,1)S(1)} %add_convert_fusion), channel_id=1, source_target_pairs={{0,16},{8,24},{16,0},{24,8},{1,17},{9,25},{17,1},{25,9},{2,18},{10... | collective-permute-start | bytes 307208 | tf_op jit(solution)/shard_map/ppermute | solution.py:50
  23.8 1.3 %collective-permute-start.1 = (bf16[32,1600]{1,0:T(8,128)(2,1)S(1)}, bf16[32,1600]{1,0:T(8,128)(2,1)S(1)}, u32[]{:S(2)}, u32[]{:S(2)}) collective-permute-start(bf16[32,1600]{1,0:T(8,128)(2,1)S(1)} %fusion.1), channel_id=1, source_target_pairs={{0,16},{8,24},{16,0},{24,8},{1,17},{9,25},{17,1},{25,9},{2,18},{10... | collective-permute-start | bytes 307208 | tf_op jit(solution)/shard_map/ppermute | solution.py:50
  25.1 2.4 %collective-permute-done.3 = bf16[32,1600]{1,0:T(8,128)(2,1)S(1)} collective-permute-done((bf16[32,1600]{1,0:T(8,128)(2,1)S(1)}, bf16[32,1600]{1,0:T(8,128)(2,1)S(1)}, u32[]{:S(2)}, u32[]{:S(2)}) %collective-permute-start.3) | collective-permute-done | bytes 102432 | tf_op jit(solution)/shard_map/ppermute | solution.py:50
  27.5 2.3 %collective-permute-done.5 = bf16[32,1600]{1,0:T(8,128)(2,1)S(1)} collective-permute-done((bf16[32,1600]{1,0:T(8,128)(2,1)S(1)}, bf16[32,1600]{1,0:T(8,128)(2,1)S(1)}, u32[]{:S(2)}, u32[]{:S(2)}) %collective-permute-start.5) | collective-permute-done | bytes 102432 | tf_op jit(solution)/shard_map/ppermute | solution.py:50
  29.7 1.5 %collective-permute-done.1 = bf16[32,1600]{1,0:T(8,128)(2,1)S(1)} collective-permute-done((bf16[32,1600]{1,0:T(8,128)(2,1)S(1)}, bf16[32,1600]{1,0:T(8,128)(2,1)S(1)}, u32[]{:S(2)}, u32[]{:S(2)}) %collective-permute-start.1) | collective-permute-done | bytes 102432 | tf_op jit(solution)/shard_map/ppermute | solution.py:50
  31.5 0.5 %collective-permute-start.8 = (bf16[32,1600]{1,0:T(8,128)(2,1)S(1)}, bf16[32,1600]{1,0:T(8,128)(2,1)S(1)}, u32[]{:S(2)}, u32[]{:S(2)}) collective-permute-start(bf16[32,1600]{1,0:T(8,128)(2,1)S(1)} %get-tuple-element.12), channel_id=1, source_target_pairs={{0,8},{8,0},{16,24},{24,16},{1,9},{9,1},{17,25},{25,17},{2,10},{10... | collective-permute-start | bytes 307208 | tf_op jit(solution)/shard_map/ppermute | solution.py:11
  32.1 0.7 %collective-permute-done.7 = bf16[32,1600]{1,0:T(8,128)(2,1)S(1)} collective-permute-done((bf16[32,1600]{1,0:T(8,128)(2,1)S(1)}, bf16[32,1600]{1,0:T(8,128)(2,1)S(1)}, u32[]{:S(2)}, u32[]{:S(2)}) %collective-permute-start.7) | collective-permute-done | bytes 102432 | tf_op jit(solution)/shard_map/ppermute | solution.py:11
  32.8 0.5 %fusion.5 = f32[64,640]{1,0:T(8,128)S(1)} fusion(bf16[640,1600]{0,1:T(8,128)(2,1)S(1)} %copy-done, bf16[32,1600]{1,0:T(8,128)(2,1)S(1)} %get-tuple-element.14, bf16[32,1600]{1,0:T(8,128)(2,1)S(1)} %collective-permute-done.7), kind=kOutput, calls=%fused_computation.24 | convolution fusion | flops 131481600 | bytes 2416640 | tf_op jit(solution)/shard_map/tf,fd->td/dot_general | solution.py:65
  33.9 0.7 %reshape.44 = bf16[32,2,640]{2,1,0:T(2,128)(2,1)} reshape(bf16[2,2,16,640]{3,2,1,0:T(8,128)(2,1)S(1)} %reverse_select_fusion) | data formatting | bytes 163840 | tf_op jit(solution)/shard_map/reshape | solution.py:67
  34.5 3.0 %all-to-all-start.1 = ((bf16[32,2,640]{2,1,0:T(2,128)(2,1)}), bf16[32,2,640]{2,1,0:T(2,128)(2,1)S(1)}, u32[]{:S(2)}, u32[]{:S(2)}) async-start(bf16[32,2,640]{2,1,0:T(2,128)(2,1)} %reshape.44), calls=%async_computation.1 | async-start | bytes 163840 | tf_op jit(solution)/shard_map/all_to_all | solution.py:68
  37.5 2.1 %multiply_convert_fusion.2 = bf16[640,1600]{0,1:T(8,128)(2,1)} fusion(bf16[64,640]{1,0:T(8,128)(2,1)S(1)} %bitcast.39, bf16[32,1600]{1,0:T(8,128)(2,1)S(1)} %get-tuple-element.13, bf16[32,1600]{1,0:T(8,128)(2,1)S(1)} %collective-permute-done.6), kind=kOutput, calls=%fused_computation.2 | convolution fusion | flops 133529600 | bytes 2334720 | tf_op jit(solution)/shard_map/td,tf->df/dot_general | solution.py:72
  39.6 2.1 %multiply_convert_fusion.1 = bf16[640,1600]{0,1:T(8,128)(2,1)} fusion(bf16[64,640]{1,0:T(8,128)(2,1)S(1)} %bitcast.40, bf16[32,1600]{1,0:T(8,128)(2,1)S(1)} %get-tuple-element.14, bf16[32,1600]{1,0:T(8,128)(2,1)S(1)} %collective-permute-done.7), kind=kOutput, calls=%fused_computation.1 | convolution fusion | flops 133529600 | bytes 2334720 | tf_op jit(solution)/shard_map/td,tf->df/dot_general | solution.py:73
  41.6 2.0 %multiply_convert_fusion = bf16[1600,640]{1,0:T(8,128)(2,1)} fusion(bf16[64,640]{1,0:T(8,128)(2,1)S(1)} %bitcast.42, bf16[32,1600]{1,0:T(8,128)(2,1)S(1)} %get-tuple-element.12, bf16[32,1600]{1,0:T(8,128)(2,1)S(1)} %collective-permute-done.8), kind=kOutput, calls=%fused_computation | convolution fusion | flops 133529600 | bytes 2334720 | tf_op jit(solution)/shard_map/tf,td->fd/dot_general | solution.py:74
  43.7 1.3 %all-to-all-done.1 = bf16[32,2,640]{2,1,0:T(2,128)(2,1)S(1)} async-done(((bf16[32,2,640]{2,1,0:T(2,128)(2,1)}), bf16[32,2,640]{2,1,0:T(2,128)(2,1)S(1)}, u32[]{:S(2)}, u32[]{:S(2)}) %all-to-all-start.1) | async-done | bytes 81952 | tf_op jit(solution)/shard_map/all_to_all | solution.py:68
  44.9 0.7 %bitcast_reduce_fusion = bf16[4,2,640]{2,1,0:T(2,128)(2,1)} fusion(bf16[32,2,640]{2,1,0:T(2,128)(2,1)S(1)} %all-to-all-done.1), kind=kLoop, calls=%fused_computation.30 | loop fusion | flops 35840 | bytes 92160 | tf_op jit(solution)/shard_map/reduce_sum | solution.py:69
  (32 shorter events, 2.1 us)
Async XLA Ops:
  0.6 17.2 %copy-start = (bf16[640,1600]{0,1:T(8,128)(2,1)S(1)}, bf16[640,1600]{0,1:T(8,128)(2,1)}, u32[]{:S(2)}) copy-start(bf16[640,1600]{0,1:T(8,128)(2,1)} %param.8) | copy-start | bytes 6144004
  2.4 15.2 %all-to-all-start = ((bf16[32,4,640]{2,1,0:T(4,128)(2,1)}), bf16[32,4,640]{2,1,0:T(4,128)(2,1)S(1)}, u32[]{:S(2)}, u32[]{:S(2)}) async-start(bf16[32,4,640]{2,1,0:T(4,128)(2,1)} %bitcast.4), calls=%async_computation | async-start | bytes 327680 | tf_op jit(solution)/shard_map/all_to_all | solution.py:27
  17.8 1.6 %copy-start.1 = (bf16[640,1600]{0,1:T(8,128)(2,1)S(1)}, bf16[640,1600]{0,1:T(8,128)(2,1)}, u32[]{:S(2)}) copy-start(bf16[640,1600]{0,1:T(8,128)(2,1)} %param.7) | copy-start | bytes 6144004
  18.6 1.7 %copy-start.2 = (bf16[1600,640]{1,0:T(8,128)(2,1)S(1)}, bf16[1600,640]{1,0:T(8,128)(2,1)}, u32[]{:S(2)}) copy-start(bf16[1600,640]{1,0:T(8,128)(2,1)} %param.9) | copy-start | bytes 6144004
  18.7 2.9 %collective-permute-start.2 = (bf16[32,1600]{1,0:T(8,128)(2,1)S(1)}, bf16[32,1600]{1,0:T(8,128)(2,1)S(1)}, u32[]{:S(2)}, u32[]{:S(2)}) collective-permute-start(bf16[32,1600]{1,0:T(8,128)(2,1)S(1)} %slice.102), channel_id=1, source_target_pairs={{0,8},{8,0},{16,24},{24,16},{1,9},{9,1},{17,25},{25,17},{2,10},{10... | collective-permute-start | bytes 307208 | tf_op jit(solution)/shard_map/ppermute | solution.py:11
  20.1 2.7 %collective-permute-start.4 = (bf16[32,1600]{1,0:T(8,128)(2,1)S(1)}, bf16[32,1600]{1,0:T(8,128)(2,1)S(1)}, u32[]{:S(2)}, u32[]{:S(2)}) collective-permute-start(bf16[32,1600]{1,0:T(8,128)(2,1)S(1)} %slice.101), channel_id=1, source_target_pairs={{0,8},{8,0},{16,24},{24,16},{1,9},{9,1},{17,25},{25,17},{2,10},{10... | collective-permute-start | bytes 307208 | tf_op jit(solution)/shard_map/ppermute | solution.py:11
  21.1 2.6 %collective-permute-start = (bf16[32,1600]{1,0:T(8,128)(2,1)S(1)}, bf16[32,1600]{1,0:T(8,128)(2,1)S(1)}, u32[]{:S(2)}, u32[]{:S(2)}) collective-permute-start(bf16[32,1600]{1,0:T(8,128)(2,1)S(1)} %slice.103), channel_id=1, source_target_pairs={{0,8},{8,0},{16,24},{24,16},{1,9},{9,1},{17,25},{25,17},{2,10},{10... | collective-permute-start | bytes 307208 | tf_op jit(solution)/shard_map/ppermute | solution.py:11
  21.6 5.9 %collective-permute-start.3 = (bf16[32,1600]{1,0:T(8,128)(2,1)S(1)}, bf16[32,1600]{1,0:T(8,128)(2,1)S(1)}, u32[]{:S(2)}, u32[]{:S(2)}) collective-permute-start(bf16[32,1600]{1,0:T(8,128)(2,1)S(1)} %add_convert_fusion.1), channel_id=1, source_target_pairs={{0,16},{8,24},{16,0},{24,8},{1,17},{9,25},{17,1},{25,9},{2,18},{10... | collective-permute-start | bytes 307208 | tf_op jit(solution)/shard_map/ppermute | solution.py:50
  22.9 6.8 %collective-permute-start.5 = (bf16[32,1600]{1,0:T(8,128)(2,1)S(1)}, bf16[32,1600]{1,0:T(8,128)(2,1)S(1)}, u32[]{:S(2)}, u32[]{:S(2)}) collective-permute-start(bf16[32,1600]{1,0:T(8,128)(2,1)S(1)} %add_convert_fusion), channel_id=1, source_target_pairs={{0,16},{8,24},{16,0},{24,8},{1,17},{9,25},{17,1},{25,9},{2,18},{10... | collective-permute-start | bytes 307208 | tf_op jit(solution)/shard_map/ppermute | solution.py:50
  23.8 7.4 %collective-permute-start.1 = (bf16[32,1600]{1,0:T(8,128)(2,1)S(1)}, bf16[32,1600]{1,0:T(8,128)(2,1)S(1)}, u32[]{:S(2)}, u32[]{:S(2)}) collective-permute-start(bf16[32,1600]{1,0:T(8,128)(2,1)S(1)} %fusion.1), channel_id=1, source_target_pairs={{0,16},{8,24},{16,0},{24,8},{1,17},{9,25},{17,1},{25,9},{2,18},{10... | collective-permute-start | bytes 307208 | tf_op jit(solution)/shard_map/ppermute | solution.py:50
  31.4 1.4 %collective-permute-start.7 = (bf16[32,1600]{1,0:T(8,128)(2,1)S(1)}, bf16[32,1600]{1,0:T(8,128)(2,1)S(1)}, u32[]{:S(2)}, u32[]{:S(2)}) collective-permute-start(bf16[32,1600]{1,0:T(8,128)(2,1)S(1)} %get-tuple-element.14), channel_id=1, source_target_pairs={{0,8},{8,0},{16,24},{24,16},{1,9},{9,1},{17,25},{25,17},{2,10},{10... | collective-permute-start | bytes 307208 | tf_op jit(solution)/shard_map/ppermute | solution.py:11
  31.5 10.1 %collective-permute-start.8 = (bf16[32,1600]{1,0:T(8,128)(2,1)S(1)}, bf16[32,1600]{1,0:T(8,128)(2,1)S(1)}, u32[]{:S(2)}, u32[]{:S(2)}) collective-permute-start(bf16[32,1600]{1,0:T(8,128)(2,1)S(1)} %get-tuple-element.12), channel_id=1, source_target_pairs={{0,8},{8,0},{16,24},{24,16},{1,9},{9,1},{17,25},{25,17},{2,10},{10... | collective-permute-start | bytes 307208 | tf_op jit(solution)/shard_map/ppermute | solution.py:11
  32.0 1.3 %collective-permute-start.6 = (bf16[32,1600]{1,0:T(8,128)(2,1)S(1)}, bf16[32,1600]{1,0:T(8,128)(2,1)S(1)}, u32[]{:S(2)}, u32[]{:S(2)}) collective-permute-start(bf16[32,1600]{1,0:T(8,128)(2,1)S(1)} %get-tuple-element.13), channel_id=1, source_target_pairs={{0,8},{8,0},{16,24},{24,16},{1,9},{9,1},{17,25},{25,17},{2,10},{10... | collective-permute-start | bytes 307208 | tf_op jit(solution)/shard_map/ppermute | solution.py:11
  34.5 10.4 %all-to-all-start.1 = ((bf16[32,2,640]{2,1,0:T(2,128)(2,1)}), bf16[32,2,640]{2,1,0:T(2,128)(2,1)S(1)}, u32[]{:S(2)}, u32[]{:S(2)}) async-start(bf16[32,2,640]{2,1,0:T(2,128)(2,1)} %reshape.44), calls=%async_computation.1 | async-start | bytes 163840 | tf_op jit(solution)/shard_map/all_to_all | solution.py:68

commit v2 on v1

--- a/solution.py
+++ b/solution.py
@@ -36,22 +36,25 @@
     tok, cot = by_core(both[:, :rows]), by_core(both[:, rows:])
 
     gate_rows, up_rows = gate_weight.T, up_weight.T
-    up_p = jnp.einsum("td,fd->tf", tok, up_rows, preferred_element_type=F32)
-    tok_gate, up_p = lax.optimization_barrier((tok, up_p))
-    gate_p = jnp.einsum("td,fd->tf", tok_gate, gate_rows, preferred_element_type=F32)
-    cot, gate_p = lax.optimization_barrier((cot, gate_p))
-    hid_p = jnp.einsum("td,fd->tf", cot, down_weight, preferred_element_type=F32)
 
-    def sum_over_dp(partial):
+    def core_sum(partial):
         got = swap_cores(partial[:half].astype(BF16), n_dp)
-        mine = (partial[half:] + got.astype(F32)).astype(BF16)
+        return (partial[half:] + got.astype(F32)).astype(BF16)
+
+    def chip_sum(mine):
         total = mine.astype(F32)
         for shift in range(1, chips):
             got = lax.ppermute(mine, "dp", [(i, (i + 2 * shift) % n_dp) for i in range(n_dp)])
             total = total + got.astype(F32)
         return total
 
-    gate, up, hidden_grad = sum_over_dp(gate_p), sum_over_dp(up_p), sum_over_dp(hid_p)
+    up_p = jnp.einsum("td,fd->tf", tok, up_rows, preferred_element_type=F32)
+    tok_gate, up_p = lax.optimization_barrier((tok, up_p))
+    gate_p = jnp.einsum("td,fd->tf", tok_gate, gate_rows, preferred_element_type=F32)
+    up, gate = core_sum(up_p), core_sum(gate_p)
+    cot_hid, up = lax.optimization_barrier((cot, up))
+    hid_p = jnp.einsum("td,fd->tf", cot_hid, down_weight, preferred_element_type=F32)
+    up, gate, hidden_grad = chip_sum(up), chip_sum(gate), chip_sum(core_sum(hid_p))
 
     sig = jax.nn.sigmoid(gate)
     hidden = (gate * sig * up).astype(BF16)

time: 45.9 us -> 45 us (0.980)
  starting transfers between devices: 15.2 us -> 14.5 us
    ppermute x3, waiting for transfers between devices: 6.14 us -> 5.52 us  [chip_sum(): lax.ppermute(mine, 'dp', [(i, (i + 2 * shift) % n_dp) for i in range(n_dp)])]
  transfers between devices with their start and end apart: 11 -> 11, of which waited for: 6 -> 7; matrix products, arithmetic and copies ran while one was open for 21% -> 21% of each run, Pallas kernels for 0% -> 0%
where the time goes in v2:
time: 45 us; the launch traced here: 44.7 us
  waiting for transfers between devices  15.9 us (35%)
  starting transfers between devices  14.5 us (32%)
  matrix products  9.33 us (21%)
  local copies, waits for them, and re-layouts  2.15 us (5%)
  other arithmetic  1.97 us (4%)
  between operations  0.87 us (2%)
    all_to_all x1, waiting for transfers between devices, local(): lax.all_to_all(slices.reshape(n_dp * n_tensor, 2 * rows, depth), ('dp', '...  7.91 us
    all_to_all x1, starting transfers between devices, local(): lax.all_to_all(slices.reshape(n_dp * n_tensor, 2 * rows, depth), ('dp', '...  7.3 us
    ppermute x3, waiting for transfers between devices, chip_sum(): lax.ppermute(mine, 'dp', [(i, (i + 2 * shift) % n_dp) for i in range(n_dp)])  5.52 us
    ppermute x3, starting transfers between devices, chip_sum(): lax.ppermute(mine, 'dp', [(i, (i + 2 * shift) % n_dp) for i in range(n_dp)])  3.12 us
    all_to_all x1, starting transfers between devices, local(): lax.all_to_all(shares, ('dp', 'tensor'), split_axis=0, concat_axis=0, til...  2.95 us
    dot_general x1, matrix products, local(): jnp.einsum('td,tf->df', tok, gate_grad, preferred_element_type=F32) / n_dp  2.06 us
    dot_general x1, matrix products, local(): jnp.einsum('td,tf->df', tok, up_grad, preferred_element_type=F32) / n_dp  2.05 us
    dot_general x1, matrix products, local(): jnp.einsum('tf,td->fd', hidden, cot, preferred_element_type=F32) / n_dp  2.03 us
  transfers between devices with their start and end apart: 11, of which 7 were waited for; matrix products, arithmetic and copies ran while one was open for 21% of the time, Pallas kernels for 0%

profile of v2, /device:TPU:0, one launch (start us, length us, event | category | flops | bytes accessed | tf_op | source)
XLA Modules:
  0.0 44.7 jit_solution(14583198962842582555)
XLA Ops:
  0.6 1.0 %fusion.14 = (bf16[1,4,640]{2,1,0:T(4,128)(2,1)S(1)}, bf16[1,4,640]{2,1,0:T(4,128)(2,1)S(1)}, bf16[1,4,640]{2,1,0:T(4,128)(2,1)S(1)}, bf16[1,4,640]{2,1,0:T(4,128)(2,1)S(1)}) fusion(bf16[2,2560]{1,0:T(2,128)(2,1)} %param.6, bf16[2,2560]{1,0:T(2,128)(2,1)} %param.5), kind=kLoop, calls=%fused_computation.46 | loop fusion | flops 40960 | bytes 40960 | tf_op jit(solution)/shard_map/stack | solution.py:25
  1.6 0.7 %broadcast_in_dim.2 = bf16[4,8,4,640]{3,2,1,0:T(4,128)(2,1)} broadcast(bf16[4,4,640]{2,1,0:T(4,128)(2,1)S(1)} %pad_maximum_fusion.6), dimensions={0,2,3} | broadcast | bytes 184320 | tf_op jit(solution)/shard_map/broadcast_in_dim | solution.py:26
  2.4 7.3 %all-to-all-start = ((bf16[32,4,640]{2,1,0:T(4,128)(2,1)}), bf16[32,4,640]{2,1,0:T(4,128)(2,1)S(1)}, u32[]{:S(2)}, u32[]{:S(2)}) async-start(bf16[32,4,640]{2,1,0:T(4,128)(2,1)} %bitcast.4), calls=%async_computation | async-start | bytes 327680 | tf_op jit(solution)/shard_map/all_to_all | solution.py:27
  9.7 7.9 %all-to-all-done = bf16[32,4,640]{2,1,0:T(4,128)(2,1)S(1)} async-done(((bf16[32,4,640]{2,1,0:T(4,128)(2,1)}), bf16[32,4,640]{2,1,0:T(4,128)(2,1)S(1)}, u32[]{:S(2)}, u32[]{:S(2)}) %all-to-all-start) | async-done | bytes 163872 | tf_op jit(solution)/shard_map/all_to_all | solution.py:27
  17.9 0.7 %fusion.22 = f32[64,1600]{1,0:T(8,128)S(1)} fusion(bf16[64,640]{1,0:T(8,128)(2,1)S(1)} %bitcast.37, bf16[640,1600]{0,1:T(8,128)(2,1)S(1)} %copy-done), kind=kOutput, calls=%fused_computation.54 | convolution fusion | flops 131072000 | bytes 2539520 | tf_op jit(solution)/shard_map/td,fd->tf/dot_general | solution.py:51
  18.9 0.5 %copy-done.1 = bf16[640,1600]{0,1:T(8,128)(2,1)S(1)} copy-done((bf16[640,1600]{0,1:T(8,128)(2,1)S(1)}, bf16[640,1600]{0,1:T(8,128)(2,1)}, u32[]{:S(2)}) %copy-start.1) | copy-done | bytes 2048024
  19.4 0.7 %fusion.24 = f32[64,1600]{1,0:T(8,128)S(1)} fusion(bf16[64,640]{1,0:T(8,128)(2,1)S(1)} %bitcast.38, bf16[640,1600]{0,1:T(8,128)(2,1)S(1)} %copy-done.1), kind=kOutput, calls=%fused_computation.56 | convolution fusion | flops 131072000 | bytes 2539520 | tf_op jit(solution)/shard_map/td,fd->tf/dot_general | solution.py:53
  20.4 1.4 %collective-permute-start.3 = (bf16[32,1600]{1,0:T(8,128)(2,1)S(1)}, bf16[32,1600]{1,0:T(8,128)(2,1)S(1)}, u32[]{:S(2)}, u32[]{:S(2)}) collective-permute-start(bf16[32,1600]{1,0:T(8,128)(2,1)S(1)} %add_convert_fusion), channel_id=1, source_target_pairs={{0,16},{8,24},{16,0},{24,8},{1,17},{9,25},{17,1},{25,9},{2,18},{10... | collective-permute-start | bytes 307208 | tf_op jit(solution)/shard_map/ppermute | solution.py:47
  21.8 0.7 %fusion.23 = f32[64,1600]{1,0:T(8,128)S(1)} fusion(bf16[64,640]{1,0:T(8,128)(2,1)S(1)} %bitcast.41, bf16[1600,640]{1,0:T(8,128)(2,1)S(1)} %copy-done.2), kind=kOutput, calls=%fused_computation.55 | convolution fusion | flops 131072000 | bytes 2539520 | tf_op jit(solution)/shard_map/td,fd->tf/dot_general | solution.py:56
  22.7 0.8 %collective-permute-start.5 = (bf16[32,1600]{1,0:T(8,128)(2,1)S(1)}, bf16[32,1600]{1,0:T(8,128)(2,1)S(1)}, u32[]{:S(2)}, u32[]{:S(2)}) collective-permute-start(bf16[32,1600]{1,0:T(8,128)(2,1)S(1)} %fusion.1), channel_id=1, source_target_pairs={{0,16},{8,24},{16,0},{24,8},{1,17},{9,25},{17,1},{25,9},{2,18},{10... | collective-permute-start | bytes 307208 | tf_op jit(solution)/shard_map/ppermute | solution.py:47
  24.0 0.9 %collective-permute-start.2 = (bf16[32,1600]{1,0:T(8,128)(2,1)S(1)}, bf16[32,1600]{1,0:T(8,128)(2,1)S(1)}, u32[]{:S(2)}, u32[]{:S(2)}) collective-permute-start(bf16[32,1600]{1,0:T(8,128)(2,1)S(1)} %fusion.2), channel_id=1, source_target_pairs={{0,16},{8,24},{16,0},{24,8},{1,17},{9,25},{17,1},{25,9},{2,18},{10... | collective-permute-start | bytes 307208 | tf_op jit(solution)/shard_map/ppermute | solution.py:47
  24.9 0.8 %collective-permute-done.3 = bf16[32,1600]{1,0:T(8,128)(2,1)S(1)} collective-permute-done((bf16[32,1600]{1,0:T(8,128)(2,1)S(1)}, bf16[32,1600]{1,0:T(8,128)(2,1)S(1)}, u32[]{:S(2)}, u32[]{:S(2)}) %collective-permute-start.3) | collective-permute-done | bytes 102432 | tf_op jit(solution)/shard_map/ppermute | solution.py:47
  25.7 2.8 %collective-permute-done.5 = bf16[32,1600]{1,0:T(8,128)(2,1)S(1)} collective-permute-done((bf16[32,1600]{1,0:T(8,128)(2,1)S(1)}, bf16[32,1600]{1,0:T(8,128)(2,1)S(1)}, u32[]{:S(2)}, u32[]{:S(2)}) %collective-permute-start.5) | collective-permute-done | bytes 102432 | tf_op jit(solution)/shard_map/ppermute | solution.py:47
  28.5 1.9 %collective-permute-done.2 = bf16[32,1600]{1,0:T(8,128)(2,1)S(1)} collective-permute-done((bf16[32,1600]{1,0:T(8,128)(2,1)S(1)}, bf16[32,1600]{1,0:T(8,128)(2,1)S(1)}, u32[]{:S(2)}, u32[]{:S(2)}) %collective-permute-start.2) | collective-permute-done | bytes 102432 | tf_op jit(solution)/shard_map/ppermute | solution.py:47
  30.7 0.5 %collective-permute-start.8 = (bf16[32,1600]{1,0:T(8,128)(2,1)S(1)}, bf16[32,1600]{1,0:T(8,128)(2,1)S(1)}, u32[]{:S(2)}, u32[]{:S(2)}) collective-permute-start(bf16[32,1600]{1,0:T(8,128)(2,1)S(1)} %get-tuple-element.12), channel_id=1, source_target_pairs={{0,8},{8,0},{16,24},{24,16},{1,9},{9,1},{17,25},{25,17},{2,10},{10... | collective-permute-start | bytes 307208 | tf_op jit(solution)/shard_map/ppermute | solution.py:11
  31.2 0.7 %collective-permute-done.7 = bf16[32,1600]{1,0:T(8,128)(2,1)S(1)} collective-permute-done((bf16[32,1600]{1,0:T(8,128)(2,1)S(1)}, bf16[32,1600]{1,0:T(8,128)(2,1)S(1)}, u32[]{:S(2)}, u32[]{:S(2)}) %collective-permute-start.7) | collective-permute-done | bytes 102432 | tf_op jit(solution)/shard_map/ppermute | solution.py:11
  32.0 0.5 %fusion.6 = f32[64,640]{1,0:T(8,128)S(1)} fusion(bf16[640,1600]{0,1:T(8,128)(2,1)S(1)} %copy-done, bf16[32,1600]{1,0:T(8,128)(2,1)S(1)} %get-tuple-element.14, bf16[32,1600]{1,0:T(8,128)(2,1)S(1)} %collective-permute-done.7), kind=kOutput, calls=%fused_computation.25 | convolution fusion | flops 131481600 | bytes 2416640 | tf_op jit(solution)/shard_map/tf,fd->td/dot_general | solution.py:68
  33.0 0.7 %reshape.44 = bf16[32,2,640]{2,1,0:T(2,128)(2,1)} reshape(bf16[2,2,16,640]{3,2,1,0:T(8,128)(2,1)S(1)} %reverse_select_fusion) | data formatting | bytes 163840 | tf_op jit(solution)/shard_map/reshape | solution.py:70
  33.7 2.9 %all-to-all-start.1 = ((bf16[32,2,640]{2,1,0:T(2,128)(2,1)}), bf16[32,2,640]{2,1,0:T(2,128)(2,1)S(1)}, u32[]{:S(2)}, u32[]{:S(2)}) async-start(bf16[32,2,640]{2,1,0:T(2,128)(2,1)} %reshape.44), calls=%async_computation.1 | async-start | bytes 163840 | tf_op jit(solution)/shard_map/all_to_all | solution.py:71
  36.6 2.1 %multiply_convert_fusion.2 = bf16[640,1600]{0,1:T(8,128)(2,1)} fusion(bf16[64,640]{1,0:T(8,128)(2,1)S(1)} %bitcast.39, bf16[32,1600]{1,0:T(8,128)(2,1)S(1)} %get-tuple-element.13, bf16[32,1600]{1,0:T(8,128)(2,1)S(1)} %collective-permute-done.6), kind=kOutput, calls=%fused_computation.2 | convolution fusion | flops 133529600 | bytes 2334720 | tf_op jit(solution)/shard_map/td,tf->df/dot_general | solution.py:75
  38.7 2.1 %multiply_convert_fusion.1 = bf16[640,1600]{0,1:T(8,128)(2,1)} fusion(bf16[64,640]{1,0:T(8,128)(2,1)S(1)} %bitcast.40, bf16[32,1600]{1,0:T(8,128)(2,1)S(1)} %get-tuple-element.14, bf16[32,1600]{1,0:T(8,128)(2,1)S(1)} %collective-permute-done.7), kind=kOutput, calls=%fused_computation.1 | convolution fusion | flops 133529600 | bytes 2334720 | tf_op jit(solution)/shard_map/td,tf->df/dot_general | solution.py:76
  40.7 2.0 %multiply_convert_fusion = bf16[1600,640]{1,0:T(8,128)(2,1)} fusion(bf16[64,640]{1,0:T(8,128)(2,1)S(1)} %bitcast.42, bf16[32,1600]{1,0:T(8,128)(2,1)S(1)} %get-tuple-element.12, bf16[32,1600]{1,0:T(8,128)(2,1)S(1)} %collective-permute-done.8), kind=kOutput, calls=%fused_computation | convolution fusion | flops 133529600 | bytes 2334720 | tf_op jit(solution)/shard_map/tf,td->fd/dot_general | solution.py:77
  42.8 1.3 %all-to-all-done.1 = bf16[32,2,640]{2,1,0:T(2,128)(2,1)S(1)} async-done(((bf16[32,2,640]{2,1,0:T(2,128)(2,1)}), bf16[32,2,640]{2,1,0:T(2,128)(2,1)S(1)}, u32[]{:S(2)}, u32[]{:S(2)}) %all-to-all-start.1) | async-done | bytes 81952 | tf_op jit(solution)/shard_map/all_to_all | solution.py:71
  44.1 0.7 %bitcast_reduce_fusion = bf16[4,2,640]{2,1,0:T(2,128)(2,1)} fusion(bf16[32,2,640]{2,1,0:T(2,128)(2,1)S(1)} %all-to-all-done.1), kind=kLoop, calls=%fused_computation.31 | loop fusion | flops 35840 | bytes 92160 | tf_op jit(solution)/shard_map/reduce_sum | solution.py:72
  (32 shorter events, 2.2 us)
Async XLA Ops:
  0.6 17.2 %copy-start = (bf16[640,1600]{0,1:T(8,128)(2,1)S(1)}, bf16[640,1600]{0,1:T(8,128)(2,1)}, u32[]{:S(2)}) copy-start(bf16[640,1600]{0,1:T(8,128)(2,1)} %param.8) | copy-start | bytes 6144004
  2.4 15.2 %all-to-all-start = ((bf16[32,4,640]{2,1,0:T(4,128)(2,1)}), bf16[32,4,640]{2,1,0:T(4,128)(2,1)S(1)}, u32[]{:S(2)}, u32[]{:S(2)}) async-start(bf16[32,4,640]{2,1,0:T(4,128)(2,1)} %bitcast.4), calls=%async_computation | async-start | bytes 327680 | tf_op jit(solution)/shard_map/all_to_all | solution.py:27
  17.8 1.6 %copy-start.1 = (bf16[640,1600]{0,1:T(8,128)(2,1)S(1)}, bf16[640,1600]{0,1:T(8,128)(2,1)}, u32[]{:S(2)}) copy-start(bf16[640,1600]{0,1:T(8,128)(2,1)} %param.7) | copy-start | bytes 6144004
  18.6 3.2 %copy-start.2 = (bf16[1600,640]{1,0:T(8,128)(2,1)S(1)}, bf16[1600,640]{1,0:T(8,128)(2,1)}, u32[]{:S(2)}) copy-start(bf16[1600,640]{1,0:T(8,128)(2,1)} %param.9) | copy-start | bytes 6144004
  18.7 1.7 %collective-permute-start = (bf16[32,1600]{1,0:T(8,128)(2,1)S(1)}, bf16[32,1600]{1,0:T(8,128)(2,1)S(1)}, u32[]{:S(2)}, u32[]{:S(2)}) collective-permute-start(bf16[32,1600]{1,0:T(8,128)(2,1)S(1)} %slice.106), channel_id=1, source_target_pairs={{0,8},{8,0},{16,24},{24,16},{1,9},{9,1},{17,25},{25,17},{2,10},{10... | collective-permute-start | bytes 307208 | tf_op jit(solution)/shard_map/ppermute | solution.py:11
  20.2 2.5 %collective-permute-start.4 = (bf16[32,1600]{1,0:T(8,128)(2,1)S(1)}, bf16[32,1600]{1,0:T(8,128)(2,1)S(1)}, u32[]{:S(2)}, u32[]{:S(2)}) collective-permute-start(bf16[32,1600]{1,0:T(8,128)(2,1)S(1)} %slice.104), channel_id=1, source_target_pairs={{0,8},{8,0},{16,24},{24,16},{1,9},{9,1},{17,25},{25,17},{2,10},{10... | collective-permute-start | bytes 307208 | tf_op jit(solution)/shard_map/ppermute | solution.py:11
  20.4 5.3 %collective-permute-start.3 = (bf16[32,1600]{1,0:T(8,128)(2,1)S(1)}, bf16[32,1600]{1,0:T(8,128)(2,1)S(1)}, u32[]{:S(2)}, u32[]{:S(2)}) collective-permute-start(bf16[32,1600]{1,0:T(8,128)(2,1)S(1)} %add_convert_fusion), channel_id=1, source_target_pairs={{0,16},{8,24},{16,0},{24,8},{1,17},{9,25},{17,1},{25,9},{2,18},{10... | collective-permute-start | bytes 307208 | tf_op jit(solution)/shard_map/ppermute | solution.py:47
  22.6 1.4 %collective-permute-start.1 = (bf16[32,1600]{1,0:T(8,128)(2,1)S(1)}, bf16[32,1600]{1,0:T(8,128)(2,1)S(1)}, u32[]{:S(2)}, u32[]{:S(2)}) collective-permute-start(bf16[32,1600]{1,0:T(8,128)(2,1)S(1)} %slice.105), channel_id=1, source_target_pairs={{0,8},{8,0},{16,24},{24,16},{1,9},{9,1},{17,25},{25,17},{2,10},{10... | collective-permute-start | bytes 307208 | tf_op jit(solution)/shard_map/ppermute | solution.py:11
  22.7 5.8 %collective-permute-start.5 = (bf16[32,1600]{1,0:T(8,128)(2,1)S(1)}, bf16[32,1600]{1,0:T(8,128)(2,1)S(1)}, u32[]{:S(2)}, u32[]{:S(2)}) collective-permute-start(bf16[32,1600]{1,0:T(8,128)(2,1)S(1)} %fusion.1), channel_id=1, source_target_pairs={{0,16},{8,24},{16,0},{24,8},{1,17},{9,25},{17,1},{25,9},{2,18},{10... | collective-permute-start | bytes 307208 | tf_op jit(solution)/shard_map/ppermute | solution.py:47
  24.0 6.4 %collective-permute-start.2 = (bf16[32,1600]{1,0:T(8,128)(2,1)S(1)}, bf16[32,1600]{1,0:T(8,128)(2,1)S(1)}, u32[]{:S(2)}, u32[]{:S(2)}) collective-permute-start(bf16[32,1600]{1,0:T(8,128)(2,1)S(1)} %fusion.2), channel_id=1, source_target_pairs={{0,16},{8,24},{16,0},{24,8},{1,17},{9,25},{17,1},{25,9},{2,18},{10... | collective-permute-start | bytes 307208 | tf_op jit(solution)/shard_map/ppermute | solution.py:47
  30.6 1.4 %collective-permute-start.7 = (bf16[32,1600]{1,0:T(8,128)(2,1)S(1)}, bf16[32,1600]{1,0:T(8,128)(2,1)S(1)}, u32[]{:S(2)}, u32[]{:S(2)}) collective-permute-start(bf16[32,1600]{1,0:T(8,128)(2,1)S(1)} %get-tuple-element.14), channel_id=1, source_target_pairs={{0,8},{8,0},{16,24},{24,16},{1,9},{9,1},{17,25},{25,17},{2,10},{10... | collective-permute-start | bytes 307208 | tf_op jit(solution)/shard_map/ppermute | solution.py:11
  30.7 10.1 %collective-permute-start.8 = (bf16[32,1600]{1,0:T(8,128)(2,1)S(1)}, bf16[32,1600]{1,0:T(8,128)(2,1)S(1)}, u32[]{:S(2)}, u32[]{:S(2)}) collective-permute-start(bf16[32,1600]{1,0:T(8,128)(2,1)S(1)} %get-tuple-element.12), channel_id=1, source_target_pairs={{0,8},{8,0},{16,24},{24,16},{1,9},{9,1},{17,25},{25,17},{2,10},{10... | collective-permute-start | bytes 307208 | tf_op jit(solution)/shard_map/ppermute | solution.py:11
  31.2 1.3 %collective-permute-start.6 = (bf16[32,1600]{1,0:T(8,128)(2,1)S(1)}, bf16[32,1600]{1,0:T(8,128)(2,1)S(1)}, u32[]{:S(2)}, u32[]{:S(2)}) collective-permute-start(bf16[32,1600]{1,0:T(8,128)(2,1)S(1)} %get-tuple-element.13), channel_id=1, source_target_pairs={{0,8},{8,0},{16,24},{24,16},{1,9},{9,1},{17,25},{25,17},{2,10},{10... | collective-permute-start | bytes 307208 | tf_op jit(solution)/shard_map/ppermute | solution.py:11
  33.7 10.4 %all-to-all-start.1 = ((bf16[32,2,640]{2,1,0:T(2,128)(2,1)}), bf16[32,2,640]{2,1,0:T(2,128)(2,1)S(1)}, u32[]{:S(2)}, u32[]{:S(2)}) async-start(bf16[32,2,640]{2,1,0:T(2,128)(2,1)} %reshape.44), calls=%async_computation.1 | async-start | bytes 163840 | tf_op jit(solution)/shard_map/all_to_all | solution.py:71

commit v3 on v2

--- a/solution.py
+++ b/solution.py
@@ -22,18 +22,25 @@
     core = lax.rem(lax.axis_index("dp"), 2)
 
     joined = jnp.concatenate([tokens, cotangent], axis=0)
-    slices = jnp.stack([joined[:, d * depth : (d + 1) * depth] for d in range(n_dp)])
-    slices = jnp.broadcast_to(slices[:, None], (n_dp, n_tensor, 2 * rows, depth))
+    slices = [joined[:, d * depth : (d + 1) * depth] for d in range(n_dp)]
+    even, odd = jnp.stack(slices[0::2]), jnp.stack(slices[1::2])
+    blocks = jnp.concatenate(
+        [swap_cores(jnp.where(core == 0, odd, even), n_dp), jnp.where(core == 0, even, odd)], axis=1
+    )
+    blocks = jnp.broadcast_to(blocks[:, None], (chips, n_tensor, 4 * rows, depth))
+    same_core = [
+        [(2 * chip + c) * n_tensor + t for chip in range(chips) for t in range(n_tensor)] for c in range(2)
+    ]
     both = lax.all_to_all(
-        slices.reshape(n_dp * n_tensor, 2 * rows, depth), ("dp", "tensor"), split_axis=0, concat_axis=0, tiled=True
+        blocks.reshape(chips * n_tensor, 4 * rows, depth),
+        ("dp", "tensor"),
+        split_axis=0,
+        concat_axis=0,
+        axis_index_groups=same_core,
+        tiled=True,
     )
-
-    def by_core(value):
-        value = value.reshape(chips, 2, group, depth)
-        value = jnp.where(core == 0, value[:, ::-1], value)
-        return value.transpose(1, 0, 2, 3).reshape(2 * half, depth)
-
-    tok, cot = by_core(both[:, :rows]), by_core(both[:, rows:])
+    both = both.reshape(chips * n_tensor, 2, 2, rows, depth).transpose(2, 1, 0, 3, 4)
+    tok, cot = both.reshape(2, 2 * half, depth)
 
     gate_rows, up_rows = gate_weight.T, up_weight.T
 

time: 45 us -> 47.7 us (1.060)
  blocking collectives: 0 us -> 16.2 us
  waiting for transfers between devices: 15.9 us -> 8.26 us
  starting transfers between devices: 14.5 us -> 7.57 us
  matrix products: 9.33 us -> 10.9 us
    all_to_all x0 -> x1, blocking collectives: none -> 16.2 us  [local(): lax.all_to_all(blocks.reshape(chips * n_tensor, 4 * rows, depth), ('dp',...]
    all_to_all x1 -> x0, waiting for transfers between devices: 7.91 us -> none  [local(): lax.all_to_all(slices.reshape(n_dp * n_tensor, 2 * rows, depth), ('dp', '...]
    all_to_all x1 -> x0, starting transfers between devices: 7.3 us -> none  [local(): lax.all_to_all(slices.reshape(n_dp * n_tensor, 2 * rows, depth), ('dp', '...]
    dot_general x1, matrix products: 0.75 us -> 2.31 us  [local(): jnp.einsum('td,fd->tf', cot_hid, down_weight, preferred_element_type=F32)]
    broadcast_in_dim x1, local copies, waits for them, and re-layouts: 0.71 us -> 0.01 us  [local(): jnp.broadcast_to(blocks[:, None], (chips, n_tensor, 4 * rows, depth))]
    ppermute x6 -> x7, waiting for transfers between devices: 1.18 us -> 1.64 us  [swap_cores(): return lax.ppermute(value, 'dp', [(i, i ^ 1) for i in range(n_dp)])]
    ppermute x6 -> x7, starting transfers between devices: 1.15 us -> 1.58 us  [swap_cores(): return lax.ppermute(value, 'dp', [(i, i ^ 1) for i in range(n_dp)])]
    another operation x2 -> x1, other arithmetic: 0.99 us -> 0.97 us  [local(): even, odd = (jnp.stack(slices[0::2]), jnp.stack(slices[1::2]))]
  transfers between devices with their start and end apart: 11 -> 11, of which waited for: 7 -> 6; matrix products, arithmetic and copies ran while one was open for 21% -> 23% of each run, Pallas kernels for 0% -> 0%
where the time goes in v3:
time: 47.7 us; the launch traced here: 47.4 us
  blocking collectives  16.2 us (34%)
  matrix products  10.9 us (23%)
  waiting for transfers between devices  8.26 us (17%)
  starting transfers between devices  7.57 us (16%)
  other arithmetic  1.97 us (4%)
  local copies, waits for them, and re-layouts  1.71 us (4%)
  between operations  0.87 us (2%)
    all_to_all x1, blocking collectives, local(): lax.all_to_all(blocks.reshape(chips * n_tensor, 4 * rows, depth), ('dp',...  16.2 us
    ppermute x3, waiting for transfers between devices, chip_sum(): lax.ppermute(mine, 'dp', [(i, (i + 2 * shift) % n_dp) for i in range(n_dp)])  5.33 us
    ppermute x3, starting transfers between devices, chip_sum(): lax.ppermute(mine, 'dp', [(i, (i + 2 * shift) % n_dp) for i in range(n_dp)])  3.25 us
    all_to_all x1, starting transfers between devices, local(): lax.all_to_all(shares, ('dp', 'tensor'), split_axis=0, concat_axis=0, til...  2.74 us
    dot_general x1, matrix products, local(): jnp.einsum('td,fd->tf', cot_hid, down_weight, preferred_element_type=F32)  2.31 us
    dot_general x1, matrix products, local(): jnp.einsum('td,tf->df', tok, gate_grad, preferred_element_type=F32) / n_dp  2.06 us
    dot_general x1, matrix products, local(): jnp.einsum('td,tf->df', tok, up_grad, preferred_element_type=F32) / n_dp  2.05 us
    dot_general x1, matrix products, local(): jnp.einsum('tf,td->fd', hidden, cot, preferred_element_type=F32) / n_dp  2.03 us
  transfers between devices with their start and end apart: 11, of which 6 were waited for; matrix products, arithmetic and copies ran while one was open for 23% of the time, Pallas kernels for 0%

profile of v3, /device:TPU:0, one launch (start us, length us, event | category | flops | bytes accessed | tf_op | source)
XLA Modules:
  0.0 47.4 jit_solution(5895646839327809661)
XLA Ops:
  0.7 1.0 %fusion.12 = (bf16[1,4,640]{2,1,0:T(4,128)(2,1)S(1)}, bf16[1,4,640]{2,1,0:T(4,128)(2,1)S(1)}, bf16[1,4,640]{2,1,0:T(4,128)(2,1)S(1)}, bf16[1,4,640]{2,1,0:T(4,128)(2,1)S(1)}) fusion(bf16[2,2560]{1,0:T(2,128)(2,1)} %param.6, bf16[2,2560]{1,0:T(2,128)(2,1)} %param.5), kind=kLoop, calls=%fused_computation.46 | loop fusion | flops 40960 | bytes 40960 | tf_op jit(solution)/shard_map/stack | solution.py:26
  1.7 0.5 %collective-permute-start = (bf16[2,4,640]{2,1,0:T(4,128)(2,1)S(1)}, bf16[2,4,640]{2,1,0:T(4,128)(2,1)S(1)}, u32[]{:S(2)}, u32[]{:S(2)}) collective-permute-start(bf16[2,4,640]{2,1,0:T(4,128)(2,1)S(1)} %get-tuple-element.17), channel_id=1, source_target_pairs={{0,8},{8,0},{16,24},{24,16},{1,9},{9,1},{17,25},{25,17},{2,10},{10... | collective-permute-start | bytes 30728 | tf_op jit(solution)/shard_map/ppermute | solution.py:11
  2.2 0.8 %collective-permute-done = bf16[2,4,640]{2,1,0:T(4,128)(2,1)S(1)} collective-permute-done((bf16[2,4,640]{2,1,0:T(4,128)(2,1)S(1)}, bf16[2,4,640]{2,1,0:T(4,128)(2,1)S(1)}, u32[]{:S(2)}, u32[]{:S(2)}) %collective-permute-start) | collective-permute-done | bytes 10272 | tf_op jit(solution)/shard_map/ppermute | solution.py:11
  3.0 16.2 %all_to_all.10 = bf16[16,8,640]{2,1,0:T(8,128)(2,1)S(1)} all-to-all(bf16[16,8,640]{2,1,0:T(8,128)(2,1)S(1)} %bitcast.35), channel_id=1, replica_groups={{0,1,2,3,4,5,6,7,16,17,18,19,20,21,22,23},{8,9,10,11,12,13,14,15,24,25,..., dimensions={0} | all-to-all | bytes 327680 | tf_op jit(solution)/shard_map/all_to_all | solution.py:34
  19.4 0.7 %fusion.20 = f32[64,1600]{1,0:T(8,128)S(1)} fusion(bf16[64,640]{1,0:T(8,128)(2,1)S(1)} %unstack.15, bf16[640,1600]{0,1:T(8,128)(2,1)S(1)} %copy-done), kind=kOutput, calls=%fused_computation.54 | convolution fusion | flops 131072000 | bytes 2539520 | tf_op jit(solution)/shard_map/td,fd->tf/dot_general | solution.py:58
  20.3 0.7 %copy-done.1 = bf16[640,1600]{0,1:T(8,128)(2,1)S(1)} copy-done((bf16[640,1600]{0,1:T(8,128)(2,1)S(1)}, bf16[640,1600]{0,1:T(8,128)(2,1)}, u32[]{:S(2)}) %copy-start.1) | copy-done | bytes 2048024
  21.0 0.7 %fusion.22 = f32[64,1600]{1,0:T(8,128)S(1)} fusion(bf16[64,640]{1,0:T(8,128)(2,1)S(1)} %unstack.15, bf16[640,1600]{0,1:T(8,128)(2,1)S(1)} %copy-done.1), kind=kOutput, calls=%fused_computation.56 | convolution fusion | flops 131072000 | bytes 2539520 | tf_op jit(solution)/shard_map/td,fd->tf/dot_general | solution.py:60
  22.0 1.1 %collective-permute-start.4 = (bf16[32,1600]{1,0:T(8,128)(2,1)S(1)}, bf16[32,1600]{1,0:T(8,128)(2,1)S(1)}, u32[]{:S(2)}, u32[]{:S(2)}) collective-permute-start(bf16[32,1600]{1,0:T(8,128)(2,1)S(1)} %add_convert_fusion), channel_id=1, source_target_pairs={{0,16},{8,24},{16,0},{24,8},{1,17},{9,25},{17,1},{25,9},{2,18},{10... | collective-permute-start | bytes 307208 | tf_op jit(solution)/shard_map/ppermute | solution.py:54
  23.1 2.3 %fusion.21 = f32[64,1600]{1,0:T(8,128)S(1)} fusion(bf16[64,640]{1,0:T(8,128)(2,1)S(1)} %unstack.13, bf16[1600,640]{1,0:T(8,128)(2,1)} %param.9), kind=kOutput, calls=%fused_computation.55 | convolution fusion | flops 131072000 | bytes 2539520 | tf_op jit(solution)/shard_map/td,fd->tf/dot_general | solution.py:63
  25.8 1.0 %collective-permute-start.6 = (bf16[32,1600]{1,0:T(8,128)(2,1)S(1)}, bf16[32,1600]{1,0:T(8,128)(2,1)S(1)}, u32[]{:S(2)}, u32[]{:S(2)}) collective-permute-start(bf16[32,1600]{1,0:T(8,128)(2,1)S(1)} %fusion.1), channel_id=1, source_target_pairs={{0,16},{8,24},{16,0},{24,8},{1,17},{9,25},{17,1},{25,9},{2,18},{10... | collective-permute-start | bytes 307208 | tf_op jit(solution)/shard_map/ppermute | solution.py:54
  26.9 1.1 %collective-permute-start.3 = (bf16[32,1600]{1,0:T(8,128)(2,1)S(1)}, bf16[32,1600]{1,0:T(8,128)(2,1)S(1)}, u32[]{:S(2)}, u32[]{:S(2)}) collective-permute-start(bf16[32,1600]{1,0:T(8,128)(2,1)S(1)} %fusion.2), channel_id=1, source_target_pairs={{0,16},{8,24},{16,0},{24,8},{1,17},{9,25},{17,1},{25,9},{2,18},{10... | collective-permute-start | bytes 307208 | tf_op jit(solution)/shard_map/ppermute | solution.py:54
  28.0 3.7 %collective-permute-done.6 = bf16[32,1600]{1,0:T(8,128)(2,1)S(1)} collective-permute-done((bf16[32,1600]{1,0:T(8,128)(2,1)S(1)}, bf16[32,1600]{1,0:T(8,128)(2,1)S(1)}, u32[]{:S(2)}, u32[]{:S(2)}) %collective-permute-start.6) | collective-permute-done | bytes 102432 | tf_op jit(solution)/shard_map/ppermute | solution.py:54
  31.6 1.7 %collective-permute-done.3 = bf16[32,1600]{1,0:T(8,128)(2,1)S(1)} collective-permute-done((bf16[32,1600]{1,0:T(8,128)(2,1)S(1)}, bf16[32,1600]{1,0:T(8,128)(2,1)S(1)}, u32[]{:S(2)}, u32[]{:S(2)}) %collective-permute-start.3) | collective-permute-done | bytes 102432 | tf_op jit(solution)/shard_map/ppermute | solution.py:54
  33.6 0.5 %collective-permute-start.9 = (bf16[32,1600]{1,0:T(8,128)(2,1)S(1)}, bf16[32,1600]{1,0:T(8,128)(2,1)S(1)}, u32[]{:S(2)}, u32[]{:S(2)}) collective-permute-start(bf16[32,1600]{1,0:T(8,128)(2,1)S(1)} %get-tuple-element.12), channel_id=1, source_target_pairs={{0,8},{8,0},{16,24},{24,16},{1,9},{9,1},{17,25},{25,17},{2,10},{10... | collective-permute-start | bytes 307208 | tf_op jit(solution)/shard_map/ppermute | solution.py:11
  34.1 0.7 %collective-permute-done.8 = bf16[32,1600]{1,0:T(8,128)(2,1)S(1)} collective-permute-done((bf16[32,1600]{1,0:T(8,128)(2,1)S(1)}, bf16[32,1600]{1,0:T(8,128)(2,1)S(1)}, u32[]{:S(2)}, u32[]{:S(2)}) %collective-permute-start.8) | collective-permute-done | bytes 102432 | tf_op jit(solution)/shard_map/ppermute | solution.py:11
  34.9 0.5 fusion.6
  35.4 0.5 %fusion = bf16[64,640]{1,0:T(8,128)(2,1)S(1)} fusion(f32[64,640]{1,0:T(8,128)S(1)} %fusion.6, bf16[640,1600]{0,1:T(8,128)(2,1)S(1)} %copy-done.2, bf16[32,1600]{1,0:T(8,128)(2,1)S(1)} %get-tuple-element.13, bf16[32,1600]{1,0:T(8,128)(2,1)S(1)} %collective-permute-done.7), kind=kOutput, calls=%fused_computation.4 | convolution fusion | flops 131563520 | bytes 2498560 | tf_op jit(solution)/shard_map/tf,fd->td/dot_general | solution.py:74
  35.9 0.7 %reshape.37 = bf16[32,2,640]{2,1,0:T(2,128)(2,1)} reshape(bf16[2,2,16,640]{3,2,1,0:T(8,128)(2,1)S(1)} %reverse_select_fusion) | data formatting | bytes 163840 | tf_op jit(solution)/shard_map/reshape | solution.py:77
  36.6 2.7 %all-to-all-start.1 = ((bf16[32,2,640]{2,1,0:T(2,128)(2,1)}), bf16[32,2,640]{2,1,0:T(2,128)(2,1)S(1)}, u32[]{:S(2)}, u32[]{:S(2)}) async-start(bf16[32,2,640]{2,1,0:T(2,128)(2,1)} %reshape.37), calls=%async_computation.1 | async-start | bytes 163840 | tf_op jit(solution)/shard_map/all_to_all | solution.py:78
  39.3 2.1 %multiply_convert_fusion.2 = bf16[640,1600]{0,1:T(8,128)(2,1)} fusion(bf16[64,640]{1,0:T(8,128)(2,1)S(1)} %unstack.15, bf16[32,1600]{1,0:T(8,128)(2,1)S(1)} %get-tuple-element.13, bf16[32,1600]{1,0:T(8,128)(2,1)S(1)} %collective-permute-done.7), kind=kOutput, calls=%fused_computation.2 | convolution fusion | flops 133529600 | bytes 2334720 | tf_op jit(solution)/shard_map/td,tf->df/dot_general | solution.py:82
  41.4 2.1 %multiply_convert_fusion.1 = bf16[640,1600]{0,1:T(8,128)(2,1)} fusion(bf16[64,640]{1,0:T(8,128)(2,1)S(1)} %unstack.15, bf16[32,1600]{1,0:T(8,128)(2,1)S(1)} %get-tuple-element.14, bf16[32,1600]{1,0:T(8,128)(2,1)S(1)} %collective-permute-done.8), kind=kOutput, calls=%fused_computation.1 | convolution fusion | flops 133529600 | bytes 2334720 | tf_op jit(solution)/shard_map/td,tf->df/dot_general | solution.py:83
  43.4 2.0 %multiply_convert_fusion = bf16[1600,640]{1,0:T(8,128)(2,1)} fusion(bf16[64,640]{1,0:T(8,128)(2,1)S(1)} %unstack.13, bf16[32,1600]{1,0:T(8,128)(2,1)S(1)} %get-tuple-element.12, bf16[32,1600]{1,0:T(8,128)(2,1)S(1)} %collective-permute-done.9), kind=kOutput, calls=%fused_computation | convolution fusion | flops 133529600 | bytes 2334720 | tf_op jit(solution)/shard_map/tf,td->fd/dot_general | solution.py:84
  45.5 1.3 %all-to-all-done.1 = bf16[32,2,640]{2,1,0:T(2,128)(2,1)S(1)} async-done(((bf16[32,2,640]{2,1,0:T(2,128)(2,1)}), bf16[32,2,640]{2,1,0:T(2,128)(2,1)S(1)}, u32[]{:S(2)}, u32[]{:S(2)}) %all-to-all-start.1) | async-done | bytes 81952 | tf_op jit(solution)/shard_map/all_to_all | solution.py:78
  46.8 0.7 %bitcast_reduce_fusion = bf16[4,2,640]{2,1,0:T(2,128)(2,1)} fusion(bf16[32,2,640]{2,1,0:T(2,128)(2,1)S(1)} %all-to-all-done.1), kind=kLoop, calls=%fused_computation.27 | loop fusion | flops 35840 | bytes 92160 | tf_op jit(solution)/shard_map/reduce_sum | solution.py:79
  (34 shorter events, 1.3 us)
Async XLA Ops:
  0.6 18.7 %copy-start = (bf16[640,1600]{0,1:T(8,128)(2,1)S(1)}, bf16[640,1600]{0,1:T(8,128)(2,1)}, u32[]{:S(2)}) copy-start(bf16[640,1600]{0,1:T(8,128)(2,1)} %param.8) | copy-start | bytes 6144004
  1.7 1.3 %collective-permute-start = (bf16[2,4,640]{2,1,0:T(4,128)(2,1)S(1)}, bf16[2,4,640]{2,1,0:T(4,128)(2,1)S(1)}, u32[]{:S(2)}, u32[]{:S(2)}) collective-permute-start(bf16[2,4,640]{2,1,0:T(4,128)(2,1)S(1)} %get-tuple-element.17), channel_id=1, source_target_pairs={{0,8},{8,0},{16,24},{24,16},{1,9},{9,1},{17,25},{25,17},{2,10},{10... | collective-permute-start | bytes 30728 | tf_op jit(solution)/shard_map/ppermute | solution.py:11
  19.4 1.6 %copy-start.1 = (bf16[640,1600]{0,1:T(8,128)(2,1)S(1)}, bf16[640,1600]{0,1:T(8,128)(2,1)}, u32[]{:S(2)}) copy-start(bf16[640,1600]{0,1:T(8,128)(2,1)} %param.7) | copy-start | bytes 6144004
  20.2 1.8 %collective-permute-start.1 = (bf16[32,1600]{1,0:T(8,128)(2,1)S(1)}, bf16[32,1600]{1,0:T(8,128)(2,1)S(1)}, u32[]{:S(2)}, u32[]{:S(2)}) collective-permute-start(bf16[32,1600]{1,0:T(8,128)(2,1)S(1)} %slice.98), channel_id=1, source_target_pairs={{0,8},{8,0},{16,24},{24,16},{1,9},{9,1},{17,25},{25,17},{2,10},{10... | collective-permute-start | bytes 307208 | tf_op jit(solution)/shard_map/ppermute | solution.py:11
  21.9 3.9 %collective-permute-start.5 = (bf16[32,1600]{1,0:T(8,128)(2,1)S(1)}, bf16[32,1600]{1,0:T(8,128)(2,1)S(1)}, u32[]{:S(2)}, u32[]{:S(2)}) collective-permute-start(bf16[32,1600]{1,0:T(8,128)(2,1)S(1)} %slice.96), channel_id=1, source_target_pairs={{0,8},{8,0},{16,24},{24,16},{1,9},{9,1},{17,25},{25,17},{2,10},{10... | collective-permute-start | bytes 307208 | tf_op jit(solution)/shard_map/ppermute | solution.py:11
  22.0 6.0 %collective-permute-start.4 = (bf16[32,1600]{1,0:T(8,128)(2,1)S(1)}, bf16[32,1600]{1,0:T(8,128)(2,1)S(1)}, u32[]{:S(2)}, u32[]{:S(2)}) collective-permute-start(bf16[32,1600]{1,0:T(8,128)(2,1)S(1)} %add_convert_fusion), channel_id=1, source_target_pairs={{0,16},{8,24},{16,0},{24,8},{1,17},{9,25},{17,1},{25,9},{2,18},{10... | collective-permute-start | bytes 307208 | tf_op jit(solution)/shard_map/ppermute | solution.py:54
  25.5 9.9 %copy-start.2 = (bf16[640,1600]{0,1:T(8,128)(2,1)S(1)}, bf16[640,1600]{0,1:T(8,128)(2,1)}, u32[]{:S(2)}) copy-start(bf16[640,1600]{0,1:T(8,128)(2,1)} %param.7) | copy-start | bytes 6144004
  25.5 1.4 %collective-permute-start.2 = (bf16[32,1600]{1,0:T(8,128)(2,1)S(1)}, bf16[32,1600]{1,0:T(8,128)(2,1)S(1)}, u32[]{:S(2)}, u32[]{:S(2)}) collective-permute-start(bf16[32,1600]{1,0:T(8,128)(2,1)S(1)} %slice.97), channel_id=1, source_target_pairs={{0,8},{8,0},{16,24},{24,16},{1,9},{9,1},{17,25},{25,17},{2,10},{10... | collective-permute-start | bytes 307208 | tf_op jit(solution)/shard_map/ppermute | solution.py:11
  25.8 5.9 %collective-permute-start.6 = (bf16[32,1600]{1,0:T(8,128)(2,1)S(1)}, bf16[32,1600]{1,0:T(8,128)(2,1)S(1)}, u32[]{:S(2)}, u32[]{:S(2)}) collective-permute-start(bf16[32,1600]{1,0:T(8,128)(2,1)S(1)} %fusion.1), channel_id=1, source_target_pairs={{0,16},{8,24},{16,0},{24,8},{1,17},{9,25},{17,1},{25,9},{2,18},{10... | collective-permute-start | bytes 307208 | tf_op jit(solution)/shard_map/ppermute | solution.py:54
  26.9 6.4 %collective-permute-start.3 = (bf16[32,1600]{1,0:T(8,128)(2,1)S(1)}, bf16[32,1600]{1,0:T(8,128)(2,1)S(1)}, u32[]{:S(2)}, u32[]{:S(2)}) collective-permute-start(bf16[32,1600]{1,0:T(8,128)(2,1)S(1)} %fusion.2), channel_id=1, source_target_pairs={{0,16},{8,24},{16,0},{24,8},{1,17},{9,25},{17,1},{25,9},{2,18},{10... | collective-permute-start | bytes 307208 | tf_op jit(solution)/shard_map/ppermute | solution.py:54
  33.5 1.4 %collective-permute-start.8 = (bf16[32,1600]{1,0:T(8,128)(2,1)S(1)}, bf16[32,1600]{1,0:T(8,128)(2,1)S(1)}, u32[]{:S(2)}, u32[]{:S(2)}) collective-permute-start(bf16[32,1600]{1,0:T(8,128)(2,1)S(1)} %get-tuple-element.14), channel_id=1, source_target_pairs={{0,8},{8,0},{16,24},{24,16},{1,9},{9,1},{17,25},{25,17},{2,10},{10... | collective-permute-start | bytes 307208 | tf_op jit(solution)/shard_map/ppermute | solution.py:11
  33.6 9.9 %collective-permute-start.9 = (bf16[32,1600]{1,0:T(8,128)(2,1)S(1)}, bf16[32,1600]{1,0:T(8,128)(2,1)S(1)}, u32[]{:S(2)}, u32[]{:S(2)}) collective-permute-start(bf16[32,1600]{1,0:T(8,128)(2,1)S(1)} %get-tuple-element.12), channel_id=1, source_target_pairs={{0,8},{8,0},{16,24},{24,16},{1,9},{9,1},{17,25},{25,17},{2,10},{10... | collective-permute-start | bytes 307208 | tf_op jit(solution)/shard_map/ppermute | solution.py:11
  34.1 1.3 %collective-permute-start.7 = (bf16[32,1600]{1,0:T(8,128)(2,1)S(1)}, bf16[32,1600]{1,0:T(8,128)(2,1)S(1)}, u32[]{:S(2)}, u32[]{:S(2)}) collective-permute-start(bf16[32,1600]{1,0:T(8,128)(2,1)S(1)} %get-tuple-element.13), channel_id=1, source_target_pairs={{0,8},{8,0},{16,24},{24,16},{1,9},{9,1},{17,25},{25,17},{2,10},{10... | collective-permute-start | bytes 307208 | tf_op jit(solution)/shard_map/ppermute | solution.py:11
  36.6 10.2 %all-to-all-start.1 = ((bf16[32,2,640]{2,1,0:T(2,128)(2,1)}), bf16[32,2,640]{2,1,0:T(2,128)(2,1)S(1)}, u32[]{:S(2)}, u32[]{:S(2)}) async-start(bf16[32,2,640]{2,1,0:T(2,128)(2,1)} %reshape.37), calls=%async_computation.1 | async-start | bytes 163840 | tf_op jit(solution)/shard_map/all_to_all | solution.py:78

commit v4 on v2

--- a/solution.py
+++ b/solution.py
@@ -49,10 +49,11 @@
         return total
 
     up_p = jnp.einsum("td,fd->tf", tok, up_rows, preferred_element_type=F32)
-    tok_gate, up_p = lax.optimization_barrier((tok, up_p))
+    up = core_sum(up_p)
+    tok_gate, cot_hid, up = lax.optimization_barrier((tok, cot, up))
     gate_p = jnp.einsum("td,fd->tf", tok_gate, gate_rows, preferred_element_type=F32)
-    up, gate = core_sum(up_p), core_sum(gate_p)
-    cot_hid, up = lax.optimization_barrier((cot, up))
+    gate = core_sum(gate_p)
+    cot_hid, gate_p = lax.optimization_barrier((cot_hid, gate_p))
     hid_p = jnp.einsum("td,fd->tf", cot_hid, down_weight, preferred_element_type=F32)
     up, gate, hidden_grad = chip_sum(up), chip_sum(gate), chip_sum(core_sum(hid_p))
 

time: 45 us -> 45.7 us (1.016)
  starting transfers between devices: 14.5 us -> 15.3 us
  local copies, waits for them, and re-layouts: 2.15 us -> 1.66 us
    ppermute x6, waiting for transfers between devices: 1.18 us -> 1.95 us  [swap_cores(): return lax.ppermute(value, 'dp', [(i, i ^ 1) for i in range(n_dp)])]
    unnamed x6, local copies, waits for them, and re-layouts: 0.51 us -> 0.02 us
  transfers between devices with their start and end apart: 11 -> 11, of which waited for: 7 -> 6; matrix products, arithmetic and copies ran while one was open for 21% -> 21% of each run, Pallas kernels for 0% -> 0%
where the time goes in v4:
time: 45.7 us; the launch traced here: 45.5 us
  waiting for transfers between devices  16.3 us (36%)
  starting transfers between devices  15.3 us (33%)
  matrix products  9.33 us (20%)
  other arithmetic  1.98 us (4%)
  local copies, waits for them, and re-layouts  1.66 us (4%)
  between operations  0.86 us (2%)
    all_to_all x1, waiting for transfers between devices, local(): lax.all_to_all(slices.reshape(n_dp * n_tensor, 2 * rows, depth), ('dp', '...  7.91 us
    all_to_all x1, starting transfers between devices, local(): lax.all_to_all(slices.reshape(n_dp * n_tensor, 2 * rows, depth), ('dp', '...  7.3 us
    ppermute x3, waiting for transfers between devices, chip_sum(): lax.ppermute(mine, 'dp', [(i, (i + 2 * shift) % n_dp) for i in range(n_dp)])  5.14 us
    ppermute x3, starting transfers between devices, chip_sum(): lax.ppermute(mine, 'dp', [(i, (i + 2 * shift) % n_dp) for i in range(n_dp)])  3.4 us
    all_to_all x1, starting transfers between devices, local(): lax.all_to_all(shares, ('dp', 'tensor'), split_axis=0, concat_axis=0, til...  3.16 us
    dot_general x1, matrix products, local(): jnp.einsum('td,tf->df', tok, gate_grad, preferred_element_type=F32) / n_dp  2.05 us
    dot_general x1, matrix products, local(): jnp.einsum('td,tf->df', tok, up_grad, preferred_element_type=F32) / n_dp  2.05 us
    dot_general x1, matrix products, local(): jnp.einsum('tf,td->fd', hidden, cot, preferred_element_type=F32) / n_dp  2.03 us
  transfers between devices with their start and end apart: 11, of which 6 were waited for; matrix products, arithmetic and copies ran while one was open for 21% of the time, Pallas kernels for 0%

profile of v4, /device:TPU:0, one launch (start us, length us, event | category | flops | bytes accessed | tf_op | source)
XLA Modules:
  0.0 45.5 jit_solution(4443575272473725426)
XLA Ops:
  0.6 1.0 %fusion.15 = (bf16[1,4,640]{2,1,0:T(4,128)(2,1)S(1)}, bf16[1,4,640]{2,1,0:T(4,128)(2,1)S(1)}, bf16[1,4,640]{2,1,0:T(4,128)(2,1)S(1)}, bf16[1,4,640]{2,1,0:T(4,128)(2,1)S(1)}) fusion(bf16[2,2560]{1,0:T(2,128)(2,1)} %param.6, bf16[2,2560]{1,0:T(2,128)(2,1)} %param.5), kind=kLoop, calls=%fused_computation.47 | loop fusion | flops 40960 | bytes 40960 | tf_op jit(solution)/shard_map/stack | solution.py:25
  1.6 0.7 %broadcast_in_dim.2 = bf16[4,8,4,640]{3,2,1,0:T(4,128)(2,1)} broadcast(bf16[4,4,640]{2,1,0:T(4,128)(2,1)S(1)} %pad_maximum_fusion.6), dimensions={0,2,3} | broadcast | bytes 184320 | tf_op jit(solution)/shard_map/broadcast_in_dim | solution.py:26
  2.4 7.3 %all-to-all-start = ((bf16[32,4,640]{2,1,0:T(4,128)(2,1)}), bf16[32,4,640]{2,1,0:T(4,128)(2,1)S(1)}, u32[]{:S(2)}, u32[]{:S(2)}) async-start(bf16[32,4,640]{2,1,0:T(4,128)(2,1)} %bitcast.4), calls=%async_computation | async-start | bytes 327680 | tf_op jit(solution)/shard_map/all_to_all | solution.py:27
  9.7 7.9 %all-to-all-done = bf16[32,4,640]{2,1,0:T(4,128)(2,1)S(1)} async-done(((bf16[32,4,640]{2,1,0:T(4,128)(2,1)}), bf16[32,4,640]{2,1,0:T(4,128)(2,1)S(1)}, u32[]{:S(2)}, u32[]{:S(2)}) %all-to-all-start) | async-done | bytes 163872 | tf_op jit(solution)/shard_map/all_to_all | solution.py:27
  17.9 0.7 %fusion.23 = f32[64,1600]{1,0:T(8,128)S(1)} fusion(bf16[64,640]{1,0:T(8,128)(2,1)S(1)} %bitcast.37, bf16[640,1600]{0,1:T(8,128)(2,1)S(1)} %copy-done), kind=kOutput, calls=%fused_computation.55 | convolution fusion | flops 131072000 | bytes 2539520 | tf_op jit(solution)/shard_map/td,fd->tf/dot_general | solution.py:51
  18.9 1.2 %collective-permute-done = bf16[32,1600]{1,0:T(8,128)(2,1)S(1)} collective-permute-done((bf16[32,1600]{1,0:T(8,128)(2,1)S(1)}, bf16[32,1600]{1,0:T(8,128)(2,1)S(1)}, u32[]{:S(2)}, u32[]{:S(2)}) %collective-permute-start) | collective-permute-done | bytes 102432 | tf_op jit(solution)/shard_map/ppermute | solution.py:11
  20.1 1.3 %collective-permute-start.3 = (bf16[32,1600]{1,0:T(8,128)(2,1)S(1)}, bf16[32,1600]{1,0:T(8,128)(2,1)S(1)}, u32[]{:S(2)}, u32[]{:S(2)}) collective-permute-start(bf16[32,1600]{1,0:T(8,128)(2,1)S(1)} %fusion.3), channel_id=1, source_target_pairs={{0,16},{8,24},{16,0},{24,8},{1,17},{9,25},{17,1},{25,9},{2,18},{10... | collective-permute-start | bytes 307208 | tf_op jit(solution)/shard_map/ppermute | solution.py:47
  21.3 0.7 %fusion.24 = f32[64,1600]{1,0:T(8,128)S(1)} fusion(bf16[64,640]{1,0:T(8,128)(2,1)S(1)} %bitcast.38, bf16[640,1600]{0,1:T(8,128)(2,1)S(1)} %copy-done.1), kind=kOutput, calls=%fused_computation.56 | convolution fusion | flops 131072000 | bytes 2539520 | tf_op jit(solution)/shard_map/td,fd->tf/dot_general | solution.py:54
  22.2 0.7 %fusion.25 = f32[64,1600]{1,0:T(8,128)S(1)} fusion(bf16[64,640]{1,0:T(8,128)(2,1)S(1)} %bitcast.41, bf16[1600,640]{1,0:T(8,128)(2,1)S(1)} %copy-done.2), kind=kOutput, calls=%fused_computation.57 | convolution fusion | flops 131072000 | bytes 2539520 | tf_op jit(solution)/shard_map/td,fd->tf/dot_general | solution.py:57
  23.0 0.6 %collective-permute-start.1 = (bf16[32,1600]{1,0:T(8,128)(2,1)S(1)}, bf16[32,1600]{1,0:T(8,128)(2,1)S(1)}, u32[]{:S(2)}, u32[]{:S(2)}) collective-permute-start(bf16[32,1600]{1,0:T(8,128)(2,1)S(1)} %slice.108), channel_id=1, source_target_pairs={{0,8},{8,0},{16,24},{24,16},{1,9},{9,1},{17,25},{25,17},{2,10},{10... | collective-permute-start | bytes 307208 | tf_op jit(solution)/shard_map/ppermute | solution.py:11
  23.6 0.9 %collective-permute-start.5 = (bf16[32,1600]{1,0:T(8,128)(2,1)S(1)}, bf16[32,1600]{1,0:T(8,128)(2,1)S(1)}, u32[]{:S(2)}, u32[]{:S(2)}) collective-permute-start(bf16[32,1600]{1,0:T(8,128)(2,1)S(1)} %fusion.1), channel_id=1, source_target_pairs={{0,16},{8,24},{16,0},{24,8},{1,17},{9,25},{17,1},{25,9},{2,18},{10... | collective-permute-start | bytes 307208 | tf_op jit(solution)/shard_map/ppermute | solution.py:47
  24.5 1.2 %collective-permute-start.2 = (bf16[32,1600]{1,0:T(8,128)(2,1)S(1)}, bf16[32,1600]{1,0:T(8,128)(2,1)S(1)}, u32[]{:S(2)}, u32[]{:S(2)}) collective-permute-start(bf16[32,1600]{1,0:T(8,128)(2,1)S(1)} %fusion.2), channel_id=1, source_target_pairs={{0,16},{8,24},{16,0},{24,8},{1,17},{9,25},{17,1},{25,9},{2,18},{10... | collective-permute-start | bytes 307208 | tf_op jit(solution)/shard_map/ppermute | solution.py:47
  25.8 3.7 %collective-permute-done.5 = bf16[32,1600]{1,0:T(8,128)(2,1)S(1)} collective-permute-done((bf16[32,1600]{1,0:T(8,128)(2,1)S(1)}, bf16[32,1600]{1,0:T(8,128)(2,1)S(1)}, u32[]{:S(2)}, u32[]{:S(2)}) %collective-permute-start.5) | collective-permute-done | bytes 102432 | tf_op jit(solution)/shard_map/ppermute | solution.py:47
  29.5 1.4 %collective-permute-done.2 = bf16[32,1600]{1,0:T(8,128)(2,1)S(1)} collective-permute-done((bf16[32,1600]{1,0:T(8,128)(2,1)S(1)}, bf16[32,1600]{1,0:T(8,128)(2,1)S(1)}, u32[]{:S(2)}, u32[]{:S(2)}) %collective-permute-start.2) | collective-permute-done | bytes 102432 | tf_op jit(solution)/shard_map/ppermute | solution.py:47
  31.2 0.5 %collective-permute-start.8 = (bf16[32,1600]{1,0:T(8,128)(2,1)S(1)}, bf16[32,1600]{1,0:T(8,128)(2,1)S(1)}, u32[]{:S(2)}, u32[]{:S(2)}) collective-permute-start(bf16[32,1600]{1,0:T(8,128)(2,1)S(1)} %get-tuple-element.12), channel_id=1, source_target_pairs={{0,8},{8,0},{16,24},{24,16},{1,9},{9,1},{17,25},{25,17},{2,10},{10... | collective-permute-start | bytes 307208 | tf_op jit(solution)/shard_map/ppermute | solution.py:11
  31.7 0.7 %collective-permute-done.7 = bf16[32,1600]{1,0:T(8,128)(2,1)S(1)} collective-permute-done((bf16[32,1600]{1,0:T(8,128)(2,1)S(1)}, bf16[32,1600]{1,0:T(8,128)(2,1)S(1)}, u32[]{:S(2)}, u32[]{:S(2)}) %collective-permute-start.7) | collective-permute-done | bytes 102432 | tf_op jit(solution)/shard_map/ppermute | solution.py:11
  32.5 0.5 %fusion.7 = f32[64,640]{1,0:T(8,128)S(1)} fusion(bf16[640,1600]{0,1:T(8,128)(2,1)S(1)} %copy-done, bf16[32,1600]{1,0:T(8,128)(2,1)S(1)} %get-tuple-element.14, bf16[32,1600]{1,0:T(8,128)(2,1)S(1)} %collective-permute-done.7), kind=kOutput, calls=%fused_computation.26 | convolution fusion | flops 131481600 | bytes 2416640 | tf_op jit(solution)/shard_map/tf,fd->td/dot_general | solution.py:69
  33.5 0.7 %reshape.44 = bf16[32,2,640]{2,1,0:T(2,128)(2,1)} reshape(bf16[2,2,16,640]{3,2,1,0:T(8,128)(2,1)S(1)} %reverse_select_fusion) | data formatting | bytes 163840 | tf_op jit(solution)/shard_map/reshape | solution.py:71
  34.2 3.2 %all-to-all-start.1 = ((bf16[32,2,640]{2,1,0:T(2,128)(2,1)}), bf16[32,2,640]{2,1,0:T(2,128)(2,1)S(1)}, u32[]{:S(2)}, u32[]{:S(2)}) async-start(bf16[32,2,640]{2,1,0:T(2,128)(2,1)} %reshape.44), calls=%async_computation.1 | async-start | bytes 163840 | tf_op jit(solution)/shard_map/all_to_all | solution.py:72
  37.4 2.1 %multiply_convert_fusion.2 = bf16[640,1600]{0,1:T(8,128)(2,1)} fusion(bf16[64,640]{1,0:T(8,128)(2,1)S(1)} %bitcast.39, bf16[32,1600]{1,0:T(8,128)(2,1)S(1)} %get-tuple-element.13, bf16[32,1600]{1,0:T(8,128)(2,1)S(1)} %collective-permute-done.6), kind=kOutput, calls=%fused_computation.2 | convolution fusion | flops 133529600 | bytes 2334720 | tf_op jit(solution)/shard_map/td,tf->df/dot_general | solution.py:76
  39.4 2.1 %multiply_convert_fusion.1 = bf16[640,1600]{0,1:T(8,128)(2,1)} fusion(bf16[64,640]{1,0:T(8,128)(2,1)S(1)} %bitcast.40, bf16[32,1600]{1,0:T(8,128)(2,1)S(1)} %get-tuple-element.14, bf16[32,1600]{1,0:T(8,128)(2,1)S(1)} %collective-permute-done.7), kind=kOutput, calls=%fused_computation.1 | convolution fusion | flops 133529600 | bytes 2334720 | tf_op jit(solution)/shard_map/td,tf->df/dot_general | solution.py:77
  41.5 2.0 %multiply_convert_fusion = bf16[1600,640]{1,0:T(8,128)(2,1)} fusion(bf16[64,640]{1,0:T(8,128)(2,1)S(1)} %bitcast.42, bf16[32,1600]{1,0:T(8,128)(2,1)S(1)} %get-tuple-element.12, bf16[32,1600]{1,0:T(8,128)(2,1)S(1)} %collective-permute-done.8), kind=kOutput, calls=%fused_computation | convolution fusion | flops 133529600 | bytes 2334720 | tf_op jit(solution)/shard_map/tf,td->fd/dot_general | solution.py:78
  43.5 1.3 %all-to-all-done.1 = bf16[32,2,640]{2,1,0:T(2,128)(2,1)S(1)} async-done(((bf16[32,2,640]{2,1,0:T(2,128)(2,1)}), bf16[32,2,640]{2,1,0:T(2,128)(2,1)S(1)}, u32[]{:S(2)}, u32[]{:S(2)}) %all-to-all-start.1) | async-done | bytes 81952 | tf_op jit(solution)/shard_map/all_to_all | solution.py:72
  44.8 0.7 %bitcast_reduce_fusion = bf16[4,2,640]{2,1,0:T(2,128)(2,1)} fusion(bf16[32,2,640]{2,1,0:T(2,128)(2,1)S(1)} %all-to-all-done.1), kind=kLoop, calls=%fused_computation.32 | loop fusion | flops 35840 | bytes 92160 | tf_op jit(solution)/shard_map/reduce_sum | solution.py:73
  (32 shorter events, 1.6 us)
Async XLA Ops:
  0.6 17.2 %copy-start = (bf16[640,1600]{0,1:T(8,128)(2,1)S(1)}, bf16[640,1600]{0,1:T(8,128)(2,1)}, u32[]{:S(2)}) copy-start(bf16[640,1600]{0,1:T(8,128)(2,1)} %param.8) | copy-start | bytes 6144004
  2.4 15.2 %all-to-all-start = ((bf16[32,4,640]{2,1,0:T(4,128)(2,1)}), bf16[32,4,640]{2,1,0:T(4,128)(2,1)S(1)}, u32[]{:S(2)}, u32[]{:S(2)}) async-start(bf16[32,4,640]{2,1,0:T(4,128)(2,1)} %bitcast.4), calls=%async_computation | async-start | bytes 327680 | tf_op jit(solution)/shard_map/all_to_all | solution.py:27
  17.8 3.6 %copy-start.1 = (bf16[640,1600]{0,1:T(8,128)(2,1)S(1)}, bf16[640,1600]{0,1:T(8,128)(2,1)}, u32[]{:S(2)}) copy-start(bf16[640,1600]{0,1:T(8,128)(2,1)} %param.7) | copy-start | bytes 6144004
  18.6 3.6 %copy-start.2 = (bf16[1600,640]{1,0:T(8,128)(2,1)S(1)}, bf16[1600,640]{1,0:T(8,128)(2,1)}, u32[]{:S(2)}) copy-start(bf16[1600,640]{1,0:T(8,128)(2,1)} %param.9) | copy-start | bytes 6144004
  18.7 1.4 %collective-permute-start = (bf16[32,1600]{1,0:T(8,128)(2,1)S(1)}, bf16[32,1600]{1,0:T(8,128)(2,1)S(1)}, u32[]{:S(2)}, u32[]{:S(2)}) collective-permute-start(bf16[32,1600]{1,0:T(8,128)(2,1)S(1)} %slice.109), channel_id=1, source_target_pairs={{0,8},{8,0},{16,24},{24,16},{1,9},{9,1},{17,25},{25,17},{2,10},{10... | collective-permute-start | bytes 307208 | tf_op jit(solution)/shard_map/ppermute | solution.py:11
  20.1 5.7 %collective-permute-start.3 = (bf16[32,1600]{1,0:T(8,128)(2,1)S(1)}, bf16[32,1600]{1,0:T(8,128)(2,1)S(1)}, u32[]{:S(2)}, u32[]{:S(2)}) collective-permute-start(bf16[32,1600]{1,0:T(8,128)(2,1)S(1)} %fusion.3), channel_id=1, source_target_pairs={{0,16},{8,24},{16,0},{24,8},{1,17},{9,25},{17,1},{25,9},{2,18},{10... | collective-permute-start | bytes 307208 | tf_op jit(solution)/shard_map/ppermute | solution.py:47
  22.1 1.4 %collective-permute-start.4 = (bf16[32,1600]{1,0:T(8,128)(2,1)S(1)}, bf16[32,1600]{1,0:T(8,128)(2,1)S(1)}, u32[]{:S(2)}, u32[]{:S(2)}) collective-permute-start(bf16[32,1600]{1,0:T(8,128)(2,1)S(1)} %slice.107), channel_id=1, source_target_pairs={{0,8},{8,0},{16,24},{24,16},{1,9},{9,1},{17,25},{25,17},{2,10},{10... | collective-permute-start | bytes 307208 | tf_op jit(solution)/shard_map/ppermute | solution.py:11
  23.0 1.5 %collective-permute-start.1 = (bf16[32,1600]{1,0:T(8,128)(2,1)S(1)}, bf16[32,1600]{1,0:T(8,128)(2,1)S(1)}, u32[]{:S(2)}, u32[]{:S(2)}) collective-permute-start(bf16[32,1600]{1,0:T(8,128)(2,1)S(1)} %slice.108), channel_id=1, source_target_pairs={{0,8},{8,0},{16,24},{24,16},{1,9},{9,1},{17,25},{25,17},{2,10},{10... | collective-permute-start | bytes 307208 | tf_op jit(solution)/shard_map/ppermute | solution.py:11
  23.6 5.9 %collective-permute-start.5 = (bf16[32,1600]{1,0:T(8,128)(2,1)S(1)}, bf16[32,1600]{1,0:T(8,128)(2,1)S(1)}, u32[]{:S(2)}, u32[]{:S(2)}) collective-permute-start(bf16[32,1600]{1,0:T(8,128)(2,1)S(1)} %fusion.1), channel_id=1, source_target_pairs={{0,16},{8,24},{16,0},{24,8},{1,17},{9,25},{17,1},{25,9},{2,18},{10... | collective-permute-start | bytes 307208 | tf_op jit(solution)/shard_map/ppermute | solution.py:47
  24.5 6.4 %collective-permute-start.2 = (bf16[32,1600]{1,0:T(8,128)(2,1)S(1)}, bf16[32,1600]{1,0:T(8,128)(2,1)S(1)}, u32[]{:S(2)}, u32[]{:S(2)}) collective-permute-start(bf16[32,1600]{1,0:T(8,128)(2,1)S(1)} %fusion.2), channel_id=1, source_target_pairs={{0,16},{8,24},{16,0},{24,8},{1,17},{9,25},{17,1},{25,9},{2,18},{10... | collective-permute-start | bytes 307208 | tf_op jit(solution)/shard_map/ppermute | solution.py:47
  31.1 1.4 %collective-permute-start.7 = (bf16[32,1600]{1,0:T(8,128)(2,1)S(1)}, bf16[32,1600]{1,0:T(8,128)(2,1)S(1)}, u32[]{:S(2)}, u32[]{:S(2)}) collective-permute-start(bf16[32,1600]{1,0:T(8,128)(2,1)S(1)} %get-tuple-element.14), channel_id=1, source_target_pairs={{0,8},{8,0},{16,24},{24,16},{1,9},{9,1},{17,25},{25,17},{2,10},{10... | collective-permute-start | bytes 307208 | tf_op jit(solution)/shard_map/ppermute | solution.py:11
  31.2 10.3 %collective-permute-start.8 = (bf16[32,1600]{1,0:T(8,128)(2,1)S(1)}, bf16[32,1600]{1,0:T(8,128)(2,1)S(1)}, u32[]{:S(2)}, u32[]{:S(2)}) collective-permute-start(bf16[32,1600]{1,0:T(8,128)(2,1)S(1)} %get-tuple-element.12), channel_id=1, source_target_pairs={{0,8},{8,0},{16,24},{24,16},{1,9},{9,1},{17,25},{25,17},{2,10},{10... | collective-permute-start | bytes 307208 | tf_op jit(solution)/shard_map/ppermute | solution.py:11
  31.7 1.3 %collective-permute-start.6 = (bf16[32,1600]{1,0:T(8,128)(2,1)S(1)}, bf16[32,1600]{1,0:T(8,128)(2,1)S(1)}, u32[]{:S(2)}, u32[]{:S(2)}) collective-permute-start(bf16[32,1600]{1,0:T(8,128)(2,1)S(1)} %get-tuple-element.13), channel_id=1, source_target_pairs={{0,8},{8,0},{16,24},{24,16},{1,9},{9,1},{17,25},{25,17},{2,10},{10... | collective-permute-start | bytes 307208 | tf_op jit(solution)/shard_map/ppermute | solution.py:11
  34.2 10.6 %all-to-all-start.1 = ((bf16[32,2,640]{2,1,0:T(2,128)(2,1)}), bf16[32,2,640]{2,1,0:T(2,128)(2,1)S(1)}, u32[]{:S(2)}, u32[]{:S(2)}) async-start(bf16[32,2,640]{2,1,0:T(2,128)(2,1)} %reshape.44), calls=%async_computation.1 | async-start | bytes 163840 | tf_op jit(solution)/shard_map/all_to_all | solution.py:72

commit v5 on v2

--- a/solution.py
+++ b/solution.py
@@ -48,26 +48,44 @@
             total = total + got.astype(F32)
         return total
 
-    up_p = jnp.einsum("td,fd->tf", tok, up_rows, preferred_element_type=F32)
-    tok_gate, up_p = lax.optimization_barrier((tok, up_p))
+    hid_p = jnp.einsum("td,fd->tf", cot, down_weight, preferred_element_type=F32)
+    tok_up, hid_p = lax.optimization_barrier((tok, hid_p))
+    up_p = jnp.einsum("td,fd->tf", tok_up, up_rows, preferred_element_type=F32)
+    hidden_grad, up = core_sum(hid_p), core_sum(up_p)
+    tok_gate, hidden_grad = lax.optimization_barrier((tok, hidden_grad))
     gate_p = jnp.einsum("td,fd->tf", tok_gate, gate_rows, preferred_element_type=F32)
-    up, gate = core_sum(up_p), core_sum(gate_p)
-    cot_hid, up = lax.optimization_barrier((cot, up))
-    hid_p = jnp.einsum("td,fd->tf", cot_hid, down_weight, preferred_element_type=F32)
-    up, gate, hidden_grad = chip_sum(up), chip_sum(gate), chip_sum(core_sum(hid_p))
+    hidden_grad, up, gate = chip_sum(hidden_grad), chip_sum(up), core_sum(gate_p)
 
-    sig = jax.nn.sigmoid(gate)
-    hidden = (gate * sig * up).astype(BF16)
-    up_grad = (hidden_grad * gate * sig).astype(BF16)
-    gate_grad = (hidden_grad * up * sig * (1.0 + gate * (1.0 - sig))).astype(BF16)
-    gate_grad, up_grad, hidden = (
-        jnp.concatenate([swap_cores(value, n_dp), value], axis=0) for value in (gate_grad, up_grad, hidden)
-    )
+    def both_cores(value):
+        return jnp.concatenate([swap_cores(value, n_dp), value], axis=0)
 
-    total = jnp.einsum("tf,fd->td", gate_grad, gate_rows, preferred_element_type=F32)
-    total = total + jnp.einsum("tf,fd->td", up_grad, up_rows, preferred_element_type=F32)
+    first = units // 256 * 128
+    spans = [slice(0, first), slice(first, units)] if first else [slice(0, units)]
+    packed, hidden = [], []
+    for span in spans:
+        part_gate, part_up, part_hid = chip_sum(gate[:, span]), up[:, span], hidden_grad[:, span]
+        sig = jax.nn.sigmoid(part_gate)
+        grads = [
+            (part_hid * part_up * sig * (1.0 + part_gate * (1.0 - sig))).astype(BF16),
+            (part_hid * part_gate * sig).astype(BF16),
+        ]
+        grads = jnp.concatenate(grads, axis=1)
+        packed.append((swap_cores(grads, n_dp), grads))
+        hidden.append((part_gate * sig * part_up).astype(BF16))
+    hidden = jnp.concatenate(hidden, axis=1)
+    total, parts = None, []
+    for span, (other, own) in zip(spans, packed):
+        if total is not None:
+            total, other = lax.optimization_barrier((total, other))
+        parts.append(jnp.split(jnp.concatenate([other, own], axis=0), 2, axis=1))
+        part = jnp.einsum("tf,fd->td", parts[-1][0], gate_rows[span], preferred_element_type=F32)
+        part = part + jnp.einsum("tf,fd->td", parts[-1][1], up_rows[span], preferred_element_type=F32)
+        total = part if total is None else total + part
+    gate_grad, up_grad = (jnp.concatenate(values, axis=1) for values in zip(*parts))
     shares = total.astype(BF16).reshape(2, chips, group, depth).transpose(1, 0, 2, 3)
     shares = jnp.where(core == 0, shares[:, ::-1], shares).reshape(n_dp * n_tensor, rows, depth)
+    shares, tok, cot, hidden = lax.optimization_barrier((shares, tok, cot, hidden))
+    hidden = both_cores(hidden)
     shares = lax.all_to_all(shares, ("dp", "tensor"), split_axis=0, concat_axis=0, tiled=True)
     shares = jnp.sum(shares.astype(F32).reshape(n_dp, n_tensor, rows, depth), axis=1)
     input_grad = shares.transpose(1, 0, 2).reshape(rows, width).astype(BF16)

time: 45 us -> 44.8 us (level)
  waiting for transfers between devices: 15.9 us -> 14 us
  starting transfers between devices: 14.5 us -> 15.5 us
    ppermute x3 -> x4, waiting for transfers between devices: 5.52 us -> 4.07 us  [chip_sum(): lax.ppermute(mine, 'dp', [(i, (i + 2 * shift) % n_dp) for i in range(n_dp)])]
    ppermute x3 -> x4, starting transfers between devices: 3.12 us -> 4.3 us  [chip_sum(): lax.ppermute(mine, 'dp', [(i, (i + 2 * shift) % n_dp) for i in range(n_dp)])]
    dot_general x4 -> x6, matrix products: 2.44 us -> 2.72 us  [the longest x1 0.75 us: local(): jnp.einsum('td,fd->tf', cot, down_weight, preferred_element_type=F32)]
  transfers between devices with their start and end apart: 11 -> 12, of which waited for: 7 -> 8; matrix products, arithmetic and copies ran while one was open for 21% -> 20% of each run, Pallas kernels for 0% -> 0%
where the time goes in v5:
time: 44.8 us; the launch traced here: 44.5 us
  starting transfers between devices  15.5 us (35%)
  waiting for transfers between devices  14 us (31%)
  matrix products  9.62 us (21%)
  other arithmetic  2.25 us (5%)
  local copies, waits for them, and re-layouts  2.17 us (5%)
  between operations  0.95 us (2%)
    all_to_all x1, waiting for transfers between devices, local(): lax.all_to_all(slices.reshape(n_dp * n_tensor, 2 * rows, depth), ('dp', '...  7.91 us
    all_to_all x1, starting transfers between devices, local(): lax.all_to_all(slices.reshape(n_dp * n_tensor, 2 * rows, depth), ('dp', '...  7.3 us
    ppermute x4, starting transfers between devices, chip_sum(): lax.ppermute(mine, 'dp', [(i, (i + 2 * shift) % n_dp) for i in range(n_dp)])  4.3 us
    ppermute x4, waiting for transfers between devices, chip_sum(): lax.ppermute(mine, 'dp', [(i, (i + 2 * shift) % n_dp) for i in range(n_dp)])  4.07 us
    all_to_all x1, starting transfers between devices, local(): lax.all_to_all(shares, ('dp', 'tensor'), split_axis=0, concat_axis=0, til...  2.95 us
    dot_general x1, matrix products, local(): jnp.einsum('td,tf->df', tok, up_grad, preferred_element_type=F32) / n_dp  2.06 us
    dot_general x1, matrix products, local(): jnp.einsum('td,tf->df', tok, gate_grad, preferred_element_type=F32) / n_dp  2.06 us
    dot_general x1, matrix products, local(): jnp.einsum('tf,td->fd', hidden, cot, preferred_element_type=F32) / n_dp  2.04 us
  transfers between devices with their start and end apart: 12, of which 8 were waited for; matrix products, arithmetic and copies ran while one was open for 20% of the time, Pallas kernels for 0%

profile of v5, /device:TPU:0, one launch (start us, length us, event | category | flops | bytes accessed | tf_op | source)
XLA Modules:
  0.0 44.5 jit_solution(9916750033010302309)
XLA Ops:
  0.6 1.0 %fusion.25 = (bf16[1,4,640]{2,1,0:T(4,128)(2,1)S(1)}, bf16[1,4,640]{2,1,0:T(4,128)(2,1)S(1)}, bf16[1,4,640]{2,1,0:T(4,128)(2,1)S(1)}, bf16[1,4,640]{2,1,0:T(4,128)(2,1)S(1)}) fusion(bf16[2,2560]{1,0:T(2,128)(2,1)} %param.6, bf16[2,2560]{1,0:T(2,128)(2,1)} %param.5), kind=kLoop, calls=%fused_computation.69 | loop fusion | flops 40960 | bytes 40960 | tf_op jit(solution)/shard_map/stack | solution.py:25
  1.6 0.7 %broadcast_in_dim.2 = bf16[4,8,4,640]{3,2,1,0:T(4,128)(2,1)} broadcast(bf16[4,4,640]{2,1,0:T(4,128)(2,1)S(1)} %pad_maximum_fusion.4), dimensions={0,2,3} | broadcast | bytes 184320 | tf_op jit(solution)/shard_map/broadcast_in_dim | solution.py:26
  2.4 7.3 %all-to-all-start = ((bf16[32,4,640]{2,1,0:T(4,128)(2,1)}), bf16[32,4,640]{2,1,0:T(4,128)(2,1)S(1)}, u32[]{:S(2)}, u32[]{:S(2)}) async-start(bf16[32,4,640]{2,1,0:T(4,128)(2,1)} %bitcast.4), calls=%async_computation | async-start | bytes 327680 | tf_op jit(solution)/shard_map/all_to_all | solution.py:27
  9.7 7.9 %all-to-all-done = bf16[32,4,640]{2,1,0:T(4,128)(2,1)S(1)} async-done(((bf16[32,4,640]{2,1,0:T(4,128)(2,1)}), bf16[32,4,640]{2,1,0:T(4,128)(2,1)S(1)}, u32[]{:S(2)}, u32[]{:S(2)}) %all-to-all-start) | async-done | bytes 163872 | tf_op jit(solution)/shard_map/all_to_all | solution.py:27
  17.9 0.7 %fusion.34 = f32[64,1600]{1,0:T(8,128)S(1)} fusion(bf16[64,640]{1,0:T(8,128)(2,1)S(1)} %bitcast.47, bf16[1600,640]{1,0:T(8,128)(2,1)S(1)} %copy-done), kind=kOutput, calls=%fused_computation.78 | convolution fusion | flops 131072000 | bytes 2539520 | tf_op jit(solution)/shard_map/td,fd->tf/dot_general | solution.py:51
  18.9 0.5 %copy-done.1 = bf16[640,1600]{0,1:T(8,128)(2,1)S(1)} copy-done((bf16[640,1600]{0,1:T(8,128)(2,1)S(1)}, bf16[640,1600]{0,1:T(8,128)(2,1)}, u32[]{:S(2)}) %copy-start.1) | copy-done | bytes 2048024
  19.4 0.7 %fusion.35 = f32[64,1600]{1,0:T(8,128)S(1)} fusion(bf16[64,640]{1,0:T(8,128)(2,1)S(1)} %bitcast.43, bf16[640,1600]{0,1:T(8,128)(2,1)S(1)} %copy-done.1), kind=kOutput, calls=%fused_computation.79 | convolution fusion | flops 131072000 | bytes 2539520 | tf_op jit(solution)/shard_map/td,fd->tf/dot_general | solution.py:53
  20.4 1.4 %collective-permute-start.1 = (bf16[32,1600]{1,0:T(8,128)(2,1)S(1)}, bf16[32,1600]{1,0:T(8,128)(2,1)S(1)}, u32[]{:S(2)}, u32[]{:S(2)}) collective-permute-start(bf16[32,1600]{1,0:T(8,128)(2,1)S(1)} %add_convert_fusion), channel_id=1, source_target_pairs={{0,16},{8,24},{16,0},{24,8},{1,17},{9,25},{17,1},{25,9},{2,18},{10... | collective-permute-start | bytes 307208 | tf_op jit(solution)/shard_map/ppermute | solution.py:47
  21.8 0.7 %fusion.36 = f32[64,1600]{1,0:T(8,128)S(1)} fusion(bf16[64,640]{1,0:T(8,128)(2,1)S(1)} %bitcast.44, bf16[640,1600]{0,1:T(8,128)(2,1)S(1)} %copy-done.2), kind=kOutput, calls=%fused_computation.80 | convolution fusion | flops 131072000 | bytes 2539520 | tf_op jit(solution)/shard_map/td,fd->tf/dot_general | solution.py:56
  22.7 0.8 %collective-permute-start.3 = (bf16[32,1600]{1,0:T(8,128)(2,1)S(1)}, bf16[32,1600]{1,0:T(8,128)(2,1)S(1)}, u32[]{:S(2)}, u32[]{:S(2)}) collective-permute-start(bf16[32,1600]{1,0:T(8,128)(2,1)S(1)} %fusion.7), channel_id=1, source_target_pairs={{0,16},{8,24},{16,0},{24,8},{1,17},{9,25},{17,1},{25,9},{2,18},{10... | collective-permute-start | bytes 307208 | tf_op jit(solution)/shard_map/ppermute | solution.py:47
  23.5 0.4 collective-permute-done.4
  24.0 0.9 %collective-permute-start.5 = (bf16[32,768]{1,0:T(8,128)(2,1)S(1)}, bf16[32,768]{1,0:T(8,128)(2,1)S(1)}, u32[]{:S(2)}, u32[]{:S(2)}) collective-permute-start(bf16[32,768]{1,0:T(8,128)(2,1)S(1)} %slice.106), channel_id=1, source_target_pairs={{0,16},{8,24},{16,0},{24,8},{1,17},{9,25},{17,1},{25,9},{2,18},{10... | collective-permute-start | bytes 147464 | tf_op jit(solution)/shard_map/ppermute | solution.py:47
  24.9 1.2 %collective-permute-start.7 = (bf16[32,832]{1,0:T(8,128)(2,1)S(1)}, bf16[32,832]{1,0:T(8,128)(2,1)S(1)}, u32[]{:S(2)}, u32[]{:S(2)}) collective-permute-start(bf16[32,832]{1,0:T(8,128)(2,1)S(1)} %slice.111), channel_id=1, source_target_pairs={{0,16},{8,24},{16,0},{24,8},{1,17},{9,25},{17,1},{25,9},{2,18},{10... | collective-permute-start | bytes 159752 | tf_op jit(solution)/shard_map/ppermute | solution.py:47
  26.1 2.4 %collective-permute-done.3 = bf16[32,1600]{1,0:T(8,128)(2,1)S(1)} collective-permute-done((bf16[32,1600]{1,0:T(8,128)(2,1)S(1)}, bf16[32,1600]{1,0:T(8,128)(2,1)S(1)}, u32[]{:S(2)}, u32[]{:S(2)}) %collective-permute-start.3) | collective-permute-done | bytes 102432 | tf_op jit(solution)/shard_map/ppermute | solution.py:47
  28.5 1.0 %collective-permute-done.5 = bf16[32,768]{1,0:T(8,128)(2,1)S(1)} collective-permute-done((bf16[32,768]{1,0:T(8,128)(2,1)S(1)}, bf16[32,768]{1,0:T(8,128)(2,1)S(1)}, u32[]{:S(2)}, u32[]{:S(2)}) %collective-permute-start.5) | collective-permute-done | bytes 49184 | tf_op jit(solution)/shard_map/ppermute | solution.py:47
  29.7 0.7 %collective-permute-done.7 = bf16[32,832]{1,0:T(8,128)(2,1)S(1)} collective-permute-done((bf16[32,832]{1,0:T(8,128)(2,1)S(1)}, bf16[32,832]{1,0:T(8,128)(2,1)S(1)}, u32[]{:S(2)}, u32[]{:S(2)}) %collective-permute-start.7) | collective-permute-done | bytes 53280 | tf_op jit(solution)/shard_map/ppermute | solution.py:47
  30.7 0.4 collective-permute-done.6
  32.8 0.7 %reshape.44 = bf16[32,2,640]{2,1,0:T(2,128)(2,1)} reshape(bf16[2,2,16,640]{3,2,1,0:T(8,128)(2,1)S(1)} %reverse_select_fusion) | data formatting | bytes 163840 | tf_op jit(solution)/shard_map/reshape | solution.py:86
  33.5 2.9 %all-to-all-start.1 = ((bf16[32,2,640]{2,1,0:T(2,128)(2,1)}), bf16[32,2,640]{2,1,0:T(2,128)(2,1)S(1)}, u32[]{:S(2)}, u32[]{:S(2)}) async-start(bf16[32,2,640]{2,1,0:T(2,128)(2,1)} %reshape.44), calls=%async_computation.1 | async-start | bytes 163840 | tf_op jit(solution)/shard_map/all_to_all | solution.py:89
  36.7 2.1 %multiply_convert_fusion.1 = bf16[640,1600]{0,1:T(8,128)(2,1)} fusion(bf16[64,640]{1,0:T(8,128)(2,1)S(1)} %bitcast.45, bf16[64,832]{1,0:T(8,128)(2,1)S(1)} %get-tuple-element.30, bf16[64,768]{1,0:T(8,128)(2,1)S(1)} %get-tuple-element.32), kind=kOutput, calls=%fused_computation.1 | convolution fusion | flops 133529600 | bytes 2334720 | tf_op jit(solution)/shard_map/td,tf->df/dot_general | solution.py:94
  38.8 2.1 %multiply_convert_fusion.2 = bf16[640,1600]{0,1:T(8,128)(2,1)} fusion(bf16[64,640]{1,0:T(8,128)(2,1)S(1)} %bitcast.46, bf16[64,832]{1,0:T(8,128)(2,1)S(1)} %get-tuple-element.31, bf16[64,768]{1,0:T(8,128)(2,1)S(1)} %get-tuple-element.33), kind=kOutput, calls=%fused_computation.2 | convolution fusion | flops 133529600 | bytes 2334720 | tf_op jit(solution)/shard_map/td,tf->df/dot_general | solution.py:93
  40.8 2.0 %multiply_convert_fusion = bf16[1600,640]{1,0:T(8,128)(2,1)} fusion(bf16[64,640]{1,0:T(8,128)(2,1)S(1)} %bitcast.48, bf16[32,1600]{1,0:T(8,128)(2,1)S(1)} %pad_maximum_fusion.2, bf16[32,1600]{1,0:T(8,128)(2,1)S(1)} %collective-permute-done.9), kind=kOutput, calls=%fused_computation | convolution fusion | flops 133529600 | bytes 2334720 | tf_op jit(solution)/shard_map/tf,td->fd/dot_general | solution.py:95
  42.9 1.0 %all-to-all-done.1 = bf16[32,2,640]{2,1,0:T(2,128)(2,1)S(1)} async-done(((bf16[32,2,640]{2,1,0:T(2,128)(2,1)}), bf16[32,2,640]{2,1,0:T(2,128)(2,1)S(1)}, u32[]{:S(2)}, u32[]{:S(2)}) %all-to-all-start.1) | async-done | bytes 81952 | tf_op jit(solution)/shard_map/all_to_all | solution.py:89
  43.8 0.7 %bitcast_reduce_fusion = bf16[4,2,640]{2,1,0:T(2,128)(2,1)} fusion(bf16[32,2,640]{2,1,0:T(2,128)(2,1)S(1)} %all-to-all-done.1), kind=kLoop, calls=%fused_computation.54 | loop fusion | flops 35840 | bytes 92160 | tf_op jit(solution)/shard_map/reduce_sum | solution.py:90
  (48 shorter events, 3.4 us)
Async XLA Ops:
  0.6 17.2 %copy-start = (bf16[1600,640]{1,0:T(8,128)(2,1)S(1)}, bf16[1600,640]{1,0:T(8,128)(2,1)}, u32[]{:S(2)}) copy-start(bf16[1600,640]{1,0:T(8,128)(2,1)} %param.9) | copy-start | bytes 6144004
  2.4 15.2 %all-to-all-start = ((bf16[32,4,640]{2,1,0:T(4,128)(2,1)}), bf16[32,4,640]{2,1,0:T(4,128)(2,1)S(1)}, u32[]{:S(2)}, u32[]{:S(2)}) async-start(bf16[32,4,640]{2,1,0:T(4,128)(2,1)} %bitcast.4), calls=%async_computation | async-start | bytes 327680 | tf_op jit(solution)/shard_map/all_to_all | solution.py:27
  17.8 1.6 %copy-start.1 = (bf16[640,1600]{0,1:T(8,128)(2,1)S(1)}, bf16[640,1600]{0,1:T(8,128)(2,1)}, u32[]{:S(2)}) copy-start(bf16[640,1600]{0,1:T(8,128)(2,1)} %param.8) | copy-start | bytes 6144004
  18.6 3.1 %copy-start.2 = (bf16[640,1600]{0,1:T(8,128)(2,1)S(1)}, bf16[640,1600]{0,1:T(8,128)(2,1)}, u32[]{:S(2)}) copy-start(bf16[640,1600]{0,1:T(8,128)(2,1)} %param.7) | copy-start | bytes 6144004
  18.7 1.7 %collective-permute-start = (bf16[32,1600]{1,0:T(8,128)(2,1)S(1)}, bf16[32,1600]{1,0:T(8,128)(2,1)S(1)}, u32[]{:S(2)}, u32[]{:S(2)}) collective-permute-start(bf16[32,1600]{1,0:T(8,128)(2,1)S(1)} %slice.178), channel_id=1, source_target_pairs={{0,8},{8,0},{16,24},{24,16},{1,9},{9,1},{17,25},{25,17},{2,10},{10... | collective-permute-start | bytes 307208 | tf_op jit(solution)/shard_map/ppermute | solution.py:11
  20.1 2.5 %collective-permute-start.2 = (bf16[32,1600]{1,0:T(8,128)(2,1)S(1)}, bf16[32,1600]{1,0:T(8,128)(2,1)S(1)}, u32[]{:S(2)}, u32[]{:S(2)}) collective-permute-start(bf16[32,1600]{1,0:T(8,128)(2,1)S(1)} %slice.177), channel_id=1, source_target_pairs={{0,8},{8,0},{16,24},{24,16},{1,9},{9,1},{17,25},{25,17},{2,10},{10... | collective-permute-start | bytes 307208 | tf_op jit(solution)/shard_map/ppermute | solution.py:11
  20.4 5.7 %collective-permute-start.1 = (bf16[32,1600]{1,0:T(8,128)(2,1)S(1)}, bf16[32,1600]{1,0:T(8,128)(2,1)S(1)}, u32[]{:S(2)}, u32[]{:S(2)}) collective-permute-start(bf16[32,1600]{1,0:T(8,128)(2,1)S(1)} %add_convert_fusion), channel_id=1, source_target_pairs={{0,16},{8,24},{16,0},{24,8},{1,17},{9,25},{17,1},{25,9},{2,18},{10... | collective-permute-start | bytes 307208 | tf_op jit(solution)/shard_map/ppermute | solution.py:47
  22.5 1.4 %collective-permute-start.4 = (bf16[32,1600]{1,0:T(8,128)(2,1)S(1)}, bf16[32,1600]{1,0:T(8,128)(2,1)S(1)}, u32[]{:S(2)}, u32[]{:S(2)}) collective-permute-start(bf16[32,1600]{1,0:T(8,128)(2,1)S(1)} %slice.176), channel_id=1, source_target_pairs={{0,8},{8,0},{16,24},{24,16},{1,9},{9,1},{17,25},{25,17},{2,10},{10... | collective-permute-start | bytes 307208 | tf_op jit(solution)/shard_map/ppermute | solution.py:11
  22.7 5.8 %collective-permute-start.3 = (bf16[32,1600]{1,0:T(8,128)(2,1)S(1)}, bf16[32,1600]{1,0:T(8,128)(2,1)S(1)}, u32[]{:S(2)}, u32[]{:S(2)}) collective-permute-start(bf16[32,1600]{1,0:T(8,128)(2,1)S(1)} %fusion.7), channel_id=1, source_target_pairs={{0,16},{8,24},{16,0},{24,8},{1,17},{9,25},{17,1},{25,9},{2,18},{10... | collective-permute-start | bytes 307208 | tf_op jit(solution)/shard_map/ppermute | solution.py:47
  24.0 5.6 %collective-permute-start.5 = (bf16[32,768]{1,0:T(8,128)(2,1)S(1)}, bf16[32,768]{1,0:T(8,128)(2,1)S(1)}, u32[]{:S(2)}, u32[]{:S(2)}) collective-permute-start(bf16[32,768]{1,0:T(8,128)(2,1)S(1)} %slice.106), channel_id=1, source_target_pairs={{0,16},{8,24},{16,0},{24,8},{1,17},{9,25},{17,1},{25,9},{2,18},{10... | collective-permute-start | bytes 147464 | tf_op jit(solution)/shard_map/ppermute | solution.py:47
  24.9 5.5 %collective-permute-start.7 = (bf16[32,832]{1,0:T(8,128)(2,1)S(1)}, bf16[32,832]{1,0:T(8,128)(2,1)S(1)}, u32[]{:S(2)}, u32[]{:S(2)}) collective-permute-start(bf16[32,832]{1,0:T(8,128)(2,1)S(1)} %slice.111), channel_id=1, source_target_pairs={{0,16},{8,24},{16,0},{24,8},{1,17},{9,25},{17,1},{25,9},{2,18},{10... | collective-permute-start | bytes 159752 | tf_op jit(solution)/shard_map/ppermute | solution.py:47
  29.6 1.4 %collective-permute-start.6 = (bf16[32,1536]{1,0:T(8,128)(2,1)S(1)}, bf16[32,1536]{1,0:T(8,128)(2,1)S(1)}, u32[]{:S(2)}, u32[]{:S(2)}) collective-permute-start(bf16[32,1536]{1,0:T(8,128)(2,1)S(1)} %pad_maximum_fusion.3), channel_id=1, source_target_pairs={{0,8},{8,0},{16,24},{24,16},{1,9},{9,1},{17,25},{25,17},{2,10},{10... | collective-permute-start | bytes 294920 | tf_op jit(solution)/shard_map/ppermute | solution.py:11
  30.6 1.4 %collective-permute-start.8 = (bf16[32,1664]{1,0:T(8,128)(2,1)S(1)}, bf16[32,1664]{1,0:T(8,128)(2,1)S(1)}, u32[]{:S(2)}, u32[]{:S(2)}) collective-permute-start(bf16[32,1664]{1,0:T(8,128)(2,1)S(1)} %pad_maximum_fusion.1), channel_id=1, source_target_pairs={{0,8},{8,0},{16,24},{24,16},{1,9},{9,1},{17,25},{25,17},{2,10},{10... | collective-permute-start | bytes 319496 | tf_op jit(solution)/shard_map/ppermute | solution.py:11
  33.5 10.4 %all-to-all-start.1 = ((bf16[32,2,640]{2,1,0:T(2,128)(2,1)}), bf16[32,2,640]{2,1,0:T(2,128)(2,1)S(1)}, u32[]{:S(2)}, u32[]{:S(2)}) async-start(bf16[32,2,640]{2,1,0:T(2,128)(2,1)} %reshape.44), calls=%async_computation.1 | async-start | bytes 163840 | tf_op jit(solution)/shard_map/all_to_all | solution.py:89
  36.4 4.4 %collective-permute-start.9 = (bf16[32,1600]{1,0:T(8,128)(2,1)S(1)}, bf16[32,1600]{1,0:T(8,128)(2,1)S(1)}, u32[]{:S(2)}, u32[]{:S(2)}) collective-permute-start(bf16[32,1600]{1,0:T(8,128)(2,1)S(1)} %pad_maximum_fusion.2), channel_id=1, source_target_pairs={{0,8},{8,0},{16,24},{24,16},{1,9},{9,1},{17,25},{25,17},{2,10},{10... | collective-permute-start | bytes 307208 | tf_op jit(solution)/shard_map/ppermute | solution.py:11

commit v6 on v5

--- a/solution.py
+++ b/solution.py
@@ -69,15 +69,14 @@
             (part_hid * part_up * sig * (1.0 + part_gate * (1.0 - sig))).astype(BF16),
             (part_hid * part_gate * sig).astype(BF16),
         ]
-        grads = jnp.concatenate(grads, axis=1)
-        packed.append((swap_cores(grads, n_dp), grads))
+        packed.append(([swap_cores(grad, n_dp) for grad in grads], grads))
         hidden.append((part_gate * sig * part_up).astype(BF16))
     hidden = jnp.concatenate(hidden, axis=1)
     total, parts = None, []
     for span, (other, own) in zip(spans, packed):
         if total is not None:
             total, other = lax.optimization_barrier((total, other))
-        parts.append(jnp.split(jnp.concatenate([other, own], axis=0), 2, axis=1))
+        parts.append([jnp.concatenate(pair, axis=0) for pair in zip(other, own)])
         part = jnp.einsum("tf,fd->td", parts[-1][0], gate_rows[span], preferred_element_type=F32)
         part = part + jnp.einsum("tf,fd->td", parts[-1][1], up_rows[span], preferred_element_type=F32)
         total = part if total is None else total + part

time: 44.8 us -> 44.7 us (level)
  starting transfers between devices: 15.5 us -> 16.5 us
  waiting for transfers between devices: 14 us -> 13.2 us
    ppermute x6 -> x8, starting transfers between devices: 0.96 us -> 1.95 us  [swap_cores(): return lax.ppermute(value, 'dp', [(i, i ^ 1) for i in range(n_dp)])]
    ppermute x4, waiting for transfers between devices: 4.07 us -> 3.6 us  [chip_sum(): lax.ppermute(mine, 'dp', [(i, (i + 2 * shift) % n_dp) for i in range(n_dp)])]
    ppermute x6 -> x8, waiting for transfers between devices: 1.07 us -> 0.71 us  [swap_cores(): return lax.ppermute(value, 'dp', [(i, i ^ 1) for i in range(n_dp)])]
  transfers between devices with their start and end apart: 12 -> 14, of which waited for: 8 -> 8; matrix products, arithmetic and copies ran while one was open for 20% -> 19% of each run, Pallas kernels for 0% -> 0%
where the time goes in v6:
time: 44.7 us; the launch traced here: 44.5 us
  starting transfers between devices  16.5 us (37%)
  waiting for transfers between devices  13.2 us (30%)
  matrix products  9.6 us (21%)
  local copies, waits for them, and re-layouts  2.15 us (5%)
  other arithmetic  2.04 us (5%)
  between operations  0.92 us (2%)
    all_to_all x1, waiting for transfers between devices, local(): lax.all_to_all(slices.reshape(n_dp * n_tensor, 2 * rows, depth), ('dp', '...  7.91 us
    all_to_all x1, starting transfers between devices, local(): lax.all_to_all(slices.reshape(n_dp * n_tensor, 2 * rows, depth), ('dp', '...  7.3 us
    ppermute x4, starting transfers between devices, chip_sum(): lax.ppermute(mine, 'dp', [(i, (i + 2 * shift) % n_dp) for i in range(n_dp)])  4.3 us
    ppermute x4, waiting for transfers between devices, chip_sum(): lax.ppermute(mine, 'dp', [(i, (i + 2 * shift) % n_dp) for i in range(n_dp)])  3.6 us
    all_to_all x1, starting transfers between devices, local(): lax.all_to_all(shares, ('dp', 'tensor'), split_axis=0, concat_axis=0, til...  2.99 us
    dot_general x1, matrix products, local(): jnp.einsum('td,tf->df', tok, up_grad, preferred_element_type=F32) / n_dp  2.05 us
    dot_general x1, matrix products, local(): jnp.einsum('td,tf->df', tok, gate_grad, preferred_element_type=F32) / n_dp  2.05 us
    dot_general x1, matrix products, local(): jnp.einsum('tf,td->fd', hidden, cot, preferred_element_type=F32) / n_dp  2.04 us
  transfers between devices with their start and end apart: 14, of which 8 were waited for; matrix products, arithmetic and copies ran while one was open for 19% of the time, Pallas kernels for 0%

profile of v6, /device:TPU:0, one launch (start us, length us, event | category | flops | bytes accessed | tf_op | source)
XLA Modules:
  0.0 44.5 jit_solution(2500025967831205819)
XLA Ops:
  0.6 1.0 %fusion.44 = (bf16[1,4,640]{2,1,0:T(4,128)(2,1)S(1)}, bf16[1,4,640]{2,1,0:T(4,128)(2,1)S(1)}, bf16[1,4,640]{2,1,0:T(4,128)(2,1)S(1)}, bf16[1,4,640]{2,1,0:T(4,128)(2,1)S(1)}) fusion(bf16[2,2560]{1,0:T(2,128)(2,1)} %param.6, bf16[2,2560]{1,0:T(2,128)(2,1)} %param.5), kind=kLoop, calls=%fused_computation.82 | loop fusion | flops 40960 | bytes 40960 | tf_op jit(solution)/shard_map/stack | solution.py:25
  1.6 0.7 %broadcast_in_dim.2 = bf16[4,8,4,640]{3,2,1,0:T(4,128)(2,1)} broadcast(bf16[4,4,640]{2,1,0:T(4,128)(2,1)S(1)} %pad_maximum_fusion.1), dimensions={0,2,3} | broadcast | bytes 184320 | tf_op jit(solution)/shard_map/broadcast_in_dim | solution.py:26
  2.4 7.3 %all-to-all-start = ((bf16[32,4,640]{2,1,0:T(4,128)(2,1)}), bf16[32,4,640]{2,1,0:T(4,128)(2,1)S(1)}, u32[]{:S(2)}, u32[]{:S(2)}) async-start(bf16[32,4,640]{2,1,0:T(4,128)(2,1)} %bitcast.4), calls=%async_computation | async-start | bytes 327680 | tf_op jit(solution)/shard_map/all_to_all | solution.py:27
  9.7 7.9 %all-to-all-done = bf16[32,4,640]{2,1,0:T(4,128)(2,1)S(1)} async-done(((bf16[32,4,640]{2,1,0:T(4,128)(2,1)}), bf16[32,4,640]{2,1,0:T(4,128)(2,1)S(1)}, u32[]{:S(2)}, u32[]{:S(2)}) %all-to-all-start) | async-done | bytes 163872 | tf_op jit(solution)/shard_map/all_to_all | solution.py:27
  17.9 0.7 %fusion.54 = f32[64,1600]{1,0:T(8,128)S(1)} fusion(bf16[64,640]{1,0:T(8,128)(2,1)S(1)} %bitcast.45, bf16[1600,640]{1,0:T(8,128)(2,1)S(1)} %copy-done), kind=kOutput, calls=%fused_computation.92 | convolution fusion | flops 131072000 | bytes 2539520 | tf_op jit(solution)/shard_map/td,fd->tf/dot_general | solution.py:51
  18.9 0.5 %copy-done.1 = bf16[640,1600]{0,1:T(8,128)(2,1)S(1)} copy-done((bf16[640,1600]{0,1:T(8,128)(2,1)S(1)}, bf16[640,1600]{0,1:T(8,128)(2,1)}, u32[]{:S(2)}) %copy-start.1) | copy-done | bytes 2048024
  19.4 0.7 %fusion.55 = f32[64,1600]{1,0:T(8,128)S(1)} fusion(bf16[64,640]{1,0:T(8,128)(2,1)S(1)} %bitcast.41, bf16[640,1600]{0,1:T(8,128)(2,1)S(1)} %copy-done.1), kind=kOutput, calls=%fused_computation.93 | convolution fusion | flops 131072000 | bytes 2539520 | tf_op jit(solution)/shard_map/td,fd->tf/dot_general | solution.py:53
  20.4 1.4 %collective-permute-start.1 = (bf16[32,1600]{1,0:T(8,128)(2,1)S(1)}, bf16[32,1600]{1,0:T(8,128)(2,1)S(1)}, u32[]{:S(2)}, u32[]{:S(2)}) collective-permute-start(bf16[32,1600]{1,0:T(8,128)(2,1)S(1)} %add_convert_fusion), channel_id=1, source_target_pairs={{0,16},{8,24},{16,0},{24,8},{1,17},{9,25},{17,1},{25,9},{2,18},{10... | collective-permute-start | bytes 307208 | tf_op jit(solution)/shard_map/ppermute | solution.py:47
  21.8 0.7 %fusion.56 = f32[64,1600]{1,0:T(8,128)S(1)} fusion(bf16[64,640]{1,0:T(8,128)(2,1)S(1)} %bitcast.42, bf16[640,1600]{0,1:T(8,128)(2,1)S(1)} %copy-done.2), kind=kOutput, calls=%fused_computation.94 | convolution fusion | flops 131072000 | bytes 2539520 | tf_op jit(solution)/shard_map/td,fd->tf/dot_general | solution.py:56
  22.7 0.8 %collective-permute-start.3 = (bf16[32,1600]{1,0:T(8,128)(2,1)S(1)}, bf16[32,1600]{1,0:T(8,128)(2,1)S(1)}, u32[]{:S(2)}, u32[]{:S(2)}) collective-permute-start(bf16[32,1600]{1,0:T(8,128)(2,1)S(1)} %fusion.7), channel_id=1, source_target_pairs={{0,16},{8,24},{16,0},{24,8},{1,17},{9,25},{17,1},{25,9},{2,18},{10... | collective-permute-start | bytes 307208 | tf_op jit(solution)/shard_map/ppermute | solution.py:47
  23.5 0.4 collective-permute-done.4
  24.0 0.9 %collective-permute-start.5 = (bf16[32,768]{1,0:T(8,128)(2,1)S(1)}, bf16[32,768]{1,0:T(8,128)(2,1)S(1)}, u32[]{:S(2)}, u32[]{:S(2)}) collective-permute-start(bf16[32,768]{1,0:T(8,128)(2,1)S(1)} %slice.106), channel_id=1, source_target_pairs={{0,16},{8,24},{16,0},{24,8},{1,17},{9,25},{17,1},{25,9},{2,18},{10... | collective-permute-start | bytes 147464 | tf_op jit(solution)/shard_map/ppermute | solution.py:47
  24.9 1.2 %collective-permute-start.8 = (bf16[32,832]{1,0:T(8,128)(2,1)S(1)}, bf16[32,832]{1,0:T(8,128)(2,1)S(1)}, u32[]{:S(2)}, u32[]{:S(2)}) collective-permute-start(bf16[32,832]{1,0:T(8,128)(2,1)S(1)} %slice.111), channel_id=1, source_target_pairs={{0,16},{8,24},{16,0},{24,8},{1,17},{9,25},{17,1},{25,9},{2,18},{10... | collective-permute-start | bytes 159752 | tf_op jit(solution)/shard_map/ppermute | solution.py:47
  26.1 2.4 %collective-permute-done.3 = bf16[32,1600]{1,0:T(8,128)(2,1)S(1)} collective-permute-done((bf16[32,1600]{1,0:T(8,128)(2,1)S(1)}, bf16[32,1600]{1,0:T(8,128)(2,1)S(1)}, u32[]{:S(2)}, u32[]{:S(2)}) %collective-permute-start.3) | collective-permute-done | bytes 102432 | tf_op jit(solution)/shard_map/ppermute | solution.py:47
  28.5 1.0 %collective-permute-done.5 = bf16[32,768]{1,0:T(8,128)(2,1)S(1)} collective-permute-done((bf16[32,768]{1,0:T(8,128)(2,1)S(1)}, bf16[32,768]{1,0:T(8,128)(2,1)S(1)}, u32[]{:S(2)}, u32[]{:S(2)}) %collective-permute-start.5) | collective-permute-done | bytes 49184 | tf_op jit(solution)/shard_map/ppermute | solution.py:47
  29.7 0.5 %collective-permute-start.7 = (bf16[32,768]{1,0:T(8,128)(2,1)S(1)}, bf16[32,768]{1,0:T(8,128)(2,1)S(1)}, u32[]{:S(2)}, u32[]{:S(2)}) collective-permute-start(bf16[32,768]{1,0:T(8,128)(2,1)S(1)} %get-tuple-element.31), channel_id=1, source_target_pairs={{0,8},{8,0},{16,24},{24,16},{1,9},{9,1},{17,25},{25,17},{2,10},{10... | collective-permute-start | bytes 147464 | tf_op jit(solution)/shard_map/ppermute | solution.py:11
  30.6 0.5 %collective-permute-start.10 = (bf16[32,832]{1,0:T(8,128)(2,1)S(1)}, bf16[32,832]{1,0:T(8,128)(2,1)S(1)}, u32[]{:S(2)}, u32[]{:S(2)}) collective-permute-start(bf16[32,832]{1,0:T(8,128)(2,1)S(1)} %get-tuple-element.28), channel_id=1, source_target_pairs={{0,8},{8,0},{16,24},{24,16},{1,9},{9,1},{17,25},{25,17},{2,10},{10... | collective-permute-start | bytes 159752 | tf_op jit(solution)/shard_map/ppermute | solution.py:11
  32.7 0.7 %reshape.44 = bf16[32,2,640]{2,1,0:T(2,128)(2,1)} reshape(bf16[2,2,16,640]{3,2,1,0:T(8,128)(2,1)S(1)} %reverse_select_fusion) | data formatting | bytes 163840 | tf_op jit(solution)/shard_map/reshape | solution.py:85
  33.3 3.0 %all-to-all-start.1 = ((bf16[32,2,640]{2,1,0:T(2,128)(2,1)}), bf16[32,2,640]{2,1,0:T(2,128)(2,1)S(1)}, u32[]{:S(2)}, u32[]{:S(2)}) async-start(bf16[32,2,640]{2,1,0:T(2,128)(2,1)} %reshape.44), calls=%async_computation.1 | async-start | bytes 163840 | tf_op jit(solution)/shard_map/all_to_all | solution.py:88
  36.7 2.1 %multiply_convert_fusion.1 = bf16[640,1600]{0,1:T(8,128)(2,1)} fusion(bf16[64,640]{1,0:T(8,128)(2,1)S(1)} %bitcast.43, bf16[32,832]{1,0:T(8,128)(2,1)S(1)} %get-tuple-element.28, bf16[32,832]{1,0:T(8,128)(2,1)S(1)} %collective-permute-done.10, bf16[32,768]{1,0:T(8,128)(2,1)S(1)} %get-tuple-element.31, bf16[32,768]{1,0:T(8,128)(2,1)S(1)} %collective-permute-done.7), kind=kOutput, calls=%fused_computation.1 | convolution fusion | flops 133939200 | bytes 2334720 | tf_op jit(solution)/shard_map/td,tf->df/dot_general | solution.py:93
  38.7 2.1 %multiply_convert_fusion.2 = bf16[640,1600]{0,1:T(8,128)(2,1)} fusion(bf16[64,640]{1,0:T(8,128)(2,1)S(1)} %bitcast.44, bf16[32,832]{1,0:T(8,128)(2,1)S(1)} %get-tuple-element.27, bf16[32,832]{1,0:T(8,128)(2,1)S(1)} %collective-permute-done.9, bf16[32,768]{1,0:T(8,128)(2,1)S(1)} %get-tuple-element.30, bf16[32,768]{1,0:T(8,128)(2,1)S(1)} %collective-permute-done.6), kind=kOutput, calls=%fused_computation.2 | convolution fusion | flops 133939200 | bytes 2334720 | tf_op jit(solution)/shard_map/td,tf->df/dot_general | solution.py:92
  40.8 2.0 %multiply_convert_fusion = bf16[1600,640]{1,0:T(8,128)(2,1)} fusion(bf16[64,640]{1,0:T(8,128)(2,1)S(1)} %bitcast.46, bf16[32,1600]{1,0:T(8,128)(2,1)S(1)} %pad_maximum_fusion, bf16[32,1600]{1,0:T(8,128)(2,1)S(1)} %collective-permute-done.11), kind=kOutput, calls=%fused_computation | convolution fusion | flops 133529600 | bytes 2334720 | tf_op jit(solution)/shard_map/tf,td->fd/dot_general | solution.py:94
  42.8 1.0 %all-to-all-done.1 = bf16[32,2,640]{2,1,0:T(2,128)(2,1)S(1)} async-done(((bf16[32,2,640]{2,1,0:T(2,128)(2,1)}), bf16[32,2,640]{2,1,0:T(2,128)(2,1)S(1)}, u32[]{:S(2)}, u32[]{:S(2)}) %all-to-all-start.1) | async-done | bytes 81952 | tf_op jit(solution)/shard_map/all_to_all | solution.py:88
  43.8 0.7 %bitcast_reduce_fusion = bf16[4,2,640]{2,1,0:T(2,128)(2,1)} fusion(bf16[32,2,640]{2,1,0:T(2,128)(2,1)S(1)} %all-to-all-done.1), kind=kLoop, calls=%fused_computation.67 | loop fusion | flops 35840 | bytes 92160 | tf_op jit(solution)/shard_map/reduce_sum | solution.py:89
  (47 shorter events, 3.3 us)
Async XLA Ops:
  0.6 17.2 %copy-start = (bf16[1600,640]{1,0:T(8,128)(2,1)S(1)}, bf16[1600,640]{1,0:T(8,128)(2,1)}, u32[]{:S(2)}) copy-start(bf16[1600,640]{1,0:T(8,128)(2,1)} %param.9) | copy-start | bytes 6144004
  2.4 15.2 %all-to-all-start = ((bf16[32,4,640]{2,1,0:T(4,128)(2,1)}), bf16[32,4,640]{2,1,0:T(4,128)(2,1)S(1)}, u32[]{:S(2)}, u32[]{:S(2)}) async-start(bf16[32,4,640]{2,1,0:T(4,128)(2,1)} %bitcast.4), calls=%async_computation | async-start | bytes 327680 | tf_op jit(solution)/shard_map/all_to_all | solution.py:27
  17.8 1.6 %copy-start.1 = (bf16[640,1600]{0,1:T(8,128)(2,1)S(1)}, bf16[640,1600]{0,1:T(8,128)(2,1)}, u32[]{:S(2)}) copy-start(bf16[640,1600]{0,1:T(8,128)(2,1)} %param.8) | copy-start | bytes 6144004
  18.6 3.1 %copy-start.2 = (bf16[640,1600]{0,1:T(8,128)(2,1)S(1)}, bf16[640,1600]{0,1:T(8,128)(2,1)}, u32[]{:S(2)}) copy-start(bf16[640,1600]{0,1:T(8,128)(2,1)} %param.7) | copy-start | bytes 6144004
  18.7 1.7 %collective-permute-start = (bf16[32,1600]{1,0:T(8,128)(2,1)S(1)}, bf16[32,1600]{1,0:T(8,128)(2,1)S(1)}, u32[]{:S(2)}, u32[]{:S(2)}) collective-permute-start(bf16[32,1600]{1,0:T(8,128)(2,1)S(1)} %slice.178), channel_id=1, source_target_pairs={{0,8},{8,0},{16,24},{24,16},{1,9},{9,1},{17,25},{25,17},{2,10},{10... | collective-permute-start | bytes 307208 | tf_op jit(solution)/shard_map/ppermute | solution.py:11
  20.1 2.5 %collective-permute-start.2 = (bf16[32,1600]{1,0:T(8,128)(2,1)S(1)}, bf16[32,1600]{1,0:T(8,128)(2,1)S(1)}, u32[]{:S(2)}, u32[]{:S(2)}) collective-permute-start(bf16[32,1600]{1,0:T(8,128)(2,1)S(1)} %slice.177), channel_id=1, source_target_pairs={{0,8},{8,0},{16,24},{24,16},{1,9},{9,1},{17,25},{25,17},{2,10},{10... | collective-permute-start | bytes 307208 | tf_op jit(solution)/shard_map/ppermute | solution.py:11
  20.4 5.7 %collective-permute-start.1 = (bf16[32,1600]{1,0:T(8,128)(2,1)S(1)}, bf16[32,1600]{1,0:T(8,128)(2,1)S(1)}, u32[]{:S(2)}, u32[]{:S(2)}) collective-permute-start(bf16[32,1600]{1,0:T(8,128)(2,1)S(1)} %add_convert_fusion), channel_id=1, source_target_pairs={{0,16},{8,24},{16,0},{24,8},{1,17},{9,25},{17,1},{25,9},{2,18},{10... | collective-permute-start | bytes 307208 | tf_op jit(solution)/shard_map/ppermute | solution.py:47
  22.5 1.4 %collective-permute-start.4 = (bf16[32,1600]{1,0:T(8,128)(2,1)S(1)}, bf16[32,1600]{1,0:T(8,128)(2,1)S(1)}, u32[]{:S(2)}, u32[]{:S(2)}) collective-permute-start(bf16[32,1600]{1,0:T(8,128)(2,1)S(1)} %slice.176), channel_id=1, source_target_pairs={{0,8},{8,0},{16,24},{24,16},{1,9},{9,1},{17,25},{25,17},{2,10},{10... | collective-permute-start | bytes 307208 | tf_op jit(solution)/shard_map/ppermute | solution.py:11
  22.7 5.8 %collective-permute-start.3 = (bf16[32,1600]{1,0:T(8,128)(2,1)S(1)}, bf16[32,1600]{1,0:T(8,128)(2,1)S(1)}, u32[]{:S(2)}, u32[]{:S(2)}) collective-permute-start(bf16[32,1600]{1,0:T(8,128)(2,1)S(1)} %fusion.7), channel_id=1, source_target_pairs={{0,16},{8,24},{16,0},{24,8},{1,17},{9,25},{17,1},{25,9},{2,18},{10... | collective-permute-start | bytes 307208 | tf_op jit(solution)/shard_map/ppermute | solution.py:47
  24.0 5.6 %collective-permute-start.5 = (bf16[32,768]{1,0:T(8,128)(2,1)S(1)}, bf16[32,768]{1,0:T(8,128)(2,1)S(1)}, u32[]{:S(2)}, u32[]{:S(2)}) collective-permute-start(bf16[32,768]{1,0:T(8,128)(2,1)S(1)} %slice.106), channel_id=1, source_target_pairs={{0,16},{8,24},{16,0},{24,8},{1,17},{9,25},{17,1},{25,9},{2,18},{10... | collective-permute-start | bytes 147464 | tf_op jit(solution)/shard_map/ppermute | solution.py:47
  24.9 5.5 %collective-permute-start.8 = (bf16[32,832]{1,0:T(8,128)(2,1)S(1)}, bf16[32,832]{1,0:T(8,128)(2,1)S(1)}, u32[]{:S(2)}, u32[]{:S(2)}) collective-permute-start(bf16[32,832]{1,0:T(8,128)(2,1)S(1)} %slice.111), channel_id=1, source_target_pairs={{0,16},{8,24},{16,0},{24,8},{1,17},{9,25},{17,1},{25,9},{2,18},{10... | collective-permute-start | bytes 159752 | tf_op jit(solution)/shard_map/ppermute | solution.py:47
  29.6 1.8 %collective-permute-start.6 = (bf16[32,768]{1,0:T(8,128)(2,1)S(1)}, bf16[32,768]{1,0:T(8,128)(2,1)S(1)}, u32[]{:S(2)}, u32[]{:S(2)}) collective-permute-start(bf16[32,768]{1,0:T(8,128)(2,1)S(1)} %get-tuple-element.30), channel_id=1, source_target_pairs={{0,8},{8,0},{16,24},{24,16},{1,9},{9,1},{17,25},{25,17},{2,10},{10... | collective-permute-start | bytes 147464 | tf_op jit(solution)/shard_map/ppermute | solution.py:11
  29.7 1.4 %collective-permute-start.7 = (bf16[32,768]{1,0:T(8,128)(2,1)S(1)}, bf16[32,768]{1,0:T(8,128)(2,1)S(1)}, u32[]{:S(2)}, u32[]{:S(2)}) collective-permute-start(bf16[32,768]{1,0:T(8,128)(2,1)S(1)} %get-tuple-element.31), channel_id=1, source_target_pairs={{0,8},{8,0},{16,24},{24,16},{1,9},{9,1},{17,25},{25,17},{2,10},{10... | collective-permute-start | bytes 147464 | tf_op jit(solution)/shard_map/ppermute | solution.py:11
  30.5 1.3 %collective-permute-start.9 = (bf16[32,832]{1,0:T(8,128)(2,1)S(1)}, bf16[32,832]{1,0:T(8,128)(2,1)S(1)}, u32[]{:S(2)}, u32[]{:S(2)}) collective-permute-start(bf16[32,832]{1,0:T(8,128)(2,1)S(1)} %get-tuple-element.27), channel_id=1, source_target_pairs={{0,8},{8,0},{16,24},{24,16},{1,9},{9,1},{17,25},{25,17},{2,10},{10... | collective-permute-start | bytes 159752 | tf_op jit(solution)/shard_map/ppermute | solution.py:11
  30.6 1.4 %collective-permute-start.10 = (bf16[32,832]{1,0:T(8,128)(2,1)S(1)}, bf16[32,832]{1,0:T(8,128)(2,1)S(1)}, u32[]{:S(2)}, u32[]{:S(2)}) collective-permute-start(bf16[32,832]{1,0:T(8,128)(2,1)S(1)} %get-tuple-element.28), channel_id=1, source_target_pairs={{0,8},{8,0},{16,24},{24,16},{1,9},{9,1},{17,25},{25,17},{2,10},{10... | collective-permute-start | bytes 159752 | tf_op jit(solution)/shard_map/ppermute | solution.py:11
  33.3 10.4 %all-to-all-start.1 = ((bf16[32,2,640]{2,1,0:T(2,128)(2,1)}), bf16[32,2,640]{2,1,0:T(2,128)(2,1)S(1)}, u32[]{:S(2)}, u32[]{:S(2)}) async-start(bf16[32,2,640]{2,1,0:T(2,128)(2,1)} %reshape.44), calls=%async_computation.1 | async-start | bytes 163840 | tf_op jit(solution)/shard_map/all_to_all | solution.py:88
  36.3 4.4 %collective-permute-start.11 = (bf16[32,1600]{1,0:T(8,128)(2,1)S(1)}, bf16[32,1600]{1,0:T(8,128)(2,1)S(1)}, u32[]{:S(2)}, u32[]{:S(2)}) collective-permute-start(bf16[32,1600]{1,0:T(8,128)(2,1)S(1)} %pad_maximum_fusion), channel_id=1, source_target_pairs={{0,8},{8,0},{16,24},{24,16},{1,9},{9,1},{17,25},{25,17},{2,10},{10... | collective-permute-start | bytes 307208 | tf_op jit(solution)/shard_map/ppermute | solution.py:11

commit v7 on v6

--- a/solution.py
+++ b/solution.py
@@ -69,7 +69,12 @@
             (part_hid * part_up * sig * (1.0 + part_gate * (1.0 - sig))).astype(BF16),
             (part_hid * part_gate * sig).astype(BF16),
         ]
-        packed.append(([swap_cores(grad, n_dp) for grad in grads], grads))
+        if span.start:
+            other = swap_cores(jnp.concatenate(grads, axis=0), n_dp)
+            other = [other[:half], other[half:]]
+        else:
+            other = [swap_cores(grad, n_dp) for grad in grads]
+        packed.append((other, grads))
         hidden.append((part_gate * sig * part_up).astype(BF16))
     hidden = jnp.concatenate(hidden, axis=1)
     total, parts = None, []
@@ -77,9 +82,9 @@
         if total is not None:
             total, other = lax.optimization_barrier((total, other))
         parts.append([jnp.concatenate(pair, axis=0) for pair in zip(other, own)])
-        part = jnp.einsum("tf,fd->td", parts[-1][0], gate_rows[span], preferred_element_type=F32)
-        part = part + jnp.einsum("tf,fd->td", parts[-1][1], up_rows[span], preferred_element_type=F32)
-        total = part if total is None else total + part
+        for grad, weight in zip(parts[-1], (gate_rows, up_rows)):
+            part = jnp.einsum("tf,fd->td", grad, weight[span], preferred_element_type=F32)
+            total = part if total is None else total + part
     gate_grad, up_grad = (jnp.concatenate(values, axis=1) for values in zip(*parts))
     shares = total.astype(BF16).reshape(2, chips, group, depth).transpose(1, 0, 2, 3)
     shares = jnp.where(core == 0, shares[:, ::-1], shares).reshape(n_dp * n_tensor, rows, depth)

time: 44.7 us -> 44.6 us (level)
    ppermute x8 -> x7, starting transfers between devices: 1.95 us -> 1.46 us  [swap_cores(): return lax.ppermute(value, 'dp', [(i, i ^ 1) for i in range(n_dp)])]
    ppermute x8 -> x7, waiting for transfers between devices: 0.71 us -> 1.12 us  [swap_cores(): return lax.ppermute(value, 'dp', [(i, i ^ 1) for i in range(n_dp)])]
  transfers between devices with their start and end apart: 14 -> 13, of which waited for: 8 -> 8; matrix products, arithmetic and copies ran while one was open for 19% -> 19% of each run, Pallas kernels for 0% -> 0%
where the time goes in v7:
time: 44.6 us; the launch traced here: 44.4 us
  starting transfers between devices  16.1 us (36%)
  waiting for transfers between devices  13.6 us (30%)
  matrix products  9.62 us (22%)
  local copies, waits for them, and re-layouts  2.16 us (5%)
  other arithmetic  2.03 us (5%)
  between operations  0.93 us (2%)
    all_to_all x1, waiting for transfers between devices, local(): lax.all_to_all(slices.reshape(n_dp * n_tensor, 2 * rows, depth), ('dp', '...  7.91 us
    all_to_all x1, starting transfers between devices, local(): lax.all_to_all(slices.reshape(n_dp * n_tensor, 2 * rows, depth), ('dp', '...  7.3 us
    ppermute x4, starting transfers between devices, chip_sum(): lax.ppermute(mine, 'dp', [(i, (i + 2 * shift) % n_dp) for i in range(n_dp)])  4.3 us
    ppermute x4, waiting for transfers between devices, chip_sum(): lax.ppermute(mine, 'dp', [(i, (i + 2 * shift) % n_dp) for i in range(n_dp)])  3.6 us
    all_to_all x1, starting transfers between devices, local(): lax.all_to_all(shares, ('dp', 'tensor'), split_axis=0, concat_axis=0, til...  3 us
    dot_general x1, matrix products, local(): jnp.einsum('td,tf->df', tok, up_grad, preferred_element_type=F32) / n_dp  2.05 us
    dot_general x1, matrix products, local(): jnp.einsum('td,tf->df', tok, gate_grad, preferred_element_type=F32) / n_dp  2.05 us
    dot_general x1, matrix products, local(): jnp.einsum('tf,td->fd', hidden, cot, preferred_element_type=F32) / n_dp  2.04 us
  transfers between devices with their start and end apart: 13, of which 8 were waited for; matrix products, arithmetic and copies ran while one was open for 19% of the time, Pallas kernels for 0%

profile of v7, /device:TPU:0, one launch (start us, length us, event | category | flops | bytes accessed | tf_op | source)
XLA Modules:
  0.0 44.4 jit_solution(13826218974295340985)
XLA Ops:
  0.6 1.0 %fusion.45 = (bf16[1,4,640]{2,1,0:T(4,128)(2,1)S(1)}, bf16[1,4,640]{2,1,0:T(4,128)(2,1)S(1)}, bf16[1,4,640]{2,1,0:T(4,128)(2,1)S(1)}, bf16[1,4,640]{2,1,0:T(4,128)(2,1)S(1)}) fusion(bf16[2,2560]{1,0:T(2,128)(2,1)} %param.6, bf16[2,2560]{1,0:T(2,128)(2,1)} %param.5), kind=kLoop, calls=%fused_computation.82 | loop fusion | flops 40960 | bytes 40960 | tf_op jit(solution)/shard_map/stack | solution.py:25
  1.6 0.7 %broadcast_in_dim.2 = bf16[4,8,4,640]{3,2,1,0:T(4,128)(2,1)} broadcast(bf16[4,4,640]{2,1,0:T(4,128)(2,1)S(1)} %pad_maximum_fusion.6), dimensions={0,2,3} | broadcast | bytes 184320 | tf_op jit(solution)/shard_map/broadcast_in_dim | solution.py:26
  2.4 7.3 %all-to-all-start = ((bf16[32,4,640]{2,1,0:T(4,128)(2,1)}), bf16[32,4,640]{2,1,0:T(4,128)(2,1)S(1)}, u32[]{:S(2)}, u32[]{:S(2)}) async-start(bf16[32,4,640]{2,1,0:T(4,128)(2,1)} %bitcast.4), calls=%async_computation | async-start | bytes 327680 | tf_op jit(solution)/shard_map/all_to_all | solution.py:27
  9.7 7.9 %all-to-all-done = bf16[32,4,640]{2,1,0:T(4,128)(2,1)S(1)} async-done(((bf16[32,4,640]{2,1,0:T(4,128)(2,1)}), bf16[32,4,640]{2,1,0:T(4,128)(2,1)S(1)}, u32[]{:S(2)}, u32[]{:S(2)}) %all-to-all-start) | async-done | bytes 163872 | tf_op jit(solution)/shard_map/all_to_all | solution.py:27
  17.9 0.8 %fusion.56 = f32[64,1600]{1,0:T(8,128)S(1)} fusion(bf16[64,640]{1,0:T(8,128)(2,1)S(1)} %bitcast.45, bf16[1600,640]{1,0:T(8,128)(2,1)S(1)} %copy-done), kind=kOutput, calls=%fused_computation.93 | convolution fusion | flops 131072000 | bytes 2539520 | tf_op jit(solution)/shard_map/td,fd->tf/dot_general | solution.py:51
  18.9 0.5 %copy-done.1 = bf16[640,1600]{0,1:T(8,128)(2,1)S(1)} copy-done((bf16[640,1600]{0,1:T(8,128)(2,1)S(1)}, bf16[640,1600]{0,1:T(8,128)(2,1)}, u32[]{:S(2)}) %copy-start.1) | copy-done | bytes 2048024
  19.4 0.7 %fusion.57 = f32[64,1600]{1,0:T(8,128)S(1)} fusion(bf16[64,640]{1,0:T(8,128)(2,1)S(1)} %bitcast.41, bf16[640,1600]{0,1:T(8,128)(2,1)S(1)} %copy-done.1), kind=kOutput, calls=%fused_computation.94 | convolution fusion | flops 131072000 | bytes 2539520 | tf_op jit(solution)/shard_map/td,fd->tf/dot_general | solution.py:53
  20.4 1.4 %collective-permute-start.1 = (bf16[32,1600]{1,0:T(8,128)(2,1)S(1)}, bf16[32,1600]{1,0:T(8,128)(2,1)S(1)}, u32[]{:S(2)}, u32[]{:S(2)}) collective-permute-start(bf16[32,1600]{1,0:T(8,128)(2,1)S(1)} %add_convert_fusion), channel_id=1, source_target_pairs={{0,16},{8,24},{16,0},{24,8},{1,17},{9,25},{17,1},{25,9},{2,18},{10... | collective-permute-start | bytes 307208 | tf_op jit(solution)/shard_map/ppermute | solution.py:47
  21.8 0.7 %fusion.58 = f32[64,1600]{1,0:T(8,128)S(1)} fusion(bf16[64,640]{1,0:T(8,128)(2,1)S(1)} %bitcast.42, bf16[640,1600]{0,1:T(8,128)(2,1)S(1)} %copy-done.2), kind=kOutput, calls=%fused_computation.95 | convolution fusion | flops 131072000 | bytes 2539520 | tf_op jit(solution)/shard_map/td,fd->tf/dot_general | solution.py:56
  22.7 0.8 %collective-permute-start.3 = (bf16[32,1600]{1,0:T(8,128)(2,1)S(1)}, bf16[32,1600]{1,0:T(8,128)(2,1)S(1)}, u32[]{:S(2)}, u32[]{:S(2)}) collective-permute-start(bf16[32,1600]{1,0:T(8,128)(2,1)S(1)} %fusion.8), channel_id=1, source_target_pairs={{0,16},{8,24},{16,0},{24,8},{1,17},{9,25},{17,1},{25,9},{2,18},{10... | collective-permute-start | bytes 307208 | tf_op jit(solution)/shard_map/ppermute | solution.py:47
  23.5 0.4 collective-permute-done.4
  24.0 0.9 %collective-permute-start.5 = (bf16[32,768]{1,0:T(8,128)(2,1)S(1)}, bf16[32,768]{1,0:T(8,128)(2,1)S(1)}, u32[]{:S(2)}, u32[]{:S(2)}) collective-permute-start(bf16[32,768]{1,0:T(8,128)(2,1)S(1)} %slice.114), channel_id=1, source_target_pairs={{0,16},{8,24},{16,0},{24,8},{1,17},{9,25},{17,1},{25,9},{2,18},{10... | collective-permute-start | bytes 147464 | tf_op jit(solution)/shard_map/ppermute | solution.py:47
  24.9 1.2 %collective-permute-start.8 = (bf16[32,832]{1,0:T(8,128)(2,1)S(1)}, bf16[32,832]{1,0:T(8,128)(2,1)S(1)}, u32[]{:S(2)}, u32[]{:S(2)}) collective-permute-start(bf16[32,832]{1,0:T(8,128)(2,1)S(1)} %slice.119), channel_id=1, source_target_pairs={{0,16},{8,24},{16,0},{24,8},{1,17},{9,25},{17,1},{25,9},{2,18},{10... | collective-permute-start | bytes 159752 | tf_op jit(solution)/shard_map/ppermute | solution.py:47
  26.1 2.4 %collective-permute-done.3 = bf16[32,1600]{1,0:T(8,128)(2,1)S(1)} collective-permute-done((bf16[32,1600]{1,0:T(8,128)(2,1)S(1)}, bf16[32,1600]{1,0:T(8,128)(2,1)S(1)}, u32[]{:S(2)}, u32[]{:S(2)}) %collective-permute-start.3) | collective-permute-done | bytes 102432 | tf_op jit(solution)/shard_map/ppermute | solution.py:47
  28.5 1.0 %collective-permute-done.5 = bf16[32,768]{1,0:T(8,128)(2,1)S(1)} collective-permute-done((bf16[32,768]{1,0:T(8,128)(2,1)S(1)}, bf16[32,768]{1,0:T(8,128)(2,1)S(1)}, u32[]{:S(2)}, u32[]{:S(2)}) %collective-permute-start.5) | collective-permute-done | bytes 49184 | tf_op jit(solution)/shard_map/ppermute | solution.py:47
  29.7 0.5 %collective-permute-start.7 = (bf16[32,768]{1,0:T(8,128)(2,1)S(1)}, bf16[32,768]{1,0:T(8,128)(2,1)S(1)}, u32[]{:S(2)}, u32[]{:S(2)}) collective-permute-start(bf16[32,768]{1,0:T(8,128)(2,1)S(1)} %get-tuple-element.31), channel_id=1, source_target_pairs={{0,8},{8,0},{16,24},{24,16},{1,9},{9,1},{17,25},{25,17},{2,10},{10... | collective-permute-start | bytes 147464 | tf_op jit(solution)/shard_map/ppermute | solution.py:11
  30.6 0.5 %collective-permute-done.7 = bf16[32,768]{1,0:T(8,128)(2,1)S(1)} collective-permute-done((bf16[32,768]{1,0:T(8,128)(2,1)S(1)}, bf16[32,768]{1,0:T(8,128)(2,1)S(1)}, u32[]{:S(2)}, u32[]{:S(2)}) %collective-permute-start.7) | collective-permute-done | bytes 49184 | tf_op jit(solution)/shard_map/ppermute | solution.py:11
  32.6 0.7 %reshape.44 = bf16[32,2,640]{2,1,0:T(2,128)(2,1)} reshape(bf16[2,2,16,640]{3,2,1,0:T(8,128)(2,1)S(1)} %reverse_select_fusion) | data formatting | bytes 163840 | tf_op jit(solution)/shard_map/reshape | solution.py:90
  33.3 3.0 %all-to-all-start.1 = ((bf16[32,2,640]{2,1,0:T(2,128)(2,1)}), bf16[32,2,640]{2,1,0:T(2,128)(2,1)S(1)}, u32[]{:S(2)}, u32[]{:S(2)}) async-start(bf16[32,2,640]{2,1,0:T(2,128)(2,1)} %reshape.44), calls=%async_computation.1 | async-start | bytes 163840 | tf_op jit(solution)/shard_map/all_to_all | solution.py:93
  36.6 2.1 %multiply_convert_fusion.1 = bf16[640,1600]{0,1:T(8,128)(2,1)} fusion(bf16[64,640]{1,0:T(8,128)(2,1)S(1)} %bitcast.43, bf16[32,832]{1,0:T(8,128)(2,1)S(1)} %get-tuple-element.28, bf16[32,832]{1,0:T(8,128)(2,1)S(1)} %get-tuple-element.21, bf16[32,768]{1,0:T(8,128)(2,1)S(1)} %get-tuple-element.31, bf16[32,768]{1,0:T(8,128)(2,1)S(1)} %collective-permute-done.7), kind=kOutput, calls=%fused_computation.1 | convolution fusion | flops 133939200 | bytes 2334720 | tf_op jit(solution)/shard_map/td,tf->df/dot_general | solution.py:98
  38.6 2.1 %multiply_convert_fusion.2 = bf16[640,1600]{0,1:T(8,128)(2,1)} fusion(bf16[64,640]{1,0:T(8,128)(2,1)S(1)} %bitcast.44, bf16[32,832]{1,0:T(8,128)(2,1)S(1)} %get-tuple-element.27, bf16[32,832]{1,0:T(8,128)(2,1)S(1)} %get-tuple-element.20, bf16[32,768]{1,0:T(8,128)(2,1)S(1)} %get-tuple-element.30, bf16[32,768]{1,0:T(8,128)(2,1)S(1)} %collective-permute-done.6), kind=kOutput, calls=%fused_computation.2 | convolution fusion | flops 133939200 | bytes 2334720 | tf_op jit(solution)/shard_map/td,tf->df/dot_general | solution.py:97
  40.7 2.0 %multiply_convert_fusion = bf16[1600,640]{1,0:T(8,128)(2,1)} fusion(bf16[64,640]{1,0:T(8,128)(2,1)S(1)} %bitcast.46, bf16[32,1600]{1,0:T(8,128)(2,1)S(1)} %pad_maximum_fusion.5, bf16[32,1600]{1,0:T(8,128)(2,1)S(1)} %collective-permute-done.10), kind=kOutput, calls=%fused_computation | convolution fusion | flops 133529600 | bytes 2334720 | tf_op jit(solution)/shard_map/tf,td->fd/dot_general | solution.py:99
  42.7 1.0 %all-to-all-done.1 = bf16[32,2,640]{2,1,0:T(2,128)(2,1)S(1)} async-done(((bf16[32,2,640]{2,1,0:T(2,128)(2,1)}), bf16[32,2,640]{2,1,0:T(2,128)(2,1)S(1)}, u32[]{:S(2)}, u32[]{:S(2)}) %all-to-all-start.1) | async-done | bytes 81952 | tf_op jit(solution)/shard_map/all_to_all | solution.py:93
  43.7 0.7 %bitcast_reduce_fusion = bf16[4,2,640]{2,1,0:T(2,128)(2,1)} fusion(bf16[32,2,640]{2,1,0:T(2,128)(2,1)S(1)} %all-to-all-done.1), kind=kLoop, calls=%fused_computation.67 | loop fusion | flops 35840 | bytes 92160 | tf_op jit(solution)/shard_map/reduce_sum | solution.py:94
  (46 shorter events, 3.3 us)
Async XLA Ops:
  0.6 17.2 %copy-start = (bf16[1600,640]{1,0:T(8,128)(2,1)S(1)}, bf16[1600,640]{1,0:T(8,128)(2,1)}, u32[]{:S(2)}) copy-start(bf16[1600,640]{1,0:T(8,128)(2,1)} %param.9) | copy-start | bytes 6144004
  2.4 15.2 %all-to-all-start = ((bf16[32,4,640]{2,1,0:T(4,128)(2,1)}), bf16[32,4,640]{2,1,0:T(4,128)(2,1)S(1)}, u32[]{:S(2)}, u32[]{:S(2)}) async-start(bf16[32,4,640]{2,1,0:T(4,128)(2,1)} %bitcast.4), calls=%async_computation | async-start | bytes 327680 | tf_op jit(solution)/shard_map/all_to_all | solution.py:27
  17.8 1.6 %copy-start.1 = (bf16[640,1600]{0,1:T(8,128)(2,1)S(1)}, bf16[640,1600]{0,1:T(8,128)(2,1)}, u32[]{:S(2)}) copy-start(bf16[640,1600]{0,1:T(8,128)(2,1)} %param.8) | copy-start | bytes 6144004
  18.6 3.1 %copy-start.2 = (bf16[640,1600]{0,1:T(8,128)(2,1)S(1)}, bf16[640,1600]{0,1:T(8,128)(2,1)}, u32[]{:S(2)}) copy-start(bf16[640,1600]{0,1:T(8,128)(2,1)} %param.7) | copy-start | bytes 6144004
  18.7 1.7 %collective-permute-start = (bf16[32,1600]{1,0:T(8,128)(2,1)S(1)}, bf16[32,1600]{1,0:T(8,128)(2,1)S(1)}, u32[]{:S(2)}, u32[]{:S(2)}) collective-permute-start(bf16[32,1600]{1,0:T(8,128)(2,1)S(1)} %slice.190), channel_id=1, source_target_pairs={{0,8},{8,0},{16,24},{24,16},{1,9},{9,1},{17,25},{25,17},{2,10},{10... | collective-permute-start | bytes 307208 | tf_op jit(solution)/shard_map/ppermute | solution.py:11
  20.1 2.5 %collective-permute-start.2 = (bf16[32,1600]{1,0:T(8,128)(2,1)S(1)}, bf16[32,1600]{1,0:T(8,128)(2,1)S(1)}, u32[]{:S(2)}, u32[]{:S(2)}) collective-permute-start(bf16[32,1600]{1,0:T(8,128)(2,1)S(1)} %slice.189), channel_id=1, source_target_pairs={{0,8},{8,0},{16,24},{24,16},{1,9},{9,1},{17,25},{25,17},{2,10},{10... | collective-permute-start | bytes 307208 | tf_op jit(solution)/shard_map/ppermute | solution.py:11
  20.4 5.7 %collective-permute-start.1 = (bf16[32,1600]{1,0:T(8,128)(2,1)S(1)}, bf16[32,1600]{1,0:T(8,128)(2,1)S(1)}, u32[]{:S(2)}, u32[]{:S(2)}) collective-permute-start(bf16[32,1600]{1,0:T(8,128)(2,1)S(1)} %add_convert_fusion), channel_id=1, source_target_pairs={{0,16},{8,24},{16,0},{24,8},{1,17},{9,25},{17,1},{25,9},{2,18},{10... | collective-permute-start | bytes 307208 | tf_op jit(solution)/shard_map/ppermute | solution.py:47
  22.5 1.4 %collective-permute-start.4 = (bf16[32,1600]{1,0:T(8,128)(2,1)S(1)}, bf16[32,1600]{1,0:T(8,128)(2,1)S(1)}, u32[]{:S(2)}, u32[]{:S(2)}) collective-permute-start(bf16[32,1600]{1,0:T(8,128)(2,1)S(1)} %slice.188), channel_id=1, source_target_pairs={{0,8},{8,0},{16,24},{24,16},{1,9},{9,1},{17,25},{25,17},{2,10},{10... | collective-permute-start | bytes 307208 | tf_op jit(solution)/shard_map/ppermute | solution.py:11
  22.7 5.8 %collective-permute-start.3 = (bf16[32,1600]{1,0:T(8,128)(2,1)S(1)}, bf16[32,1600]{1,0:T(8,128)(2,1)S(1)}, u32[]{:S(2)}, u32[]{:S(2)}) collective-permute-start(bf16[32,1600]{1,0:T(8,128)(2,1)S(1)} %fusion.8), channel_id=1, source_target_pairs={{0,16},{8,24},{16,0},{24,8},{1,17},{9,25},{17,1},{25,9},{2,18},{10... | collective-permute-start | bytes 307208 | tf_op jit(solution)/shard_map/ppermute | solution.py:47
  24.0 5.6 %collective-permute-start.5 = (bf16[32,768]{1,0:T(8,128)(2,1)S(1)}, bf16[32,768]{1,0:T(8,128)(2,1)S(1)}, u32[]{:S(2)}, u32[]{:S(2)}) collective-permute-start(bf16[32,768]{1,0:T(8,128)(2,1)S(1)} %slice.114), channel_id=1, source_target_pairs={{0,16},{8,24},{16,0},{24,8},{1,17},{9,25},{17,1},{25,9},{2,18},{10... | collective-permute-start | bytes 147464 | tf_op jit(solution)/shard_map/ppermute | solution.py:47
  24.9 5.5 %collective-permute-start.8 = (bf16[32,832]{1,0:T(8,128)(2,1)S(1)}, bf16[32,832]{1,0:T(8,128)(2,1)S(1)}, u32[]{:S(2)}, u32[]{:S(2)}) collective-permute-start(bf16[32,832]{1,0:T(8,128)(2,1)S(1)} %slice.119), channel_id=1, source_target_pairs={{0,16},{8,24},{16,0},{24,8},{1,17},{9,25},{17,1},{25,9},{2,18},{10... | collective-permute-start | bytes 159752 | tf_op jit(solution)/shard_map/ppermute | solution.py:47
  29.6 1.8 %collective-permute-start.6 = (bf16[32,768]{1,0:T(8,128)(2,1)S(1)}, bf16[32,768]{1,0:T(8,128)(2,1)S(1)}, u32[]{:S(2)}, u32[]{:S(2)}) collective-permute-start(bf16[32,768]{1,0:T(8,128)(2,1)S(1)} %get-tuple-element.30), channel_id=1, source_target_pairs={{0,8},{8,0},{16,24},{24,16},{1,9},{9,1},{17,25},{25,17},{2,10},{10... | collective-permute-start | bytes 147464 | tf_op jit(solution)/shard_map/ppermute | solution.py:11
  29.7 1.4 %collective-permute-start.7 = (bf16[32,768]{1,0:T(8,128)(2,1)S(1)}, bf16[32,768]{1,0:T(8,128)(2,1)S(1)}, u32[]{:S(2)}, u32[]{:S(2)}) collective-permute-start(bf16[32,768]{1,0:T(8,128)(2,1)S(1)} %get-tuple-element.31), channel_id=1, source_target_pairs={{0,8},{8,0},{16,24},{24,16},{1,9},{9,1},{17,25},{25,17},{2,10},{10... | collective-permute-start | bytes 147464 | tf_op jit(solution)/shard_map/ppermute | solution.py:11
  30.5 1.4 %collective-permute-start.9 = (bf16[64,832]{1,0:T(8,128)(2,1)S(1)}, bf16[64,832]{1,0:T(8,128)(2,1)S(1)}, u32[]{:S(2)}, u32[]{:S(2)}) collective-permute-start(bf16[64,832]{1,0:T(8,128)(2,1)S(1)} %pad_maximum_fusion.1), channel_id=1, source_target_pairs={{0,8},{8,0},{16,24},{24,16},{1,9},{9,1},{17,25},{25,17},{2,10},{10... | collective-permute-start | bytes 319496 | tf_op jit(solution)/shard_map/ppermute | solution.py:11
  33.3 10.4 %all-to-all-start.1 = ((bf16[32,2,640]{2,1,0:T(2,128)(2,1)}), bf16[32,2,640]{2,1,0:T(2,128)(2,1)S(1)}, u32[]{:S(2)}, u32[]{:S(2)}) async-start(bf16[32,2,640]{2,1,0:T(2,128)(2,1)} %reshape.44), calls=%async_computation.1 | async-start | bytes 163840 | tf_op jit(solution)/shard_map/all_to_all | solution.py:93
  36.3 4.4 %collective-permute-start.10 = (bf16[32,1600]{1,0:T(8,128)(2,1)S(1)}, bf16[32,1600]{1,0:T(8,128)(2,1)S(1)}, u32[]{:S(2)}, u32[]{:S(2)}) collective-permute-start(bf16[32,1600]{1,0:T(8,128)(2,1)S(1)} %pad_maximum_fusion.5), channel_id=1, source_target_pairs={{0,8},{8,0},{16,24},{24,16},{1,9},{9,1},{17,25},{25,17},{2,10},{10... | collective-permute-start | bytes 307208 | tf_op jit(solution)/shard_map/ppermute | solution.py:11

commit v8 on v6

--- a/solution.py
+++ b/solution.py
@@ -33,7 +33,7 @@
         value = jnp.where(core == 0, value[:, ::-1], value)
         return value.transpose(1, 0, 2, 3).reshape(2 * half, depth)
 
-    tok, cot = by_core(both[:, :rows]), by_core(both[:, rows:])
+    cot = by_core(both[:, rows:])
 
     gate_rows, up_rows = gate_weight.T, up_weight.T
 
@@ -49,8 +49,9 @@
         return total
 
     hid_p = jnp.einsum("td,fd->tf", cot, down_weight, preferred_element_type=F32)
-    tok_up, hid_p = lax.optimization_barrier((tok, hid_p))
-    up_p = jnp.einsum("td,fd->tf", tok_up, up_rows, preferred_element_type=F32)
+    both, hid_p = lax.optimization_barrier((both, hid_p))
+    tok = by_core(both[:, :rows])
+    up_p = jnp.einsum("td,fd->tf", tok, up_rows, preferred_element_type=F32)
     hidden_grad, up = core_sum(hid_p), core_sum(up_p)
     tok_gate, hidden_grad = lax.optimization_barrier((tok, hidden_grad))
     gate_p = jnp.einsum("td,fd->tf", tok_gate, gate_rows, preferred_element_type=F32)

time: 44.7 us -> 46.2 us (1.034)
  matrix products: 9.6 us -> 11.3 us
    dot_general x1, matrix products: 0.74 us -> 2.46 us  [local(): up_p = jnp.einsum('td,fd->tf', tok, up_rows, preferred_element_type=F32)]
    unnamed x6, local copies, waits for them, and re-layouts: 0.5 us -> 0.02 us
  transfers between devices with their start and end apart: 14 -> 14, of which waited for: 8 -> 8; matrix products, arithmetic and copies ran while one was open for 19% -> 22% of each run, Pallas kernels for 0% -> 0%
where the time goes in v8:
time: 46.2 us; the launch traced here: 45.9 us
  starting transfers between devices  16.6 us (36%)
  waiting for transfers between devices  13.2 us (29%)
  matrix products  11.3 us (24%)
  other arithmetic  2.05 us (4%)
  local copies, waits for them, and re-layouts  1.7 us (4%)
  between operations  0.94 us (2%)
    all_to_all x1, waiting for transfers between devices, local(): lax.all_to_all(slices.reshape(n_dp * n_tensor, 2 * rows, depth), ('dp', '...  7.91 us
    all_to_all x1, starting transfers between devices, local(): lax.all_to_all(slices.reshape(n_dp * n_tensor, 2 * rows, depth), ('dp', '...  7.3 us
    ppermute x4, starting transfers between devices, chip_sum(): lax.ppermute(mine, 'dp', [(i, (i + 2 * shift) % n_dp) for i in range(n_dp)])  4.25 us
    ppermute x4, waiting for transfers between devices, chip_sum(): lax.ppermute(mine, 'dp', [(i, (i + 2 * shift) % n_dp) for i in range(n_dp)])  3.58 us
    all_to_all x1, starting transfers between devices, local(): lax.all_to_all(shares, ('dp', 'tensor'), split_axis=0, concat_axis=0, til...  2.97 us
    dot_general x1, matrix products, local(): up_p = jnp.einsum('td,fd->tf', tok, up_rows, preferred_element_type=F32)  2.46 us
    ppermute x8, starting transfers between devices, swap_cores(): return lax.ppermute(value, 'dp', [(i, i ^ 1) for i in range(n_dp)])  2.13 us
    dot_general x1, matrix products, local(): jnp.einsum('td,tf->df', tok, gate_grad, preferred_element_type=F32) / n_dp  2.05 us
  transfers between devices with their start and end apart: 14, of which 8 were waited for; matrix products, arithmetic and copies ran while one was open for 22% of the time, Pallas kernels for 0%

profile of v8, /device:TPU:0, one launch (start us, length us, event | category | flops | bytes accessed | tf_op | source)
XLA Modules:
  0.0 45.9 jit_solution(8379781466870420470)
XLA Ops:
  0.6 1.0 %fusion.44 = (bf16[1,4,640]{2,1,0:T(4,128)(2,1)S(1)}, bf16[1,4,640]{2,1,0:T(4,128)(2,1)S(1)}, bf16[1,4,640]{2,1,0:T(4,128)(2,1)S(1)}, bf16[1,4,640]{2,1,0:T(4,128)(2,1)S(1)}) fusion(bf16[2,2560]{1,0:T(2,128)(2,1)} %param.6, bf16[2,2560]{1,0:T(2,128)(2,1)} %param.5), kind=kLoop, calls=%fused_computation.82 | loop fusion | flops 40960 | bytes 40960 | tf_op jit(solution)/shard_map/stack | solution.py:25
  1.6 0.7 %broadcast_in_dim.2 = bf16[4,8,4,640]{3,2,1,0:T(4,128)(2,1)} broadcast(bf16[4,4,640]{2,1,0:T(4,128)(2,1)S(1)} %pad_maximum_fusion.1), dimensions={0,2,3} | broadcast | bytes 184320 | tf_op jit(solution)/shard_map/broadcast_in_dim | solution.py:26
  2.4 7.3 %all-to-all-start = ((bf16[32,4,640]{2,1,0:T(4,128)(2,1)}), bf16[32,4,640]{2,1,0:T(4,128)(2,1)S(1)}, u32[]{:S(2)}, u32[]{:S(2)}) async-start(bf16[32,4,640]{2,1,0:T(4,128)(2,1)} %bitcast.4), calls=%async_computation | async-start | bytes 327680 | tf_op jit(solution)/shard_map/all_to_all | solution.py:27
  9.7 7.9 %all-to-all-done = bf16[32,4,640]{2,1,0:T(4,128)(2,1)S(1)} async-done(((bf16[32,4,640]{2,1,0:T(4,128)(2,1)}), bf16[32,4,640]{2,1,0:T(4,128)(2,1)S(1)}, u32[]{:S(2)}, u32[]{:S(2)}) %all-to-all-start) | async-done | bytes 163872 | tf_op jit(solution)/shard_map/all_to_all | solution.py:27
  17.8 0.7 %fusion.53 = f32[64,1600]{1,0:T(8,128)S(1)} fusion(bf16[64,640]{1,0:T(8,128)(2,1)S(1)} %bitcast.45, bf16[1600,640]{1,0:T(8,128)(2,1)S(1)} %copy-done), kind=kOutput, calls=%fused_computation.91 | convolution fusion | flops 131072000 | bytes 2539520 | tf_op jit(solution)/shard_map/td,fd->tf/dot_general | solution.py:51
  18.9 2.5 %fusion.54 = f32[64,1600]{1,0:T(8,128)S(1)} fusion(bf16[64,640]{1,0:T(8,128)(2,1)S(1)} %bitcast.41, bf16[640,1600]{0,1:T(8,128)(2,1)} %param.8), kind=kOutput, calls=%fused_computation.92 | convolution fusion | flops 131072000 | bytes 2539520 | tf_op jit(solution)/shard_map/td,fd->tf/dot_general | solution.py:54
  21.4 0.4 collective-permute-start.2
  21.8 1.4 %collective-permute-start.1 = (bf16[32,1600]{1,0:T(8,128)(2,1)S(1)}, bf16[32,1600]{1,0:T(8,128)(2,1)S(1)}, u32[]{:S(2)}, u32[]{:S(2)}) collective-permute-start(bf16[32,1600]{1,0:T(8,128)(2,1)S(1)} %add_convert_fusion), channel_id=1, source_target_pairs={{0,16},{8,24},{16,0},{24,8},{1,17},{9,25},{17,1},{25,9},{2,18},{10... | collective-permute-start | bytes 307208 | tf_op jit(solution)/shard_map/ppermute | solution.py:47
  23.2 0.7 %fusion.55 = f32[64,1600]{1,0:T(8,128)S(1)} fusion(bf16[64,640]{1,0:T(8,128)(2,1)S(1)} %bitcast.42, bf16[640,1600]{0,1:T(8,128)(2,1)S(1)} %copy-done.2), kind=kOutput, calls=%fused_computation.93 | convolution fusion | flops 131072000 | bytes 2539520 | tf_op jit(solution)/shard_map/td,fd->tf/dot_general | solution.py:57
  24.1 0.8 %collective-permute-start.3 = (bf16[32,1600]{1,0:T(8,128)(2,1)S(1)}, bf16[32,1600]{1,0:T(8,128)(2,1)S(1)}, u32[]{:S(2)}, u32[]{:S(2)}) collective-permute-start(bf16[32,1600]{1,0:T(8,128)(2,1)S(1)} %fusion.7), channel_id=1, source_target_pairs={{0,16},{8,24},{16,0},{24,8},{1,17},{9,25},{17,1},{25,9},{2,18},{10... | collective-permute-start | bytes 307208 | tf_op jit(solution)/shard_map/ppermute | solution.py:47
  24.9 0.5 %collective-permute-done.4 = bf16[32,1600]{1,0:T(8,128)(2,1)S(1)} collective-permute-done((bf16[32,1600]{1,0:T(8,128)(2,1)S(1)}, bf16[32,1600]{1,0:T(8,128)(2,1)S(1)}, u32[]{:S(2)}, u32[]{:S(2)}) %collective-permute-start.4) | collective-permute-done | bytes 102432 | tf_op jit(solution)/shard_map/ppermute | solution.py:11
  25.4 0.9 %collective-permute-start.5 = (bf16[32,768]{1,0:T(8,128)(2,1)S(1)}, bf16[32,768]{1,0:T(8,128)(2,1)S(1)}, u32[]{:S(2)}, u32[]{:S(2)}) collective-permute-start(bf16[32,768]{1,0:T(8,128)(2,1)S(1)} %slice.105), channel_id=1, source_target_pairs={{0,16},{8,24},{16,0},{24,8},{1,17},{9,25},{17,1},{25,9},{2,18},{10... | collective-permute-start | bytes 147464 | tf_op jit(solution)/shard_map/ppermute | solution.py:47
  26.3 1.2 %collective-permute-start.8 = (bf16[32,832]{1,0:T(8,128)(2,1)S(1)}, bf16[32,832]{1,0:T(8,128)(2,1)S(1)}, u32[]{:S(2)}, u32[]{:S(2)}) collective-permute-start(bf16[32,832]{1,0:T(8,128)(2,1)S(1)} %slice.110), channel_id=1, source_target_pairs={{0,16},{8,24},{16,0},{24,8},{1,17},{9,25},{17,1},{25,9},{2,18},{10... | collective-permute-start | bytes 159752 | tf_op jit(solution)/shard_map/ppermute | solution.py:47
  27.6 2.4 %collective-permute-done.3 = bf16[32,1600]{1,0:T(8,128)(2,1)S(1)} collective-permute-done((bf16[32,1600]{1,0:T(8,128)(2,1)S(1)}, bf16[32,1600]{1,0:T(8,128)(2,1)S(1)}, u32[]{:S(2)}, u32[]{:S(2)}) %collective-permute-start.3) | collective-permute-done | bytes 102432 | tf_op jit(solution)/shard_map/ppermute | solution.py:47
  30.0 1.0 %collective-permute-done.5 = bf16[32,768]{1,0:T(8,128)(2,1)S(1)} collective-permute-done((bf16[32,768]{1,0:T(8,128)(2,1)S(1)}, bf16[32,768]{1,0:T(8,128)(2,1)S(1)}, u32[]{:S(2)}, u32[]{:S(2)}) %collective-permute-start.5) | collective-permute-done | bytes 49184 | tf_op jit(solution)/shard_map/ppermute | solution.py:47
  31.2 0.5 %collective-permute-start.7 = (bf16[32,768]{1,0:T(8,128)(2,1)S(1)}, bf16[32,768]{1,0:T(8,128)(2,1)S(1)}, u32[]{:S(2)}, u32[]{:S(2)}) collective-permute-start(bf16[32,768]{1,0:T(8,128)(2,1)S(1)} %get-tuple-element.31), channel_id=1, source_target_pairs={{0,8},{8,0},{16,24},{24,16},{1,9},{9,1},{17,25},{25,17},{2,10},{10... | collective-permute-start | bytes 147464 | tf_op jit(solution)/shard_map/ppermute | solution.py:11
  32.0 0.5 %collective-permute-start.10 = (bf16[32,832]{1,0:T(8,128)(2,1)S(1)}, bf16[32,832]{1,0:T(8,128)(2,1)S(1)}, u32[]{:S(2)}, u32[]{:S(2)}) collective-permute-start(bf16[32,832]{1,0:T(8,128)(2,1)S(1)} %get-tuple-element.28), channel_id=1, source_target_pairs={{0,8},{8,0},{16,24},{24,16},{1,9},{9,1},{17,25},{25,17},{2,10},{10... | collective-permute-start | bytes 159752 | tf_op jit(solution)/shard_map/ppermute | solution.py:11
  34.1 0.7 %reshape.44 = bf16[32,2,640]{2,1,0:T(2,128)(2,1)} reshape(bf16[2,2,16,640]{3,2,1,0:T(8,128)(2,1)S(1)} %reverse_select_fusion) | data formatting | bytes 163840 | tf_op jit(solution)/shard_map/reshape | solution.py:86
  34.8 3.0 %all-to-all-start.1 = ((bf16[32,2,640]{2,1,0:T(2,128)(2,1)}), bf16[32,2,640]{2,1,0:T(2,128)(2,1)S(1)}, u32[]{:S(2)}, u32[]{:S(2)}) async-start(bf16[32,2,640]{2,1,0:T(2,128)(2,1)} %reshape.44), calls=%async_computation.1 | async-start | bytes 163840 | tf_op jit(solution)/shard_map/all_to_all | solution.py:89
  38.1 2.1 %multiply_convert_fusion.1 = bf16[640,1600]{0,1:T(8,128)(2,1)} fusion(bf16[64,640]{1,0:T(8,128)(2,1)S(1)} %bitcast.43, bf16[32,832]{1,0:T(8,128)(2,1)S(1)} %get-tuple-element.28, bf16[32,832]{1,0:T(8,128)(2,1)S(1)} %collective-permute-done.10, bf16[32,768]{1,0:T(8,128)(2,1)S(1)} %get-tuple-element.31, bf16[32,768]{1,0:T(8,128)(2,1)S(1)} %collective-permute-done.7), kind=kOutput, calls=%fused_computation.1 | convolution fusion | flops 133939200 | bytes 2334720 | tf_op jit(solution)/shard_map/td,tf->df/dot_general | solution.py:94
  40.1 2.1 %multiply_convert_fusion.2 = bf16[640,1600]{0,1:T(8,128)(2,1)} fusion(bf16[64,640]{1,0:T(8,128)(2,1)S(1)} %bitcast.44, bf16[32,832]{1,0:T(8,128)(2,1)S(1)} %get-tuple-element.27, bf16[32,832]{1,0:T(8,128)(2,1)S(1)} %collective-permute-done.9, bf16[32,768]{1,0:T(8,128)(2,1)S(1)} %get-tuple-element.30, bf16[32,768]{1,0:T(8,128)(2,1)S(1)} %collective-permute-done.6), kind=kOutput, calls=%fused_computation.2 | convolution fusion | flops 133939200 | bytes 2334720 | tf_op jit(solution)/shard_map/td,tf->df/dot_general | solution.py:93
  42.2 2.0 %multiply_convert_fusion = bf16[1600,640]{1,0:T(8,128)(2,1)} fusion(bf16[64,640]{1,0:T(8,128)(2,1)S(1)} %bitcast.46, bf16[32,1600]{1,0:T(8,128)(2,1)S(1)} %pad_maximum_fusion, bf16[32,1600]{1,0:T(8,128)(2,1)S(1)} %collective-permute-done.11), kind=kOutput, calls=%fused_computation | convolution fusion | flops 133529600 | bytes 2334720 | tf_op jit(solution)/shard_map/tf,td->fd/dot_general | solution.py:95
  44.2 1.0 %all-to-all-done.1 = bf16[32,2,640]{2,1,0:T(2,128)(2,1)S(1)} async-done(((bf16[32,2,640]{2,1,0:T(2,128)(2,1)}), bf16[32,2,640]{2,1,0:T(2,128)(2,1)S(1)}, u32[]{:S(2)}, u32[]{:S(2)}) %all-to-all-start.1) | async-done | bytes 81952 | tf_op jit(solution)/shard_map/all_to_all | solution.py:89
  45.2 0.7 %bitcast_reduce_fusion = bf16[4,2,640]{2,1,0:T(2,128)(2,1)} fusion(bf16[32,2,640]{2,1,0:T(2,128)(2,1)S(1)} %all-to-all-done.1), kind=kLoop, calls=%fused_computation.67 | loop fusion | flops 35840 | bytes 92160 | tf_op jit(solution)/shard_map/reduce_sum | solution.py:90
  (49 shorter events, 3.2 us)
Async XLA Ops:
  0.6 17.1 %copy-start = (bf16[1600,640]{1,0:T(8,128)(2,1)S(1)}, bf16[1600,640]{1,0:T(8,128)(2,1)}, u32[]{:S(2)}) copy-start(bf16[1600,640]{1,0:T(8,128)(2,1)} %param.9) | copy-start | bytes 6144004
  2.4 15.2 %all-to-all-start = ((bf16[32,4,640]{2,1,0:T(4,128)(2,1)}), bf16[32,4,640]{2,1,0:T(4,128)(2,1)S(1)}, u32[]{:S(2)}, u32[]{:S(2)}) async-start(bf16[32,4,640]{2,1,0:T(4,128)(2,1)} %bitcast.4), calls=%async_computation | async-start | bytes 327680 | tf_op jit(solution)/shard_map/all_to_all | solution.py:27
  18.6 4.6 %copy-start.2 = (bf16[640,1600]{0,1:T(8,128)(2,1)S(1)}, bf16[640,1600]{0,1:T(8,128)(2,1)}, u32[]{:S(2)}) copy-start(bf16[640,1600]{0,1:T(8,128)(2,1)} %param.7) | copy-start | bytes 6144004
  18.7 3.1 %collective-permute-start = (bf16[32,1600]{1,0:T(8,128)(2,1)S(1)}, bf16[32,1600]{1,0:T(8,128)(2,1)S(1)}, u32[]{:S(2)}, u32[]{:S(2)}) collective-permute-start(bf16[32,1600]{1,0:T(8,128)(2,1)S(1)} %slice.177), channel_id=1, source_target_pairs={{0,8},{8,0},{16,24},{24,16},{1,9},{9,1},{17,25},{25,17},{2,10},{10... | collective-permute-start | bytes 307208 | tf_op jit(solution)/shard_map/ppermute | solution.py:11
  21.4 2.7 %collective-permute-start.2 = (bf16[32,1600]{1,0:T(8,128)(2,1)S(1)}, bf16[32,1600]{1,0:T(8,128)(2,1)S(1)}, u32[]{:S(2)}, u32[]{:S(2)}) collective-permute-start(bf16[32,1600]{1,0:T(8,128)(2,1)S(1)} %slice.176), channel_id=1, source_target_pairs={{0,8},{8,0},{16,24},{24,16},{1,9},{9,1},{17,25},{25,17},{2,10},{10... | collective-permute-start | bytes 307208 | tf_op jit(solution)/shard_map/ppermute | solution.py:11
  21.8 5.7 %collective-permute-start.1 = (bf16[32,1600]{1,0:T(8,128)(2,1)S(1)}, bf16[32,1600]{1,0:T(8,128)(2,1)S(1)}, u32[]{:S(2)}, u32[]{:S(2)}) collective-permute-start(bf16[32,1600]{1,0:T(8,128)(2,1)S(1)} %add_convert_fusion), channel_id=1, source_target_pairs={{0,16},{8,24},{16,0},{24,8},{1,17},{9,25},{17,1},{25,9},{2,18},{10... | collective-permute-start | bytes 307208 | tf_op jit(solution)/shard_map/ppermute | solution.py:47
  24.0 8.6 %copy-start.1 = (bf16[640,1600]{0,1:T(8,128)(2,1)S(1)}, bf16[640,1600]{0,1:T(8,128)(2,1)}, u32[]{:S(2)}) copy-start(bf16[640,1600]{0,1:T(8,128)(2,1)} %param.8) | copy-start | bytes 6144004
  24.0 1.4 %collective-permute-start.4 = (bf16[32,1600]{1,0:T(8,128)(2,1)S(1)}, bf16[32,1600]{1,0:T(8,128)(2,1)S(1)}, u32[]{:S(2)}, u32[]{:S(2)}) collective-permute-start(bf16[32,1600]{1,0:T(8,128)(2,1)S(1)} %slice.175), channel_id=1, source_target_pairs={{0,8},{8,0},{16,24},{24,16},{1,9},{9,1},{17,25},{25,17},{2,10},{10... | collective-permute-start | bytes 307208 | tf_op jit(solution)/shard_map/ppermute | solution.py:11
  24.1 5.8 %collective-permute-start.3 = (bf16[32,1600]{1,0:T(8,128)(2,1)S(1)}, bf16[32,1600]{1,0:T(8,128)(2,1)S(1)}, u32[]{:S(2)}, u32[]{:S(2)}) collective-permute-start(bf16[32,1600]{1,0:T(8,128)(2,1)S(1)} %fusion.7), channel_id=1, source_target_pairs={{0,16},{8,24},{16,0},{24,8},{1,17},{9,25},{17,1},{25,9},{2,18},{10... | collective-permute-start | bytes 307208 | tf_op jit(solution)/shard_map/ppermute | solution.py:47
  25.4 5.6 %collective-permute-start.5 = (bf16[32,768]{1,0:T(8,128)(2,1)S(1)}, bf16[32,768]{1,0:T(8,128)(2,1)S(1)}, u32[]{:S(2)}, u32[]{:S(2)}) collective-permute-start(bf16[32,768]{1,0:T(8,128)(2,1)S(1)} %slice.105), channel_id=1, source_target_pairs={{0,16},{8,24},{16,0},{24,8},{1,17},{9,25},{17,1},{25,9},{2,18},{10... | collective-permute-start | bytes 147464 | tf_op jit(solution)/shard_map/ppermute | solution.py:47
  26.3 5.5 %collective-permute-start.8 = (bf16[32,832]{1,0:T(8,128)(2,1)S(1)}, bf16[32,832]{1,0:T(8,128)(2,1)S(1)}, u32[]{:S(2)}, u32[]{:S(2)}) collective-permute-start(bf16[32,832]{1,0:T(8,128)(2,1)S(1)} %slice.110), channel_id=1, source_target_pairs={{0,16},{8,24},{16,0},{24,8},{1,17},{9,25},{17,1},{25,9},{2,18},{10... | collective-permute-start | bytes 159752 | tf_op jit(solution)/shard_map/ppermute | solution.py:47
  31.1 1.8 %collective-permute-start.6 = (bf16[32,768]{1,0:T(8,128)(2,1)S(1)}, bf16[32,768]{1,0:T(8,128)(2,1)S(1)}, u32[]{:S(2)}, u32[]{:S(2)}) collective-permute-start(bf16[32,768]{1,0:T(8,128)(2,1)S(1)} %get-tuple-element.30), channel_id=1, source_target_pairs={{0,8},{8,0},{16,24},{24,16},{1,9},{9,1},{17,25},{25,17},{2,10},{10... | collective-permute-start | bytes 147464 | tf_op jit(solution)/shard_map/ppermute | solution.py:11
  31.2 1.4 %collective-permute-start.7 = (bf16[32,768]{1,0:T(8,128)(2,1)S(1)}, bf16[32,768]{1,0:T(8,128)(2,1)S(1)}, u32[]{:S(2)}, u32[]{:S(2)}) collective-permute-start(bf16[32,768]{1,0:T(8,128)(2,1)S(1)} %get-tuple-element.31), channel_id=1, source_target_pairs={{0,8},{8,0},{16,24},{24,16},{1,9},{9,1},{17,25},{25,17},{2,10},{10... | collective-permute-start | bytes 147464 | tf_op jit(solution)/shard_map/ppermute | solution.py:11
  31.9 1.3 %collective-permute-start.9 = (bf16[32,832]{1,0:T(8,128)(2,1)S(1)}, bf16[32,832]{1,0:T(8,128)(2,1)S(1)}, u32[]{:S(2)}, u32[]{:S(2)}) collective-permute-start(bf16[32,832]{1,0:T(8,128)(2,1)S(1)} %get-tuple-element.27), channel_id=1, source_target_pairs={{0,8},{8,0},{16,24},{24,16},{1,9},{9,1},{17,25},{25,17},{2,10},{10... | collective-permute-start | bytes 159752 | tf_op jit(solution)/shard_map/ppermute | solution.py:11
  32.0 1.4 %collective-permute-start.10 = (bf16[32,832]{1,0:T(8,128)(2,1)S(1)}, bf16[32,832]{1,0:T(8,128)(2,1)S(1)}, u32[]{:S(2)}, u32[]{:S(2)}) collective-permute-start(bf16[32,832]{1,0:T(8,128)(2,1)S(1)} %get-tuple-element.28), channel_id=1, source_target_pairs={{0,8},{8,0},{16,24},{24,16},{1,9},{9,1},{17,25},{25,17},{2,10},{10... | collective-permute-start | bytes 159752 | tf_op jit(solution)/shard_map/ppermute | solution.py:11
  34.8 10.4 %all-to-all-start.1 = ((bf16[32,2,640]{2,1,0:T(2,128)(2,1)}), bf16[32,2,640]{2,1,0:T(2,128)(2,1)S(1)}, u32[]{:S(2)}, u32[]{:S(2)}) async-start(bf16[32,2,640]{2,1,0:T(2,128)(2,1)} %reshape.44), calls=%async_computation.1 | async-start | bytes 163840 | tf_op jit(solution)/shard_map/all_to_all | solution.py:89
  37.8 4.4 %collective-permute-start.11 = (bf16[32,1600]{1,0:T(8,128)(2,1)S(1)}, bf16[32,1600]{1,0:T(8,128)(2,1)S(1)}, u32[]{:S(2)}, u32[]{:S(2)}) collective-permute-start(bf16[32,1600]{1,0:T(8,128)(2,1)S(1)} %pad_maximum_fusion), channel_id=1, source_target_pairs={{0,8},{8,0},{16,24},{24,16},{1,9},{9,1},{17,25},{25,17},{2,10},{10... | collective-permute-start | bytes 307208 | tf_op jit(solution)/shard_map/ppermute | solution.py:11

commit v9 on v6

--- a/solution.py
+++ b/solution.py
@@ -59,7 +59,7 @@
     def both_cores(value):
         return jnp.concatenate([swap_cores(value, n_dp), value], axis=0)
 
-    first = units // 256 * 128
+    first = units // 320 * 128
     spans = [slice(0, first), slice(first, units)] if first else [slice(0, units)]
     packed, hidden = [], []
     for span in spans:

time: 44.7 us -> 44.7 us (level)
  no operation moved by 1% of the time
where the time goes in v9:
time: 44.7 us; the launch traced here: 44.5 us
  starting transfers between devices  16.5 us (37%)
  waiting for transfers between devices  13.2 us (30%)
  matrix products  9.59 us (21%)
  local copies, waits for them, and re-layouts  2.15 us (5%)
  other arithmetic  2.03 us (5%)
  between operations  0.94 us (2%)
    all_to_all x1, waiting for transfers between devices, local(): lax.all_to_all(slices.reshape(n_dp * n_tensor, 2 * rows, depth), ('dp', '...  7.91 us
    all_to_all x1, starting transfers between devices, local(): lax.all_to_all(slices.reshape(n_dp * n_tensor, 2 * rows, depth), ('dp', '...  7.3 us
    ppermute x4, starting transfers between devices, chip_sum(): lax.ppermute(mine, 'dp', [(i, (i + 2 * shift) % n_dp) for i in range(n_dp)])  4.3 us
    ppermute x4, waiting for transfers between devices, chip_sum(): lax.ppermute(mine, 'dp', [(i, (i + 2 * shift) % n_dp) for i in range(n_dp)])  3.61 us
    all_to_all x1, starting transfers between devices, local(): lax.all_to_all(shares, ('dp', 'tensor'), split_axis=0, concat_axis=0, til...  2.95 us
    dot_general x1, matrix products, local(): jnp.einsum('td,tf->df', tok, gate_grad, preferred_element_type=F32) / n_dp  2.05 us
    dot_general x1, matrix products, local(): jnp.einsum('td,tf->df', tok, up_grad, preferred_element_type=F32) / n_dp  2.05 us
    dot_general x1, matrix products, local(): jnp.einsum('tf,td->fd', hidden, cot, preferred_element_type=F32) / n_dp  2.04 us
  transfers between devices with their start and end apart: 14, of which 8 were waited for; matrix products, arithmetic and copies ran while one was open for 19% of the time, Pallas kernels for 0%

profile of v9, /device:TPU:0, one launch (start us, length us, event | category | flops | bytes accessed | tf_op | source)
XLA Modules:
  0.0 44.5 jit_solution(10130496371134844942)
XLA Ops:
  0.6 1.0 %fusion.48 = (bf16[1,4,640]{2,1,0:T(4,128)(2,1)S(1)}, bf16[1,4,640]{2,1,0:T(4,128)(2,1)S(1)}, bf16[1,4,640]{2,1,0:T(4,128)(2,1)S(1)}, bf16[1,4,640]{2,1,0:T(4,128)(2,1)S(1)}) fusion(bf16[2,2560]{1,0:T(2,128)(2,1)} %param.6, bf16[2,2560]{1,0:T(2,128)(2,1)} %param.5), kind=kLoop, calls=%fused_computation.83 | loop fusion | flops 40960 | bytes 40960 | tf_op jit(solution)/shard_map/stack | solution.py:25
  1.6 0.7 %broadcast_in_dim.2 = bf16[4,8,4,640]{3,2,1,0:T(4,128)(2,1)} broadcast(bf16[4,4,640]{2,1,0:T(4,128)(2,1)S(1)} %pad_maximum_fusion.1), dimensions={0,2,3} | broadcast | bytes 184320 | tf_op jit(solution)/shard_map/broadcast_in_dim | solution.py:26
  2.4 7.3 %all-to-all-start = ((bf16[32,4,640]{2,1,0:T(4,128)(2,1)}), bf16[32,4,640]{2,1,0:T(4,128)(2,1)S(1)}, u32[]{:S(2)}, u32[]{:S(2)}) async-start(bf16[32,4,640]{2,1,0:T(4,128)(2,1)} %bitcast.4), calls=%async_computation | async-start | bytes 327680 | tf_op jit(solution)/shard_map/all_to_all | solution.py:27
  9.7 7.9 %all-to-all-done = bf16[32,4,640]{2,1,0:T(4,128)(2,1)S(1)} async-done(((bf16[32,4,640]{2,1,0:T(4,128)(2,1)}), bf16[32,4,640]{2,1,0:T(4,128)(2,1)S(1)}, u32[]{:S(2)}, u32[]{:S(2)}) %all-to-all-start) | async-done | bytes 163872 | tf_op jit(solution)/shard_map/all_to_all | solution.py:27
  17.9 0.7 %fusion.58 = f32[64,1600]{1,0:T(8,128)S(1)} fusion(bf16[64,640]{1,0:T(8,128)(2,1)S(1)} %bitcast.45, bf16[1600,640]{1,0:T(8,128)(2,1)S(1)} %copy-done), kind=kOutput, calls=%fused_computation.93 | convolution fusion | flops 131072000 | bytes 2539520 | tf_op jit(solution)/shard_map/td,fd->tf/dot_general | solution.py:51
  18.9 0.5 %copy-done.2 = bf16[640,1600]{0,1:T(8,128)(2,1)S(1)} copy-done((bf16[640,1600]{0,1:T(8,128)(2,1)S(1)}, bf16[640,1600]{0,1:T(8,128)(2,1)}, u32[]{:S(2)}) %copy-start.2) | copy-done | bytes 2048024
  19.4 0.7 %fusion.59 = f32[64,1600]{1,0:T(8,128)S(1)} fusion(bf16[64,640]{1,0:T(8,128)(2,1)S(1)} %bitcast.39, bf16[640,1600]{0,1:T(8,128)(2,1)S(1)} %copy-done.2), kind=kOutput, calls=%fused_computation.94 | convolution fusion | flops 131072000 | bytes 2539520 | tf_op jit(solution)/shard_map/td,fd->tf/dot_general | solution.py:53
  20.4 1.4 %collective-permute-start.1 = (bf16[32,1600]{1,0:T(8,128)(2,1)S(1)}, bf16[32,1600]{1,0:T(8,128)(2,1)S(1)}, u32[]{:S(2)}, u32[]{:S(2)}) collective-permute-start(bf16[32,1600]{1,0:T(8,128)(2,1)S(1)} %add_convert_fusion), channel_id=1, source_target_pairs={{0,16},{8,24},{16,0},{24,8},{1,17},{9,25},{17,1},{25,9},{2,18},{10... | collective-permute-start | bytes 307208 | tf_op jit(solution)/shard_map/ppermute | solution.py:47
  21.8 0.7 %fusion.60 = f32[64,1600]{1,0:T(8,128)S(1)} fusion(bf16[64,640]{1,0:T(8,128)(2,1)S(1)} %bitcast.40, bf16[640,1600]{0,1:T(8,128)(2,1)S(1)} %copy-done.1), kind=kOutput, calls=%fused_computation.95 | convolution fusion | flops 131072000 | bytes 2539520 | tf_op jit(solution)/shard_map/td,fd->tf/dot_general | solution.py:56
  22.7 0.8 %collective-permute-start.3 = (bf16[32,1600]{1,0:T(8,128)(2,1)S(1)}, bf16[32,1600]{1,0:T(8,128)(2,1)S(1)}, u32[]{:S(2)}, u32[]{:S(2)}) collective-permute-start(bf16[32,1600]{1,0:T(8,128)(2,1)S(1)} %fusion.11), channel_id=1, source_target_pairs={{0,16},{8,24},{16,0},{24,8},{1,17},{9,25},{17,1},{25,9},{2,18},{10... | collective-permute-start | bytes 307208 | tf_op jit(solution)/shard_map/ppermute | solution.py:47
  23.5 0.4 collective-permute-done.4
  24.0 0.9 %collective-permute-start.5 = (bf16[32,640]{1,0:T(8,128)(2,1)S(1)}, bf16[32,640]{1,0:T(8,128)(2,1)S(1)}, u32[]{:S(2)}, u32[]{:S(2)}) collective-permute-start(bf16[32,640]{1,0:T(8,128)(2,1)S(1)} %slice.106), channel_id=1, source_target_pairs={{0,16},{8,24},{16,0},{24,8},{1,17},{9,25},{17,1},{25,9},{2,18},{10... | collective-permute-start | bytes 122888 | tf_op jit(solution)/shard_map/ppermute | solution.py:47
  24.9 1.2 %collective-permute-start.8 = (bf16[32,960]{1,0:T(8,128)(2,1)S(1)}, bf16[32,960]{1,0:T(8,128)(2,1)S(1)}, u32[]{:S(2)}, u32[]{:S(2)}) collective-permute-start(bf16[32,960]{1,0:T(8,128)(2,1)S(1)} %slice.111), channel_id=1, source_target_pairs={{0,16},{8,24},{16,0},{24,8},{1,17},{9,25},{17,1},{25,9},{2,18},{10... | collective-permute-start | bytes 184328 | tf_op jit(solution)/shard_map/ppermute | solution.py:47
  26.1 2.4 %collective-permute-done.3 = bf16[32,1600]{1,0:T(8,128)(2,1)S(1)} collective-permute-done((bf16[32,1600]{1,0:T(8,128)(2,1)S(1)}, bf16[32,1600]{1,0:T(8,128)(2,1)S(1)}, u32[]{:S(2)}, u32[]{:S(2)}) %collective-permute-start.3) | collective-permute-done | bytes 102432 | tf_op jit(solution)/shard_map/ppermute | solution.py:47
  28.5 0.8 %collective-permute-done.5 = bf16[32,640]{1,0:T(8,128)(2,1)S(1)} collective-permute-done((bf16[32,640]{1,0:T(8,128)(2,1)S(1)}, bf16[32,640]{1,0:T(8,128)(2,1)S(1)}, u32[]{:S(2)}, u32[]{:S(2)}) %collective-permute-start.5) | collective-permute-done | bytes 40992 | tf_op jit(solution)/shard_map/ppermute | solution.py:47
  29.5 0.5 %collective-permute-start.7 = (bf16[32,640]{1,0:T(8,128)(2,1)S(1)}, bf16[32,640]{1,0:T(8,128)(2,1)S(1)}, u32[]{:S(2)}, u32[]{:S(2)}) collective-permute-start(bf16[32,640]{1,0:T(8,128)(2,1)S(1)} %get-tuple-element.31), channel_id=1, source_target_pairs={{0,8},{8,0},{16,24},{24,16},{1,9},{9,1},{17,25},{25,17},{2,10},{10... | collective-permute-start | bytes 122888 | tf_op jit(solution)/shard_map/ppermute | solution.py:11
  30.6 0.5 %collective-permute-start.10 = (bf16[32,960]{1,0:T(8,128)(2,1)S(1)}, bf16[32,960]{1,0:T(8,128)(2,1)S(1)}, u32[]{:S(2)}, u32[]{:S(2)}) collective-permute-start(bf16[32,960]{1,0:T(8,128)(2,1)S(1)} %get-tuple-element.28), channel_id=1, source_target_pairs={{0,8},{8,0},{16,24},{24,16},{1,9},{9,1},{17,25},{25,17},{2,10},{10... | collective-permute-start | bytes 184328 | tf_op jit(solution)/shard_map/ppermute | solution.py:11
  32.7 0.7 %reshape.44 = bf16[32,2,640]{2,1,0:T(2,128)(2,1)} reshape(bf16[2,2,16,640]{3,2,1,0:T(8,128)(2,1)S(1)} %reverse_select_fusion) | data formatting | bytes 163840 | tf_op jit(solution)/shard_map/reshape | solution.py:85
  33.4 2.9 %all-to-all-start.1 = ((bf16[32,2,640]{2,1,0:T(2,128)(2,1)}), bf16[32,2,640]{2,1,0:T(2,128)(2,1)S(1)}, u32[]{:S(2)}, u32[]{:S(2)}) async-start(bf16[32,2,640]{2,1,0:T(2,128)(2,1)} %reshape.44), calls=%async_computation.1 | async-start | bytes 163840 | tf_op jit(solution)/shard_map/all_to_all | solution.py:88
  36.7 2.1 %multiply_convert_fusion.1 = bf16[640,1600]{0,1:T(8,128)(2,1)} fusion(bf16[64,640]{1,0:T(8,128)(2,1)S(1)} %bitcast.41, bf16[32,960]{1,0:T(8,128)(2,1)S(1)} %get-tuple-element.28, bf16[32,960]{1,0:T(8,128)(2,1)S(1)} %collective-permute-done.10, bf16[32,640]{1,0:T(8,128)(2,1)S(1)} %get-tuple-element.31, bf16[32,640]{1,0:T(8,128)(2,1)S(1)} %collective-permute-done.7), kind=kOutput, calls=%fused_computation.1 | convolution fusion | flops 133939200 | bytes 2334720 | tf_op jit(solution)/shard_map/td,tf->df/dot_general | solution.py:93
  38.7 2.1 %multiply_convert_fusion.2 = bf16[640,1600]{0,1:T(8,128)(2,1)} fusion(bf16[64,640]{1,0:T(8,128)(2,1)S(1)} %bitcast.42, bf16[32,960]{1,0:T(8,128)(2,1)S(1)} %get-tuple-element.27, bf16[32,960]{1,0:T(8,128)(2,1)S(1)} %collective-permute-done.9, bf16[32,640]{1,0:T(8,128)(2,1)S(1)} %get-tuple-element.30, bf16[32,640]{1,0:T(8,128)(2,1)S(1)} %collective-permute-done.6), kind=kOutput, calls=%fused_computation.2 | convolution fusion | flops 133939200 | bytes 2334720 | tf_op jit(solution)/shard_map/td,tf->df/dot_general | solution.py:92
  40.8 2.0 %multiply_convert_fusion = bf16[1600,640]{1,0:T(8,128)(2,1)} fusion(bf16[64,640]{1,0:T(8,128)(2,1)S(1)} %bitcast.46, bf16[32,1600]{1,0:T(8,128)(2,1)S(1)} %pad_maximum_fusion, bf16[32,1600]{1,0:T(8,128)(2,1)S(1)} %collective-permute-done.11), kind=kOutput, calls=%fused_computation | convolution fusion | flops 133529600 | bytes 2334720 | tf_op jit(solution)/shard_map/tf,td->fd/dot_general | solution.py:94
  42.8 1.0 %all-to-all-done.1 = bf16[32,2,640]{2,1,0:T(2,128)(2,1)S(1)} async-done(((bf16[32,2,640]{2,1,0:T(2,128)(2,1)}), bf16[32,2,640]{2,1,0:T(2,128)(2,1)S(1)}, u32[]{:S(2)}, u32[]{:S(2)}) %all-to-all-start.1) | async-done | bytes 81952 | tf_op jit(solution)/shard_map/all_to_all | solution.py:88
  43.8 0.7 %bitcast_reduce_fusion = bf16[4,2,640]{2,1,0:T(2,128)(2,1)} fusion(bf16[32,2,640]{2,1,0:T(2,128)(2,1)S(1)} %all-to-all-done.1), kind=kLoop, calls=%fused_computation.63 | loop fusion | flops 35840 | bytes 92160 | tf_op jit(solution)/shard_map/reduce_sum | solution.py:89
  (47 shorter events, 3.5 us)
Async XLA Ops:
  0.6 17.2 %copy-start = (bf16[1600,640]{1,0:T(8,128)(2,1)S(1)}, bf16[1600,640]{1,0:T(8,128)(2,1)}, u32[]{:S(2)}) copy-start(bf16[1600,640]{1,0:T(8,128)(2,1)} %param.9) | copy-start | bytes 6144004
  2.4 15.2 %all-to-all-start = ((bf16[32,4,640]{2,1,0:T(4,128)(2,1)}), bf16[32,4,640]{2,1,0:T(4,128)(2,1)S(1)}, u32[]{:S(2)}, u32[]{:S(2)}) async-start(bf16[32,4,640]{2,1,0:T(4,128)(2,1)} %bitcast.4), calls=%async_computation | async-start | bytes 327680 | tf_op jit(solution)/shard_map/all_to_all | solution.py:27
  17.8 1.6 %copy-start.2 = (bf16[640,1600]{0,1:T(8,128)(2,1)S(1)}, bf16[640,1600]{0,1:T(8,128)(2,1)}, u32[]{:S(2)}) copy-start(bf16[640,1600]{0,1:T(8,128)(2,1)} %param.8) | copy-start | bytes 6144004
  18.6 3.1 %copy-start.1 = (bf16[640,1600]{0,1:T(8,128)(2,1)S(1)}, bf16[640,1600]{0,1:T(8,128)(2,1)}, u32[]{:S(2)}) copy-start(bf16[640,1600]{0,1:T(8,128)(2,1)} %param.7) | copy-start | bytes 6144004
  18.7 1.7 %collective-permute-start = (bf16[32,1600]{1,0:T(8,128)(2,1)S(1)}, bf16[32,1600]{1,0:T(8,128)(2,1)S(1)}, u32[]{:S(2)}, u32[]{:S(2)}) collective-permute-start(bf16[32,1600]{1,0:T(8,128)(2,1)S(1)} %slice.180), channel_id=1, source_target_pairs={{0,8},{8,0},{16,24},{24,16},{1,9},{9,1},{17,25},{25,17},{2,10},{10... | collective-permute-start | bytes 307208 | tf_op jit(solution)/shard_map/ppermute | solution.py:11
  20.1 2.5 %collective-permute-start.2 = (bf16[32,1600]{1,0:T(8,128)(2,1)S(1)}, bf16[32,1600]{1,0:T(8,128)(2,1)S(1)}, u32[]{:S(2)}, u32[]{:S(2)}) collective-permute-start(bf16[32,1600]{1,0:T(8,128)(2,1)S(1)} %slice.179), channel_id=1, source_target_pairs={{0,8},{8,0},{16,24},{24,16},{1,9},{9,1},{17,25},{25,17},{2,10},{10... | collective-permute-start | bytes 307208 | tf_op jit(solution)/shard_map/ppermute | solution.py:11
  20.4 5.7 %collective-permute-start.1 = (bf16[32,1600]{1,0:T(8,128)(2,1)S(1)}, bf16[32,1600]{1,0:T(8,128)(2,1)S(1)}, u32[]{:S(2)}, u32[]{:S(2)}) collective-permute-start(bf16[32,1600]{1,0:T(8,128)(2,1)S(1)} %add_convert_fusion), channel_id=1, source_target_pairs={{0,16},{8,24},{16,0},{24,8},{1,17},{9,25},{17,1},{25,9},{2,18},{10... | collective-permute-start | bytes 307208 | tf_op jit(solution)/shard_map/ppermute | solution.py:47
  22.5 1.4 %collective-permute-start.4 = (bf16[32,1600]{1,0:T(8,128)(2,1)S(1)}, bf16[32,1600]{1,0:T(8,128)(2,1)S(1)}, u32[]{:S(2)}, u32[]{:S(2)}) collective-permute-start(bf16[32,1600]{1,0:T(8,128)(2,1)S(1)} %slice.178), channel_id=1, source_target_pairs={{0,8},{8,0},{16,24},{24,16},{1,9},{9,1},{17,25},{25,17},{2,10},{10... | collective-permute-start | bytes 307208 | tf_op jit(solution)/shard_map/ppermute | solution.py:11
  22.7 5.8 %collective-permute-start.3 = (bf16[32,1600]{1,0:T(8,128)(2,1)S(1)}, bf16[32,1600]{1,0:T(8,128)(2,1)S(1)}, u32[]{:S(2)}, u32[]{:S(2)}) collective-permute-start(bf16[32,1600]{1,0:T(8,128)(2,1)S(1)} %fusion.11), channel_id=1, source_target_pairs={{0,16},{8,24},{16,0},{24,8},{1,17},{9,25},{17,1},{25,9},{2,18},{10... | collective-permute-start | bytes 307208 | tf_op jit(solution)/shard_map/ppermute | solution.py:47
  24.0 5.4 %collective-permute-start.5 = (bf16[32,640]{1,0:T(8,128)(2,1)S(1)}, bf16[32,640]{1,0:T(8,128)(2,1)S(1)}, u32[]{:S(2)}, u32[]{:S(2)}) collective-permute-start(bf16[32,640]{1,0:T(8,128)(2,1)S(1)} %slice.106), channel_id=1, source_target_pairs={{0,16},{8,24},{16,0},{24,8},{1,17},{9,25},{17,1},{25,9},{2,18},{10... | collective-permute-start | bytes 122888 | tf_op jit(solution)/shard_map/ppermute | solution.py:47
  24.9 5.5 %collective-permute-start.8 = (bf16[32,960]{1,0:T(8,128)(2,1)S(1)}, bf16[32,960]{1,0:T(8,128)(2,1)S(1)}, u32[]{:S(2)}, u32[]{:S(2)}) collective-permute-start(bf16[32,960]{1,0:T(8,128)(2,1)S(1)} %slice.111), channel_id=1, source_target_pairs={{0,16},{8,24},{16,0},{24,8},{1,17},{9,25},{17,1},{25,9},{2,18},{10... | collective-permute-start | bytes 184328 | tf_op jit(solution)/shard_map/ppermute | solution.py:47
  29.4 1.9 %collective-permute-start.6 = (bf16[32,640]{1,0:T(8,128)(2,1)S(1)}, bf16[32,640]{1,0:T(8,128)(2,1)S(1)}, u32[]{:S(2)}, u32[]{:S(2)}) collective-permute-start(bf16[32,640]{1,0:T(8,128)(2,1)S(1)} %get-tuple-element.30), channel_id=1, source_target_pairs={{0,8},{8,0},{16,24},{24,16},{1,9},{9,1},{17,25},{25,17},{2,10},{10... | collective-permute-start | bytes 122888 | tf_op jit(solution)/shard_map/ppermute | solution.py:11
  29.5 1.6 %collective-permute-start.7 = (bf16[32,640]{1,0:T(8,128)(2,1)S(1)}, bf16[32,640]{1,0:T(8,128)(2,1)S(1)}, u32[]{:S(2)}, u32[]{:S(2)}) collective-permute-start(bf16[32,640]{1,0:T(8,128)(2,1)S(1)} %get-tuple-element.31), channel_id=1, source_target_pairs={{0,8},{8,0},{16,24},{24,16},{1,9},{9,1},{17,25},{25,17},{2,10},{10... | collective-permute-start | bytes 122888 | tf_op jit(solution)/shard_map/ppermute | solution.py:11
  30.5 1.3 %collective-permute-start.9 = (bf16[32,960]{1,0:T(8,128)(2,1)S(1)}, bf16[32,960]{1,0:T(8,128)(2,1)S(1)}, u32[]{:S(2)}, u32[]{:S(2)}) collective-permute-start(bf16[32,960]{1,0:T(8,128)(2,1)S(1)} %get-tuple-element.27), channel_id=1, source_target_pairs={{0,8},{8,0},{16,24},{24,16},{1,9},{9,1},{17,25},{25,17},{2,10},{10... | collective-permute-start | bytes 184328 | tf_op jit(solution)/shard_map/ppermute | solution.py:11
  30.6 1.4 %collective-permute-start.10 = (bf16[32,960]{1,0:T(8,128)(2,1)S(1)}, bf16[32,960]{1,0:T(8,128)(2,1)S(1)}, u32[]{:S(2)}, u32[]{:S(2)}) collective-permute-start(bf16[32,960]{1,0:T(8,128)(2,1)S(1)} %get-tuple-element.28), channel_id=1, source_target_pairs={{0,8},{8,0},{16,24},{24,16},{1,9},{9,1},{17,25},{25,17},{2,10},{10... | collective-permute-start | bytes 184328 | tf_op jit(solution)/shard_map/ppermute | solution.py:11
  33.4 10.4 %all-to-all-start.1 = ((bf16[32,2,640]{2,1,0:T(2,128)(2,1)}), bf16[32,2,640]{2,1,0:T(2,128)(2,1)S(1)}, u32[]{:S(2)}, u32[]{:S(2)}) async-start(bf16[32,2,640]{2,1,0:T(2,128)(2,1)} %reshape.44), calls=%async_computation.1 | async-start | bytes 163840 | tf_op jit(solution)/shard_map/all_to_all | solution.py:88
  36.4 4.4 %collective-permute-start.11 = (bf16[32,1600]{1,0:T(8,128)(2,1)S(1)}, bf16[32,1600]{1,0:T(8,128)(2,1)S(1)}, u32[]{:S(2)}, u32[]{:S(2)}) collective-permute-start(bf16[32,1600]{1,0:T(8,128)(2,1)S(1)} %pad_maximum_fusion), channel_id=1, source_target_pairs={{0,8},{8,0},{16,24},{24,16},{1,9},{9,1},{17,25},{25,17},{2,10},{10... | collective-permute-start | bytes 307208 | tf_op jit(solution)/shard_map/ppermute | solution.py:11
